TPU v7x, 1024 devices: a whole 4x8x16 slice. The times are simulated.
1024 devices in a mesh: gx: 16 (over z), gy: 64 (over x, y, core).
Axes of the slice: x: 4, y: 8, z: 16, core: 2. Of those that a mesh axis runs over, the one named last changes fastest.
Arguments:
- right_side: float32 [512, 16384], P('gx', 'gy'), may hold values from -6 to 6
- class_map: int32 [512, 16384], P('gx', 'gy'), may hold values from 0 to 3
- class_perm: float32 [4], replicated, may hold values from 0.05 to 20
- eigenvectors: float32 [40, 512, 16384], P(None, 'gx', 'gy'), may hold values from -0.0625 to 0.0625
- coarse_inverse: float32 [40960, 5120], P(('gx', 'gy')), may hold values from -4 to 40, as said below
Outputs:
- solution: float32 [512, 16384], P('gx', 'gy')
- residual: float32 [512, 16384], P('gx', 'gy')
Inputs may be any that keep to these rules, and one draw needn't show every extreme that they name: `coarse_inverse`: each coarse group's 5120 x 5120 block is symmetric positive definite.
All inputs are finite; a program needn't handle non-finite values.
Results may differ from a plain program's by a relative error of at most 0.0003.
Values sent between devices are 32-bit elements; how exact they have to be, the bound alone decides.
No kernel may reach another device: no remote copies, remote signals or barrier semaphores. Data moves between devices by JAX's collectives and lax.ppermute only.
A program may use at most 32 MiB of HBM per device.

v0:
```python
import jax
import jax.numpy as jnp
from jax import lax
from jax.sharding import PartitionSpec as P

CHEB = 4
ITERS = 2


REACTION = 0.05
EIGEN_TOP = 2.0
EIGEN_LOW = 0.1
HIGHEST = lax.Precision.HIGHEST


def extended(block, sides, width):
    for axis, dim in sides:
        count = lax.axis_size(axis)
        forward = [(i, i + 1) for i in range(count - 1)]
        backward = [(target, source) for source, target in forward]
        low = lax.ppermute(
            lax.slice_in_dim(block, block.shape[dim] - width, None, axis=dim), axis, forward
        )
        high = lax.ppermute(lax.slice_in_dim(block, 0, width, axis=dim), axis, backward)
        block = jnp.concatenate([low, block, high], axis=dim)
    return block


def swapped(x, axis, bit):
    return lax.ppermute(x, axis, [(i, i ^ 1 << bit) for i in range(lax.axis_size(axis))])


def shifted(padded):
    return (padded[:-2, 1:-1], padded[2:, 1:-1], padded[1:-1, :-2], padded[1:-1, 2:])


def harmonic(centre, beside):
    return jnp.where(beside > 0.0, 2.0 * centre * beside / (centre + beside), centre)


def coefficients_of(centre, padded):
    face_terms = tuple((harmonic(centre, beside) for beside in shifted(padded)))
    diagonal = REACTION + face_terms[0] + face_terms[1] + face_terms[2] + face_terms[3]
    return (face_terms, diagonal)


def operate(vector, neighbours, face_terms, diagonal):
    result = diagonal * vector
    for weight, beside in zip(face_terms, neighbours):
        result = result - weight * beside
    return result


def chebyshev(source, local_apply, diagonal):
    centre = 0.5 * (EIGEN_TOP + EIGEN_LOW)
    radius = 0.5 * (EIGEN_TOP - EIGEN_LOW)
    ratio_start = centre / radius
    factor = 1.0 / ratio_start
    update = source / diagonal / centre
    smoothed = update
    for degree in range(1, CHEB):
        defect = source - local_apply(smoothed)
        factor_next = 1.0 / (2.0 * ratio_start - factor)
        update = factor_next * factor * update + 2.0 * factor_next / radius * (defect / diagonal)
        smoothed = smoothed + update
        factor = factor_next
    return smoothed


def dot_residual(residual, preconditioned):
    return lax.psum(jnp.sum(residual * preconditioned), ("gx", "gy"))


def dot_direction(direction, operated):
    return lax.psum(jnp.sum(direction * operated), ("gx", "gy"))


def local(right_side, class_map, class_perm, eigenvectors, coarse_inverse):
    classes = jnp.arange(class_perm.shape[0], dtype=jnp.int32)
    permeability = jnp.sum(
        jnp.where(class_map[None] == classes[:, None, None], class_perm[:, None, None], 0.0), axis=0
    )
    widened = extended(permeability, (("gx", 0), ("gy", 1)), 1)
    face_terms, diagonal = coefficients_of(permeability, widened)

    def local_apply(vector):
        return operate(vector, shifted(jnp.pad(vector, 1)), face_terms, diagonal)

    def precondition(source):
        smoothed = chebyshev(source, local_apply, diagonal)
        projected = jnp.einsum("eij,ij->e", eigenvectors, source, precision=HIGHEST)
        own_row = lax.all_gather(projected, "gy", axis=0, tiled=True)
        partner_row = swapped(own_row, "gx", 0)
        upper_first = lax.axis_index("gx") % 2 == 0
        grouped = jnp.where(
            upper_first,
            jnp.concatenate([own_row, partner_row]),
            jnp.concatenate([partner_row, own_row]),
        )
        coarse = jnp.dot(coarse_inverse, grouped, precision=HIGHEST)
        prolonged = jnp.einsum("e,eij->ij", coarse, eigenvectors, precision=HIGHEST)
        return smoothed + prolonged

    solution = jnp.zeros_like(right_side)
    residual = right_side
    preconditioned = precondition(residual)
    direction = preconditioned
    product_rz = dot_residual(residual, preconditioned)
    for iteration in range(ITERS):
        padded = extended(direction, (("gx", 0), ("gy", 1)), 1)
        operated = operate(direction, shifted(padded), face_terms, diagonal)
        step_size = product_rz / dot_direction(direction, operated)
        solution = solution + step_size * direction
        residual = residual - step_size * operated
        if iteration + 1 < ITERS:
            preconditioned = precondition(residual)
            product_next = dot_residual(residual, preconditioned)
            direction = preconditioned + product_next / product_rz * direction
            product_rz = product_next
    return (solution, residual)


def solution(mesh):
    in_specs = (P("gx", "gy"), P("gx", "gy"), P(), P(None, "gx", "gy"), P(("gx", "gy"), None))
    out_specs = (P("gx", "gy"), P("gx", "gy"))
    return jax.shard_map(local, mesh=mesh, in_specs=in_specs, out_specs=out_specs, check_vma=False)
```

profile of v0, /device:TPU:1, one launch (start us, length us, event | category | flops | bytes accessed | tf_op | source)
XLA Modules:
  0.0 941.6 jit_solution(3607546156034181486)
XLA Ops:
  1.6 4.8 collective-permute-start
  9.7 3.2 convolution_bitcast_fusion.1
  13.1 251.1 %all-reduce.6 = f32[2560]{0:T(1024)S(1)} all-reduce(f32[2560]{0:T(1024)S(1)} %dynamic-update-slice), channel_id=1, replica_groups=mesh['gx'=16,'gy'=64] {'gy'}, use_global_device_ids=true, to_apply=%add.6 | all-reduce | flops 2560 | bytes 20480
  264.2 4.3 collective-permute-start.4
  268.6 3.9 collective-permute-start.2
  272.5 5.2 collective-permute-start.3
  279.6 1.5 fusion.3
  281.2 1.6 collective-permute-start.5
  284.2 3.0 collective-permute-done.6
  287.3 2.4 collective-permute-start.7
  289.6 2.6 collective-permute-start.8
  292.3 2.5 collective-permute-done.8
  295.5 126.2 %all-reduce.8 = (f32[]{:T(128)}, f32[]{:T(128)}) all-reduce(f32[]{:T(128)} %get-tuple-element.3, f32[]{:T(128)} %get-tuple-element.2), channel_id=1, replica_groups=mesh['gx'=16,'gy'=64] {'gx','gy'}, use_global_device_ids=true, to_apply=%region_2.3 | all-reduce | flops 2 | bytes 16 | tf_op jit(solution)/shard_map/psum | solution.py:71
  423.0 1.8 convolution_bitcast_fusion
  425.0 242.0 %all-reduce.7 = f32[2560]{0:T(1024)S(1)} all-reduce(f32[2560]{0:T(1024)S(1)} %dynamic-update-slice.1), channel_id=1, replica_groups=mesh['gx'=16,'gy'=64] {'gy'}, use_global_device_ids=true, to_apply=%add.7 | all-reduce | flops 2560 | bytes 20480
  667.0 1.9 collective-permute-start.9
  669.1 2.6 collective-permute-done.9
  674.6 122.3 %psum.30 = f32[]{:T(128)} all-reduce(f32[]{:T(128)} %get-tuple-element.8), channel_id=1, replica_groups=mesh['gx'=16,'gy'=64] {'gx','gy'}, use_global_device_ids=true, to_apply=%region_6.7 | all-reduce | flops 1 | bytes 8 | tf_op jit(solution)/shard_map/psum | solution.py:71
  798.2 3.6 collective-permute-start.10
  803.2 3.0 collective-permute-done.11
  806.3 2.2 collective-permute-start.12
  808.4 3.1 collective-permute-start.13
  811.6 2.0 collective-permute-done.13
  814.2 125.4 %psum.31 = f32[]{:T(128)} all-reduce(f32[]{:T(128)} %get-tuple-element.6), channel_id=1, replica_groups=mesh['gx'=16,'gy'=64] {'gx','gy'}, use_global_device_ids=true, to_apply=%region_8.9 | all-reduce | flops 1 | bytes 8 | tf_op jit(solution)/shard_map/psum | solution.py:75
  (50 shorter events, 14.0 us)
Async XLA Ops:
  0.6 278.3 %copy-start = (f32[40,5120]{1,0:T(8,128)S(1)}, f32[40,5120]{1,0:T(8,128)}, u32[]{:S(2)}) copy-start(f32[40,5120]{1,0:T(8,128)} %param.9) | copy-start | bytes 2457604
  0.6 277.9 %copy-start.2 = (f32[32,256]{1,0:T(8,128)S(1)}, f32[32,256]{1,0:T(8,128)}, u32[]{:S(2)}) copy-start(f32[32,256]{1,0:T(8,128)} %param.5) | copy-start | bytes 98308
  1.6 266.9 %collective-permute-start = (f32[1,256]{1,0:T(1,128)S(1)}, f32[1,256]{1,0:T(1,128)S(1)}, u32[]{:S(2)}, u32[]{:S(2)}) collective-permute-start(f32[1,256]{1,0:T(1,128)S(1)} %get-tuple-element.36), channel_id=1, source_target_pairs={{0,64},{64,128},{128,192},{192,256},{256,320},{320,384},{384,448},... | collective-permute-start | bytes 3080 | tf_op jit(solution)/shard_map/ppermute | solution.py:21
  6.4 262.0 %collective-permute-start.1 = (f32[1,256]{1,0:T(1,128)S(1)}, f32[1,256]{1,0:T(1,128)S(1)}, u32[]{:S(2)}, u32[]{:S(2)}) collective-permute-start(f32[1,256]{1,0:T(1,128)S(1)} %get-tuple-element.37), channel_id=1, source_target_pairs={{64,0},{128,64},{192,128},{256,192},{320,256},{384,320},{448,384},... | collective-permute-start | bytes 3080 | tf_op jit(solution)/shard_map/ppermute | solution.py:24
  9.7 270.0 %copy-start.1 = (f32[40,32,256]{2,1,0:T(8,128)S(1)}, f32[40,32,256]{2,1,0:T(8,128)}, u32[]{:S(2)}) copy-start(f32[40,32,256]{2,1,0:T(8,128)} %param.8) | copy-start | bytes 3932164
  264.2 14.7 %collective-permute-start.4 = (f32[2560]{0:T(1024)S(1)}, f32[2560]{0:T(1024)S(1)}, u32[]{:S(2)}, u32[]{:S(2)}) collective-permute-start(f32[2560]{0:T(1024)S(1)} %all-reduce.6), channel_id=1, source_target_pairs={{0,64},{64,0},{128,192},{192,128},{256,320},{320,256},{384,448},{4... | collective-permute-start | bytes 30728 | tf_op jit(solution)/shard_map/ppermute | solution.py:30
  268.6 9.1 collective-permute-start.2
  272.5 6.1 collective-permute-start.3
  281.2 2.9 collective-permute-start.5
  282.9 4.3 collective-permute-start.6
  287.3 5.0 collective-permute-start.7
  289.6 5.1 collective-permute-start.8
  667.0 4.7 collective-permute-start.9
  798.2 5.0 collective-permute-start.10
  801.9 4.3 collective-permute-start.11
  806.3 5.3 collective-permute-start.12
  808.4 5.1 collective-permute-start.13
where the time goes:
time: 942 us
  blocking collectives  867 us (92%)
  starting transfers between devices  39.5 us (4%)
  waiting for transfers between devices  13.9 us (1%)
    unnamed x2, blocking collectives  493 us
    psum x2, blocking collectives, dot_residual(): return lax.psum(jnp.sum(residual * preconditioned), ('gx', 'gy'))  249 us
    psum x1, blocking collectives, dot_direction(): return lax.psum(jnp.sum(direction * operated), ('gx', 'gy'))  125 us
  transfers between devices with their start and end apart: 14, of which 6 were waited for; matrix products, arithmetic and copies ran while one was open for 1% of the time, Pallas kernels for 0%

commit v1 on v0

v1 whole, which is shorter than its diff:
```python
import jax
import jax.numpy as jnp
from jax import lax
from jax.sharding import Mesh, PartitionSpec as P

CHEB = 4
REACTION = 0.05
EIGEN_TOP = 2.0
EIGEN_LOW = 0.1
HIGHEST = lax.Precision.HIGHEST

ROWS = ("zh", "zl")
COLS = ("xy", "core")
GROUP = ("zl", "xy", "core")
STACK = ("zh", "zl", "core")
PLANE = ("xy",)
FINE = ("zh", "zl", "xy", "core")


def spread(message, axes):
    count = 1
    for axis in axes:
        count *= lax.axis_size(axis)
    copies = jnp.broadcast_to(message[None], (count,) + message.shape)
    return lax.all_to_all(copies, axes, 0, 0, tiled=True)


def moved(x, axes, by):
    count = lax.axis_size(axes)
    pairs = [(i, i + by) for i in range(count) if 0 <= i + by < count]
    return lax.ppermute(x, axes, pairs)


def harmonic(centre, beside):
    return jnp.where(beside > 0.0, 2.0 * centre * beside / (centre + beside), centre)


def beside(v, up, down, left, right):
    return (
        jnp.concatenate([up, v[:-1]], axis=0),
        jnp.concatenate([v[1:], down], axis=0),
        jnp.concatenate([left, v[:, :-1]], axis=1),
        jnp.concatenate([v[:, 1:], right], axis=1),
    )


def beside_inside(v):
    row, column = jnp.zeros_like(v[:1]), jnp.zeros_like(v[:, :1])
    return beside(v, row, row, column, column)


def operate(vector, neighbours, face_terms, diagonal):
    result = diagonal * vector
    for weight, near in zip(face_terms, neighbours):
        result = result - weight * near
    return result


def chebyshev(source, local_apply, diagonal):
    centre = 0.5 * (EIGEN_TOP + EIGEN_LOW)
    radius = 0.5 * (EIGEN_TOP - EIGEN_LOW)
    ratio_start = centre / radius
    factor = 1.0 / ratio_start
    update = source / diagonal / centre
    smoothed = update
    for degree in range(1, CHEB):
        defect = source - local_apply(smoothed)
        factor_next = 1.0 / (2.0 * ratio_start - factor)
        update = factor_next * factor * update + 2.0 * factor_next / radius * (defect / diagonal)
        smoothed = smoothed + update
        factor = factor_next
    return smoothed


def padded(parts, width):
    used = sum(p.shape[0] for p in parts)
    return jnp.concatenate(parts + [jnp.zeros((width - used,), jnp.float32)])


def local(right_side, class_map, class_perm, eigenvectors, coarse_inverse):
    rows, columns = right_side.shape
    nev = eigenvectors.shape[0]
    z_count, z = lax.axis_size(ROWS), lax.axis_index(ROWS)
    b_count, b = lax.axis_size(COLS), lax.axis_index(COLS)
    zl = lax.axis_index("zl")
    xy_count, xy = lax.axis_size("xy"), lax.axis_index("xy")
    core = lax.axis_index("core")

    classes = jnp.arange(class_perm.shape[0], dtype=jnp.int32)
    perm = jnp.sum(
        jnp.where(class_map[None] == classes[:, None, None], class_perm[:, None, None], 0.0), axis=0
    )
    perm_up = moved(perm[-1:], ROWS, 1)
    perm_down = moved(perm[:1], ROWS, -1)

    def project(v):
        return jnp.einsum("eij,ij->e", eigenvectors, v, precision=HIGHEST)

    def prolong(gathered):
        grouped = gathered[:, :nev].reshape(-1)
        coarse = jnp.dot(coarse_inverse, grouped, precision=HIGHEST)
        return jnp.einsum("e,eij->ij", coarse, eigenvectors, precision=HIGHEST)

    first = spread(padded([project(right_side), perm[:, 0], perm[:, -1]], 128), GROUP)
    place = zl * b_count + b
    at_left = lax.dynamic_index_in_dim(first, jnp.maximum(place - 1, 0), 0, keepdims=False)
    at_right = lax.dynamic_index_in_dim(
        first, jnp.minimum(place + 1, first.shape[0] - 1), 0, keepdims=False
    )
    perm_left = jnp.where(b > 0, at_left[nev + rows : nev + 2 * rows], 0.0)[:, None]
    perm_right = jnp.where(b < b_count - 1, at_right[nev : nev + rows], 0.0)[:, None]
    near = beside(perm, perm_up, perm_down, perm_left, perm_right)
    faces = tuple(harmonic(perm, n) for n in near)
    diagonal = REACTION + faces[0] + faces[1] + faces[2] + faces[3]

    def local_apply(vector):
        return operate(vector, beside_inside(vector), faces, diagonal)

    z0 = chebyshev(right_side, local_apply, diagonal) + prolong(first)
    halo = (
        moved(z0[-1:], ROWS, 1),
        moved(z0[:1], ROWS, -1),
        moved(z0[:, -1:], COLS, 1),
        moved(z0[:, :1], COLS, -1),
    )
    q0 = operate(z0, beside(z0, *halo), faces, diagonal)
    second = spread(padded([project(q0)], 128), GROUP)
    w = chebyshev(q0, local_apply, diagonal) + prolong(second)
    inner = local_apply(w)

    scalars = jnp.stack([
        jnp.sum(right_side * z0),
        jnp.sum(z0 * q0),
        jnp.sum(right_side * w),
        jnp.sum(q0 * w),
        jnp.sum(w * inner),
    ])
    low = (faces[1] * w)[-1]
    right = (faces[3] * w)[:, -1]
    s = 2 * columns
    t = s + 2 * rows
    third = spread(padded([low, w[0], w[:, 0], right, scalars], t + 128 - t % 128), STACK)
    third = third.reshape(z_count, 2, -1)
    lows, tops = third[:, :, :columns], third[:, :, columns:s]
    lefts, rights = third[:, :, s : s + rows], third[:, :, s + rows : t]
    between = jnp.sum(lows[:-1] * tops[1:]) + jnp.sum(rights[:, 0] * lefts[:, 1])
    sums = jnp.sum(third[:, :, t : t + 5], axis=(0, 1)) - 2.0 * between * (jnp.arange(5) == 4)
    own = lax.dynamic_index_in_dim(third, core, 1, keepdims=False)
    from_up = lax.dynamic_index_in_dim(own, jnp.maximum(z - 1, 0), 0, keepdims=False)[:columns]
    from_down = lax.dynamic_index_in_dim(own, jnp.minimum(z + 1, z_count - 1), 0, keepdims=False)[
        columns:s
    ]
    mine = lax.dynamic_index_in_dim(third, z, 0, keepdims=False)

    wide = z_count * rows
    fourth = spread(
        padded([lefts[:, 0].reshape(-1), rights[:, 1].reshape(-1), sums], 2 * wide + 128), PLANE
    )
    outer_lefts, outer_rights = fourth[:, :wide], fourth[:, wide : 2 * wide]
    totals = jnp.sum(fourth[:, 2 * wide : 2 * wide + 5], axis=0)
    across = jnp.sum(outer_rights[:-1] * outer_lefts[1:])
    outer_left = lax.dynamic_slice(
        outer_rights, (jnp.maximum(xy - 1, 0), z * rows), (1, rows)
    )[0]
    outer_right = lax.dynamic_slice(
        outer_lefts, (jnp.minimum(xy + 1, xy_count - 1), z * rows), (1, rows)
    )[0]
    up = jnp.where(z > 0, from_up, 0.0)
    down = jnp.where(z < z_count - 1, from_down, 0.0) * faces[1][-1]
    left = jnp.where(core == 1, mine[0, s + rows : t], jnp.where(xy > 0, outer_left, 0.0))
    right_in = jnp.where(
        core == 0, mine[1, s : s + rows], jnp.where(xy < xy_count - 1, outer_right, 0.0)
    )
    right_in = right_in * faces[3][:, -1]
    row_id = lax.broadcasted_iota(jnp.int32, (rows, columns), 0)
    column_id = lax.broadcasted_iota(jnp.int32, (rows, columns), 1)
    v = inner - jnp.where(row_id == 0, up[None], 0.0) - jnp.where(row_id == rows - 1, down[None], 0.0)
    v = v - jnp.where(column_id == 0, left[:, None], 0.0)
    v = v - jnp.where(column_id == columns - 1, right_in[:, None], 0.0)

    rz, zq, rw, qw = totals[0], totals[1], totals[2], totals[3]
    wv = totals[4] - 2.0 * across
    step = rz / zq
    rz_new = rz - step * ((rw + zq) - step * qw)
    beta = rz_new / rz
    grow = 1.0 + beta
    curve = grow * grow * zq - 2.0 * grow * step * qw + step * step * wv
    step_next = rz_new / curve
    on_z = step + step_next * grow
    on_w = step_next * step
    solution = on_z * z0 - on_w * w
    residual = right_side - on_z * q0 + on_w * v
    return (solution, residual)


def solution(mesh):
    n_gx, n_gy = mesh.devices.shape
    fine = Mesh(mesh.devices.reshape(n_gx // 2, 2, n_gy // 2, 2), FINE)
    in_specs = (P(ROWS, COLS), P(ROWS, COLS), P(), P(None, ROWS, COLS), P(FINE, None))
    out_specs = (P(ROWS, COLS), P(ROWS, COLS))
    return jax.shard_map(local, mesh=fine, in_specs=in_specs, out_specs=out_specs, check_vma=False)
```

time: 942 us -> 146 us (0.15)
  blocking collectives: 867 us -> 0 us
  waiting for transfers between devices: 13.9 us -> 46.6 us
  starting transfers between devices: 39.5 us -> 63.4 us
    unnamed x2 -> x0, blocking collectives: 493 us -> none
    psum x3 -> x0, blocking collectives: 374 us -> none  [the longest x2 249 us: dot_residual(): return lax.psum(jnp.sum(residual * preconditioned), ('gx', 'gy'))]
    all_to_all x0 -> x4, starting transfers between devices: none -> 48.7 us  [spread(): return lax.all_to_all(copies, axes, 0, 0, tiled=True)]
    all_to_all x0 -> x4, waiting for transfers between devices: none -> 43.5 us  [spread(): return lax.all_to_all(copies, axes, 0, 0, tiled=True)]
    ppermute x14 -> x6, starting transfers between devices: 39.5 us -> 14.6 us  [moved(): return lax.ppermute(x, axes, pairs)]
    ppermute x14 -> x6, waiting for transfers between devices: 13.9 us -> 3.12 us  [moved(): return lax.ppermute(x, axes, pairs)]
  transfers between devices with their start and end apart: 14 -> 10, of which waited for: 6 -> 5; matrix products, arithmetic and copies ran while one was open for 1% -> 3% of each run, Pallas kernels for 0% -> 0%
where the time goes in v1:
time: 146 us; the launch traced here: 144 us
  starting transfers between devices  63.4 us (43%)
  waiting for transfers between devices  46.6 us (32%)
  between operations  9.29 us (6%)
  matrix products  9.19 us (6%)
  local copies, waits for them, and re-layouts  8.46 us (6%)
  other arithmetic  6.84 us (5%)
    all_to_all x4, starting transfers between devices, spread(): return lax.all_to_all(copies, axes, 0, 0, tiled=True)  48.7 us
    all_to_all x4, waiting for transfers between devices, spread(): return lax.all_to_all(copies, axes, 0, 0, tiled=True)  43.5 us
    ppermute x6, starting transfers between devices, moved(): return lax.ppermute(x, axes, pairs)  14.6 us
    dot_general x2, matrix products, project(): return jnp.einsum('eij,ij->e', eigenvectors, v, precision=HIGHEST)  4.81 us
    concatenate x3, local copies, waits for them, and re-layouts, padded(): return jnp.concatenate(parts + [jnp.zeros((width - used,), jnp.float32)])  3.34 us
    ppermute x6, waiting for transfers between devices, moved(): return lax.ppermute(x, axes, pairs)  3.12 us
  transfers between devices with their start and end apart: 10, of which 5 were waited for; matrix products, arithmetic and copies ran while one was open for 3% of the time, Pallas kernels for 0%

profile of v1, /device:TPU:1, one launch (start us, length us, event | category | flops | bytes accessed | tf_op | source)
XLA Modules:
  0.0 143.8 jit_solution(14164728476416741773)
XLA Ops:
  0.7 0.9 select_reduce_fusion
  1.6 4.8 %collective-permute-start.1 = (f32[1,256]{1,0:T(1,128)S(1)}, f32[1,256]{1,0:T(1,128)S(1)}, u32[]{:S(2)}, u32[]{:S(2)}) collective-permute-start(f32[1,256]{1,0:T(1,128)S(1)} %get-tuple-element.74), channel_id=1, source_target_pairs={{0,64},{64,128},{128,192},{192,256},{256,320},{320,384},{384,448},... | collective-permute-start | bytes 3080 | tf_op jit(solution)/shard_map/ppermute | solution.py:31
  6.4 1.3 collective-permute-start
  7.9 3.1 %convolution_bitcast_fusion.1 = f32[40]{0:T(128)S(1)} fusion(f32[40,32,256]{2,1,0:T(8,128)} %param.8, f32[32,256,1]{1,0,2:T(8,128)} %bitcast.63), kind=kOutput, calls=%fused_computation.1 | convolution fusion | flops 3932160 | bytes 1343648 | tf_op jit(solution)/shard_map/eij,ij->e/dot_general | solution.py:97
  11.7 15.9 %all-to-all-start = ((f32[128,1,128]{2,1,0:T(1,128)}), f32[128,1,128]{2,1,0:T(1,128)S(1)}, u32[]{:S(2)}, u32[]{:S(2)}) async-start(f32[128,1,128]{2,1,0:T(1,128)} %broadcast_in_dim.102), calls=%async_computation | async-start | bytes 131072 | tf_op jit(solution)/shard_map/all_to_all | solution.py:25
  27.7 10.4 %all-to-all-done = f32[128,1,128]{2,1,0:T(1,128)S(1)} async-done(((f32[128,1,128]{2,1,0:T(1,128)}), f32[128,1,128]{2,1,0:T(1,128)S(1)}, u32[]{:S(2)}, u32[]{:S(2)}) %all-to-all-start) | async-done | bytes 65568 | tf_op jit(solution)/shard_map/all_to_all | solution.py:25
  39.1 0.7 convolution_bitcast_fusion.3
  39.9 1.5 %fusion.3 = f32[1,32,256]{2,0,1:T(1,128)S(1)} fusion(f32[40,1,1]{0,1,2:T(1,128)S(1)} %convolution_bitcast_fusion.3, f32[40,32,256]{2,1,0:T(8,128)S(1)} %copy-done.1), kind=kOutput, calls=%fused_computation.7 | convolution fusion | flops 3932160 | bytes 1343648 | tf_op jit(solution)/shard_map/e,eij->ij/dot_general | solution.py:102
  41.6 2.2 %collective-permute-start.2 = (f32[1,256]{1,0:T(1,128)S(1)}, f32[1,256]{1,0:T(1,128)S(1)}, u32[]{:S(2)}, u32[]{:S(2)}) collective-permute-start(f32[1,256]{1,0:T(1,128)S(1)} %get-tuple-element.54), channel_id=1, source_target_pairs={{0,64},{64,128},{128,192},{192,256},{256,320},{320,384},{384,448},... | collective-permute-start | bytes 3080 | tf_op jit(solution)/shard_map/ppermute | solution.py:31
  43.8 1.3 collective-permute-start.3
  45.1 3.1 %collective-permute-start.4 = (f32[32,1]{1,0:T(8,128)S(1)}, f32[32,1]{1,0:T(8,128)S(1)}, u32[]{:S(2)}, u32[]{:S(2)}) collective-permute-start(f32[32,1]{1,0:T(8,128)S(1)} %get-tuple-element.58), channel_id=1, source_target_pairs={{0,1},{1,2},{2,3},{3,4},{4,5},{5,6},{6,7},{7,8},{8,9},{9,10},{10,1... | collective-permute-start | bytes 392 | tf_op jit(solution)/shard_map/ppermute | solution.py:31
  48.2 1.9 %collective-permute-start.5 = (f32[32,1]{1,0:T(8,128)S(1)}, f32[32,1]{1,0:T(8,128)S(1)}, u32[]{:S(2)}, u32[]{:S(2)}) collective-permute-start(f32[32,1]{1,0:T(8,128)S(1)} %get-tuple-element.59), channel_id=1, source_target_pairs={{1,0},{2,1},{3,2},{4,3},{5,4},{6,5},{7,6},{8,7},{9,8},{10,9},{11,1... | collective-permute-start | bytes 392 | tf_op jit(solution)/shard_map/ppermute | solution.py:31
  50.1 3.1 %collective-permute-done.5 = f32[32,1]{1,0:T(8,128)S(1)} collective-permute-done((f32[32,1]{1,0:T(8,128)S(1)}, f32[32,1]{1,0:T(8,128)S(1)}, u32[]{:S(2)}, u32[]{:S(2)}) %collective-permute-start.5) | collective-permute-done | bytes 160 | tf_op jit(solution)/shard_map/ppermute | solution.py:31
  53.6 1.8 %convolution_bitcast_fusion = f32[40]{0:T(128)S(1)} fusion(f32[40,32,256]{2,1,0:T(8,128)S(1)} %copy-done.1, f32[32,256,1]{1,0,2:T(8,128)S(1)} %bitcast.64), kind=kOutput, calls=%fused_computation | convolution fusion | flops 3932160 | bytes 1343648 | tf_op jit(solution)/shard_map/eij,ij->e/dot_general | solution.py:97
  56.0 12.6 %all-to-all-start.1 = ((f32[128,1,128]{2,1,0:T(1,128)}), f32[128,1,128]{2,1,0:T(1,128)S(1)}, u32[]{:S(2)}, u32[]{:S(2)}) async-start(f32[128,1,128]{2,1,0:T(1,128)} %broadcast_in_dim.104), calls=%async_computation.1 | async-start | bytes 131072 | tf_op jit(solution)/shard_map/all_to_all | solution.py:25
  68.9 10.3 %all-to-all-done.1 = f32[128,1,128]{2,1,0:T(1,128)S(1)} async-done(((f32[128,1,128]{2,1,0:T(1,128)}), f32[128,1,128]{2,1,0:T(1,128)S(1)}, u32[]{:S(2)}, u32[]{:S(2)}) %all-to-all-start.1) | async-done | bytes 65568 | tf_op jit(solution)/shard_map/all_to_all | solution.py:25
  79.3 0.7 convolution_bitcast_fusion.2
  80.0 1.4 %fusion = f32[1,32,256]{2,0,1:T(1,128)S(1)} fusion(f32[40,1,1]{0,1,2:T(1,128)S(1)} %convolution_bitcast_fusion.2, f32[40,32,256]{2,1,0:T(8,128)S(1)} %copy-done.1), kind=kOutput, calls=%fused_computation.4 | convolution fusion | flops 3932160 | bytes 1343648 | tf_op jit(solution)/shard_map/e,eij->ij/dot_general | solution.py:102
  81.9 0.8 multiply_reduce_fusion
  82.7 3.3 %concatenate.158 = f32[640]{0:T(1024)S(1)} concatenate(f32[256]{0:T(256)S(1)} %bitcast.73, f32[256]{0:T(256)S(1)} %bitcast.72, f32[32]{0:T(128)S(1)} %get-tuple-element.13, f32[32]{0:T(128)S(1)} %get-tuple-element.12, f32[1]{0:T(128)} %bitcast.18, f32[1]{0:T(128)} %bitcast.19, f32[1]{0:T(128)} %bitcast.20, f32[1]{0:T(128)} %bitcast.21, f32[1]{0:T(128)} %bitcast.22, ...), dimensions={0} | concatenate | bytes 5120 | tf_op jit(solution)/shard_map/concatenate | solution.py:77
  86.6 16.4 %all-to-all-start.2 = ((f32[32,1,640]{2,1,0:T(1,128)}), f32[32,1,640]{2,1,0:T(1,128)S(1)}, u32[]{:S(2)}, u32[]{:S(2)}) async-start(f32[32,1,640]{2,1,0:T(1,128)} %broadcast_in_dim.106), calls=%async_computation.2 | async-start | bytes 163840 | tf_op jit(solution)/shard_map/all_to_all | solution.py:25
  103.0 13.6 %all-to-all-done.2 = f32[32,1,640]{2,1,0:T(1,128)S(1)} async-done(((f32[32,1,640]{2,1,0:T(1,128)}), f32[32,1,640]{2,1,0:T(1,128)S(1)}, u32[]{:S(2)}, u32[]{:S(2)}) %all-to-all-start.2) | async-done | bytes 81952 | tf_op jit(solution)/shard_map/all_to_all | solution.py:25
  120.6 3.9 %all-to-all-start.3 = ((f32[32,1,1152]{2,1,0:T(1,128)}), f32[32,1,1152]{2,1,0:T(1,128)S(1)}, u32[]{:S(2)}, u32[]{:S(2)}) async-start(f32[32,1,1152]{2,1,0:T(1,128)} %broadcast_in_dim.108), calls=%async_computation.3 | async-start | bytes 294912 | tf_op jit(solution)/shard_map/all_to_all | solution.py:25
  124.6 9.1 %all-to-all-done.3 = f32[32,1,1152]{2,1,0:T(1,128)S(1)} async-done(((f32[32,1,1152]{2,1,0:T(1,128)}), f32[32,1,1152]{2,1,0:T(1,128)S(1)}, u32[]{:S(2)}, u32[]{:S(2)}) %all-to-all-start.3) | async-done | bytes 147488 | tf_op jit(solution)/shard_map/all_to_all | solution.py:25
  (82 shorter events, 10.3 us)
Async XLA Ops:
  0.6 38.5 %copy-start = (f32[40,5120]{1,0:T(8,128)S(1)}, f32[40,5120]{1,0:T(8,128)}, u32[]{:S(2)}) copy-start(f32[40,5120]{1,0:T(8,128)} %param.9) | copy-start | bytes 2457604
  0.6 37.8 %copy-start.2 = (f32[32,256]{1,0:T(8,128)S(1)}, f32[32,256]{1,0:T(8,128)}, u32[]{:S(2)}) copy-start(f32[32,256]{1,0:T(8,128)} %param.5) | copy-start | bytes 98308
  1.6 36.8 %collective-permute-start.1 = (f32[1,256]{1,0:T(1,128)S(1)}, f32[1,256]{1,0:T(1,128)S(1)}, u32[]{:S(2)}, u32[]{:S(2)}) collective-permute-start(f32[1,256]{1,0:T(1,128)S(1)} %get-tuple-element.74), channel_id=1, source_target_pairs={{0,64},{64,128},{128,192},{192,256},{256,320},{320,384},{384,448},... | collective-permute-start | bytes 3080 | tf_op jit(solution)/shard_map/ppermute | solution.py:31
  6.4 32.0 %collective-permute-start = (f32[1,256]{1,0:T(1,128)S(1)}, f32[1,256]{1,0:T(1,128)S(1)}, u32[]{:S(2)}, u32[]{:S(2)}) collective-permute-start(f32[1,256]{1,0:T(1,128)S(1)} %get-tuple-element.75), channel_id=1, source_target_pairs={{64,0},{128,64},{192,128},{256,192},{320,256},{384,320},{448,384},... | collective-permute-start | bytes 3080 | tf_op jit(solution)/shard_map/ppermute | solution.py:31
  11.7 26.4 %all-to-all-start = ((f32[128,1,128]{2,1,0:T(1,128)}), f32[128,1,128]{2,1,0:T(1,128)S(1)}, u32[]{:S(2)}, u32[]{:S(2)}) async-start(f32[128,1,128]{2,1,0:T(1,128)} %broadcast_in_dim.102), calls=%async_computation | async-start | bytes 131072 | tf_op jit(solution)/shard_map/all_to_all | solution.py:25
  38.5 1.3 copy-start.1
  41.6 11.7 %collective-permute-start.2 = (f32[1,256]{1,0:T(1,128)S(1)}, f32[1,256]{1,0:T(1,128)S(1)}, u32[]{:S(2)}, u32[]{:S(2)}) collective-permute-start(f32[1,256]{1,0:T(1,128)S(1)} %get-tuple-element.54), channel_id=1, source_target_pairs={{0,64},{64,128},{128,192},{192,256},{256,320},{320,384},{384,448},... | collective-permute-start | bytes 3080 | tf_op jit(solution)/shard_map/ppermute | solution.py:31
  43.8 9.5 %collective-permute-start.3 = (f32[1,256]{1,0:T(1,128)S(1)}, f32[1,256]{1,0:T(1,128)S(1)}, u32[]{:S(2)}, u32[]{:S(2)}) collective-permute-start(f32[1,256]{1,0:T(1,128)S(1)} %get-tuple-element.55), channel_id=1, source_target_pairs={{64,0},{128,64},{192,128},{256,192},{320,256},{384,320},{448,384},... | collective-permute-start | bytes 3080 | tf_op jit(solution)/shard_map/ppermute | solution.py:31
  45.1 5.1 %collective-permute-start.4 = (f32[32,1]{1,0:T(8,128)S(1)}, f32[32,1]{1,0:T(8,128)S(1)}, u32[]{:S(2)}, u32[]{:S(2)}) collective-permute-start(f32[32,1]{1,0:T(8,128)S(1)} %get-tuple-element.58), channel_id=1, source_target_pairs={{0,1},{1,2},{2,3},{3,4},{4,5},{5,6},{6,7},{7,8},{8,9},{9,10},{10,1... | collective-permute-start | bytes 392 | tf_op jit(solution)/shard_map/ppermute | solution.py:31
  48.2 5.1 %collective-permute-start.5 = (f32[32,1]{1,0:T(8,128)S(1)}, f32[32,1]{1,0:T(8,128)S(1)}, u32[]{:S(2)}, u32[]{:S(2)}) collective-permute-start(f32[32,1]{1,0:T(8,128)S(1)} %get-tuple-element.59), channel_id=1, source_target_pairs={{1,0},{2,1},{3,2},{4,3},{5,4},{6,5},{7,6},{8,7},{9,8},{10,9},{11,1... | collective-permute-start | bytes 392 | tf_op jit(solution)/shard_map/ppermute | solution.py:31
  56.0 23.2 %all-to-all-start.1 = ((f32[128,1,128]{2,1,0:T(1,128)}), f32[128,1,128]{2,1,0:T(1,128)S(1)}, u32[]{:S(2)}, u32[]{:S(2)}) async-start(f32[128,1,128]{2,1,0:T(1,128)} %broadcast_in_dim.104), calls=%async_computation.1 | async-start | bytes 131072 | tf_op jit(solution)/shard_map/all_to_all | solution.py:25
  86.6 30.1 %all-to-all-start.2 = ((f32[32,1,640]{2,1,0:T(1,128)}), f32[32,1,640]{2,1,0:T(1,128)S(1)}, u32[]{:S(2)}, u32[]{:S(2)}) async-start(f32[32,1,640]{2,1,0:T(1,128)} %broadcast_in_dim.106), calls=%async_computation.2 | async-start | bytes 163840 | tf_op jit(solution)/shard_map/all_to_all | solution.py:25
  120.6 13.1 %all-to-all-start.3 = ((f32[32,1,1152]{2,1,0:T(1,128)}), f32[32,1,1152]{2,1,0:T(1,128)S(1)}, u32[]{:S(2)}, u32[]{:S(2)}) async-start(f32[32,1,1152]{2,1,0:T(1,128)} %broadcast_in_dim.108), calls=%async_computation.3 | async-start | bytes 294912 | tf_op jit(solution)/shard_map/all_to_all | solution.py:25

commit v2 on v0

v2 whole, which is shorter than its diff:
```python
import functools

import jax
import jax.numpy as jnp
from jax import lax
from jax.experimental import pallas as pl
from jax.experimental.pallas import tpu as pltpu
from jax.sharding import Mesh, PartitionSpec as P

CHEB = 4
REACTION = 0.05
EIGEN_TOP = 2.0
EIGEN_LOW = 0.1
LANES = 128

ROWS = ("zh", "zl")
COLS = ("xy", "core")
GROUP = ("zl", "xy", "core")
STACK = ("zh", "zl", "core")
PLANE = ("xy",)
FINE = ("zh", "zl", "xy", "core")
VMEM_LIMIT = 24 * 1024 * 1024


def iota(shape, dim):
    return lax.broadcasted_iota(jnp.int32, shape, dim)


def harmonic(centre, beside):
    return jnp.where(beside > 0.0, 2.0 * centre * beside / (centre + beside), centre)


def shifts(v):
    rows, columns = v.shape
    return (
        pltpu.roll(v, 1, 0),
        pltpu.roll(v, rows - 1, 0),
        pltpu.roll(v, 1, 1),
        pltpu.roll(v, columns - 1, 1),
    )


def edges_of(shape):
    row, column = iota(shape, 0), iota(shape, 1)
    return (row == 0, row == shape[0] - 1, column == 0, column == shape[1] - 1)


class Stencil:
    def __init__(self, coef):
        self.faces = tuple(coef[k] for k in range(4))
        self.diagonal, self.inverse = coef[4], coef[5]
        self.edges = edges_of(self.diagonal.shape)
        self.inner = tuple(
            jnp.where(edge, 0.0, face) for edge, face in zip(self.edges, self.faces)
        )

    def apply(self, v):
        result = self.diagonal * v
        for weight, near in zip(self.inner, shifts(v)):
            result = result - weight * near
        return result

    def smooth(self, source):
        centre = 0.5 * (EIGEN_TOP + EIGEN_LOW)
        radius = 0.5 * (EIGEN_TOP - EIGEN_LOW)
        ratio_start = centre / radius
        factor = 1.0 / ratio_start
        update = source * self.inverse * (1.0 / centre)
        smoothed = update
        for _ in range(1, CHEB):
            defect = source - self.apply(smoothed)
            factor_next = 1.0 / (2.0 * ratio_start - factor)
            update = factor_next * factor * update + (2.0 * factor_next / radius) * (
                defect * self.inverse
            )
            smoothed = smoothed + update
            factor = factor_next
        return smoothed


def to_lanes(column, start):
    n = column.shape[0]
    want = lax.rem(iota((n, LANES), 1) - start + 8 * LANES, LANES)
    hit = want == iota((n, LANES), 0)
    return jnp.sum(jnp.where(hit, column, 0.0), axis=0, keepdims=True)


def to_column(row, start, n):
    want = lax.rem(iota((n, LANES), 1) - start + 8 * LANES, LANES)
    hit = want == iota((n, LANES), 0)
    return jnp.sum(jnp.where(hit, row, 0.0), axis=1, keepdims=True)


def project(e_ref, v, rows_ref):
    nev, rows, columns = e_ref.shape
    for e in range(nev):
        p = e_ref[e] * v
        q = p[:, :LANES]
        for k in range(1, columns // LANES):
            q = q + p[:, k * LANES : (k + 1) * LANES]
        s = q[:8]
        for k in range(1, rows // 8):
            s = s + q[8 * k : 8 * k + 8]
        rows_ref[e : e + 1, :] = jnp.sum(s, axis=0, keepdims=True)
    return jnp.sum(rows_ref[...], axis=1, keepdims=True)


def coarse(c_ref, gathered_ref, nev):
    dofs = c_ref.shape[1]
    lane = iota((1, LANES), 1)
    total = None
    for r in range(dofs // LANES):
        low = r * LANES // nev
        high = (r * LANES + LANES - 1) // nev
        flat = gathered_ref[low : low + 1, :]
        for d in range(low + 1, high + 1):
            flat = jnp.where(lane >= d * nev - r * LANES, gathered_ref[d : d + 1, :], flat)
        term = c_ref[:, r * LANES : (r + 1) * LANES] * flat
        total = term if total is None else total + term
    return jnp.sum(total, axis=1, keepdims=True)


def prolong(e_ref, y, rows_ref):
    nev = e_ref.shape[0]
    rows_ref[...] = jnp.broadcast_to(y, (nev, LANES))
    reps = e_ref.shape[2] // LANES
    result = None
    for e in range(nev):
        weight = jnp.concatenate([rows_ref[e : e + 1, :]] * reps, axis=1)
        term = weight * e_ref[e]
        result = term if result is None else result + term
    return result


def total_of(v):
    return jnp.sum(jnp.sum(v, axis=0, keepdims=True), axis=1, keepdims=True)


def group_place():
    return (lax.axis_index("zl") * lax.axis_size("xy") + lax.axis_index("xy")) * 2 + lax.axis_index(
        "core"
    )


def lane_start(place, nev):
    return lax.rem(place * nev, LANES)


def opening_kernel(kinds_ref, r_ref, map_ref, e_ref, perm_ref, over_ref, in_ref, out_ref, rows_ref):
    nev, rows, _ = e_ref.shape
    classes = map_ref[...]
    perm = jnp.full(classes.shape, kinds_ref[0])
    for k in range(1, kinds_ref.shape[0]):
        perm = jnp.where(classes == k, kinds_ref[k], perm)
    perm_ref[...] = perm
    upper = lax.axis_index("zl") == 0
    over_ref[...] = jnp.where(upper, perm[:1], perm[-1:])
    in_ref[...] = jnp.where(upper, perm[-1:], perm[:1])
    c = project(e_ref, r_ref[...], rows_ref)
    start = lane_start(group_place(), nev)
    message = to_lanes(c, start) + to_lanes(perm[:, :1], start + nev)
    message = message + to_lanes(perm[:, -1:], start + nev + rows)
    out_ref[...] = jnp.broadcast_to(message, out_ref.shape)


def first_kernel(
    got_ref, over_ref, in_ref, perm_ref, r_ref, e_ref, c_ref,
    z_ref, coef_ref, z_over_ref, z_in_ref, y_over_ref, y_in_ref, rows_ref,
):
    nev, rows, columns = e_ref.shape
    xy, core = lax.axis_index("xy"), lax.axis_index("core")
    b = xy * 2 + core
    b_count = lax.axis_size("xy") * 2
    upper = lax.axis_index("zl") == 0
    place = group_place()
    before, after = jnp.maximum(place - 1, 0), jnp.minimum(place + 1, got_ref.shape[0] - 1)
    left = to_column(got_ref[pl.ds(before, 1), :], lane_start(before, nev) + nev + rows, rows)
    right = to_column(got_ref[pl.ds(after, 1), :], lane_start(after, nev) + nev, rows)
    left = jnp.where(b > 0, left, 0.0)
    right = jnp.where(b < b_count - 1, right, 0.0)
    over, within = over_ref[...], in_ref[...]
    halo = (jnp.where(upper, over, within), jnp.where(upper, within, over), left, right)
    perm = perm_ref[...]
    edges = edges_of(perm.shape)
    faces = []
    for edge, near, outside in zip(edges, shifts(perm), halo):
        faces.append(harmonic(perm, jnp.where(edge, outside, near)))
    diagonal = REACTION + faces[0] + faces[1] + faces[2] + faces[3]
    coef = faces + [diagonal, 1.0 / diagonal]
    for k in range(6):
        coef_ref[k] = coef[k]
    stencil = Stencil(coef)
    y = coarse(c_ref, got_ref, nev)
    z = stencil.smooth(r_ref[...]) + prolong(e_ref, y, rows_ref)
    z_ref[...] = z
    top, low = (faces[0] * z)[:1], (faces[1] * z)[-1:]
    z_over_ref[...] = jnp.where(upper, top, low)
    z_in_ref[...] = jnp.where(upper, low, top)
    lefts, rights = to_lanes((faces[2] * z)[:, :1], 0), to_lanes((faces[3] * z)[:, -1:], 0)
    y_over_ref[...] = jnp.where(core == 0, lefts, rights)
    y_in_ref[...] = jnp.where(core == 0, rights, lefts)


def second_kernel(
    z_over_ref, z_in_ref, y_over_ref, y_in_ref, z_ref, coef_ref, e_ref, q_ref, out_ref, rows_ref
):
    nev, rows, _ = e_ref.shape
    upper = lax.axis_index("zl") == 0
    first = lax.axis_index("core") == 0
    stencil = Stencil(coef_ref)
    over, within = z_over_ref[...], z_in_ref[...]
    y_over, y_in = to_column(y_over_ref[...], 0, rows), to_column(y_in_ref[...], 0, rows)
    halo = (
        jnp.where(upper, over, within),
        jnp.where(upper, within, over),
        jnp.where(first, y_over, y_in),
        jnp.where(first, y_in, y_over),
    )
    q = stencil.apply(z_ref[...])
    for edge, outside in zip(stencil.edges, halo):
        q = q - jnp.where(edge, outside, 0.0)
    q_ref[...] = q
    message = to_lanes(project(e_ref, q, rows_ref), lane_start(group_place(), nev))
    out_ref[...] = jnp.broadcast_to(message, out_ref.shape)


def third_kernel(
    got_ref, q_ref, z_ref, r_ref, coef_ref, e_ref, c_ref, w_ref, v_ref, out_ref, rows_ref, block_ref
):
    nev, rows, columns = e_ref.shape
    half = columns // LANES
    stencil = Stencil(coef_ref)
    q, z, r = q_ref[...], z_ref[...], r_ref[...]
    y = coarse(c_ref, got_ref, nev)
    w = stencil.smooth(q) + prolong(e_ref, y, rows_ref)
    v = stencil.apply(w)
    w_ref[...] = w
    v_ref[...] = v
    position = lax.rem(lax.axis_index("zh") * 2 + lax.axis_index("zl"), LANES // rows) * rows
    low = (stencil.faces[1] * w)[-1:]
    block_ref[...] = jnp.zeros_like(block_ref)
    for k in range(half):
        block_ref[k : k + 1, :] = low[:, k * LANES : (k + 1) * LANES]
        block_ref[half + k : half + k + 1, :] = w[:1, k * LANES : (k + 1) * LANES]
    block_ref[2 * half : 2 * half + 1, :] = to_lanes(w[:, :1], position)
    block_ref[2 * half + 1 : 2 * half + 2, :] = to_lanes(
        (stencil.faces[3] * w)[:, -1:], position
    )
    lane = iota((1, LANES), 1)
    sums = jnp.zeros((1, LANES), jnp.float32)
    for k, product in enumerate((r * z, z * q, r * w, q * w, w * v)):
        sums = jnp.where(lane == k, total_of(product), sums)
    block_ref[2 * half + 2 : 2 * half + 3, :] = sums
    out_ref[...] = jnp.broadcast_to(block_ref[...][None], out_ref.shape)


def fourth_kernel(got_ref, v_ref, coef_ref, v_out_ref, out_ref, block_ref):
    count, height, _ = got_ref.shape
    rows, columns = v_ref.shape
    half = columns // LANES
    z_count = count // 2
    z = lax.axis_index("zh") * 2 + lax.axis_index("zl")
    core = lax.axis_index("core")
    sub = iota((height, LANES), 0)
    lane = iota((1, LANES), 1)
    total = jnp.zeros((height, LANES), jnp.float32)
    flat = jnp.zeros((1, LANES), jnp.float32)
    for i in range(count):
        total = total + got_ref[i]
    for i in range(z_count - 1):
        for c in range(2):
            for k in range(half):
                here = got_ref[2 * i + c, k : k + 1, :]
                below = got_ref[2 * i + 2 + c, half + k : half + k + 1, :]
                flat = flat + here * below
    for i in range(z_count):
        flat = flat + (
            got_ref[2 * i, 2 * half + 1 : 2 * half + 2, :]
            * got_ref[2 * i + 1, 2 * half : 2 * half + 1, :]
        )
    between = jnp.sum(flat, axis=1, keepdims=True)
    sums = total[2 * half + 2 : 2 * half + 3]
    sums = jnp.where(lane == 4, sums - 2.0 * between, sums)
    pack = LANES // rows
    zr = z_count // pack
    for g in range(zr):
        lefts, rights = None, None
        for i in range(g * pack, (g + 1) * pack):
            a = got_ref[2 * i, 2 * half : 2 * half + 1, :]
            d = got_ref[2 * i + 1, 2 * half + 1 : 2 * half + 2, :]
            lefts = a if lefts is None else lefts + a
            rights = d if rights is None else rights + d
        block_ref[g : g + 1, :] = lefts
        block_ref[zr + g : zr + g + 1, :] = rights
    block_ref[2 * zr : 2 * zr + 1, :] = sums
    message = block_ref[...]
    size = block_ref.shape[0]
    for i in range(out_ref.shape[0] // size):
        out_ref[i * size : (i + 1) * size, :] = message

    above = got_ref[jnp.maximum(2 * z - 2 + core, 0)]
    below = got_ref[jnp.minimum(2 * z + 2 + core, count - 1)]
    up = jnp.concatenate([above[k : k + 1] for k in range(half)], axis=1)
    down = jnp.concatenate([below[half + k : half + k + 1] for k in range(half)], axis=1)
    up = jnp.where(z > 0, up, 0.0)
    down = jnp.where(z < z_count - 1, down, 0.0) * coef_ref[1, rows - 1 : rows, :]
    partner = got_ref[2 * z + 1 - core]
    position = lax.rem(z, pack) * rows
    left = to_column(partner[2 * half + 1 : 2 * half + 2], position, rows)
    right = to_column(partner[2 * half : 2 * half + 1], position, rows)
    edges = edges_of((rows, columns))
    v = v_ref[...]
    v = v - jnp.where(edges[0], up, 0.0) - jnp.where(edges[1], down, 0.0)
    v = v - jnp.where(edges[2], jnp.where(core == 1, left, 0.0), 0.0)
    v = v - jnp.where(edges[3], jnp.where(core == 0, right, 0.0) * coef_ref[3], 0.0)
    v_out_ref[...] = v


def closing_kernel(got_ref, v_ref, z_ref, w_ref, q_ref, r_ref, coef_ref, x_ref, res_ref):
    rows, columns = v_ref.shape
    pack = LANES // rows
    zr = lax.axis_size("zh") * 2 // pack
    size = 2 * zr + 1
    count = got_ref.shape[0] // size
    z = lax.axis_index("zh") * 2 + lax.axis_index("zl")
    xy, core = lax.axis_index("xy"), lax.axis_index("core")
    sums = got_ref[2 * zr : 2 * zr + 1, :]
    flat = jnp.zeros((zr, LANES), jnp.float32)
    for i in range(1, count):
        at = i * size
        sums = sums + got_ref[at + 2 * zr : at + 2 * zr + 1, :]
        flat = flat + got_ref[at - size + zr : at - size + 2 * zr, :] * got_ref[at : at + zr, :]
    across = total_of(flat)
    lane = iota((1, LANES), 1)
    rz, zq, rw, qw, wv = (
        jnp.sum(jnp.where(lane == k, sums, 0.0), axis=1, keepdims=True) for k in range(5)
    )
    wv = wv - 2.0 * across
    step = rz / zq
    rz_new = rz - step * ((rw + zq) - step * qw)
    grow = 1.0 + rz_new / rz
    curve = grow * grow * zq - 2.0 * grow * step * qw + step * step * wv
    step_next = rz_new / curve
    on_z = step + step_next * grow
    on_w = step_next * step

    left_of, right_of = jnp.maximum(xy - 1, 0), jnp.minimum(xy + 1, count - 1)
    row = z // pack
    position = lax.rem(z, pack) * rows
    left = to_column(got_ref[pl.ds(left_of * size + zr + row, 1), :], position, rows)
    right = to_column(got_ref[pl.ds(right_of * size + row, 1), :], position, rows)
    left = jnp.where((core == 0) & (xy > 0), left, 0.0)
    right = jnp.where((core == 1) & (xy < count - 1), right, 0.0)
    edges = edges_of((rows, columns))
    v = v_ref[...]
    v = v - jnp.where(edges[2], left, 0.0) - jnp.where(edges[3], right * coef_ref[3], 0.0)
    x_ref[...] = on_z * z_ref[...] - on_w * w_ref[...]
    res_ref[...] = r_ref[...] - on_z * q_ref[...] + on_w * v


def call(kernel, name, args, outs, scratch=(), smem=()):
    whole = pl.BlockSpec(memory_space=pltpu.VMEM)
    scalar = pl.BlockSpec(memory_space=pltpu.SMEM)
    return pl.pallas_call(
        kernel,
        out_shape=[jax.ShapeDtypeStruct(shape, jnp.float32) for shape in outs],
        in_specs=[scalar if k in smem else whole for k in range(len(args))],
        out_specs=[whole] * len(outs),
        scratch_shapes=[pltpu.VMEM(shape, jnp.float32) for shape in scratch],
        compiler_params=pltpu.CompilerParams(vmem_limit_bytes=VMEM_LIMIT),
        name=name,
    )(*args)


def exchanged(x, axes):
    return lax.all_to_all(x, axes, 0, 0, tiled=True)


def swap_in(x, axis):
    return lax.ppermute(x, axis, [(0, 1), (1, 0)])


def swap_over(x, axes):
    count = lax.axis_size(axes)
    pairs = [(i, i + 1) for i in range(1, count - 1, 2)]
    return lax.ppermute(x, axes, pairs + [(j, i) for i, j in pairs])


def local(right_side, class_map, class_perm, eigenvectors, coarse_inverse):
    rows, columns = right_side.shape
    nev = eigenvectors.shape[0]
    field = (rows, columns)
    group = 2 * lax.axis_size(COLS)
    z_count, chips = lax.axis_size(ROWS), lax.axis_size("xy")
    size = 2 * (z_count * rows // LANES) + 1
    per_vector = (nev, LANES)

    perm, over, within, message = call(
        opening_kernel, "opening", (class_perm, right_side, class_map, eigenvectors),
        [field, (1, columns), (1, columns), (group, LANES)], [per_vector], smem=(0,),
    )
    over, within = swap_over(over, ROWS), swap_in(within, "zl")
    got = exchanged(message, GROUP)
    z0, coef, z_over, z_in, y_over, y_in = call(
        first_kernel, "first",
        (got, over, within, perm, right_side, eigenvectors, coarse_inverse),
        [field, (6,) + field, (1, columns), (1, columns), (1, LANES), (1, LANES)], [per_vector],
    )
    z_over, z_in = swap_over(z_over, ROWS), swap_in(z_in, "zl")
    y_over, y_in = swap_over(y_over, COLS), swap_in(y_in, "core")
    q0, message = call(
        second_kernel, "second", (z_over, z_in, y_over, y_in, z0, coef, eigenvectors),
        [field, (group, LANES)], [per_vector],
    )
    got = exchanged(message, GROUP)
    w, v, message = call(
        third_kernel, "third", (got, q0, z0, right_side, coef, eigenvectors, coarse_inverse),
        [field, field, (2 * z_count, 8, LANES)], [per_vector, (8, LANES)],
    )
    got = exchanged(message, STACK)
    v, message = call(
        fourth_kernel, "fourth", (got, v, coef),
        [field, (chips * size, LANES)], [(size, LANES)],
    )
    got = exchanged(message.reshape(chips, size * LANES), PLANE).reshape(chips * size, LANES)
    return tuple(
        call(
            closing_kernel, "closing", (got, v, z0, w, q0, right_side, coef), [field, field]
        )
    )


def solution(mesh):
    n_gx, n_gy = mesh.devices.shape
    fine = Mesh(mesh.devices.reshape(n_gx // 2, 2, n_gy // 2, 2), FINE)
    in_specs = (P(ROWS, COLS), P(ROWS, COLS), P(), P(None, ROWS, COLS), P(FINE, None))
    out_specs = (P(ROWS, COLS), P(ROWS, COLS))
    return jax.shard_map(local, mesh=fine, in_specs=in_specs, out_specs=out_specs, check_vma=False)
```

time: 942 us -> 115 us (0.12)
  blocking collectives: 867 us -> 63.6 us
    unnamed x2 -> x0, blocking collectives: 493 us -> none
    psum x3 -> x0, blocking collectives: 374 us -> none  [the longest x2 249 us: dot_residual(): return lax.psum(jnp.sum(residual * preconditioned), ('gx', 'gy'))]
    all_to_all x0 -> x3, blocking collectives: none -> 63.6 us  [exchanged(): return lax.all_to_all(x, axes, 0, 0, tiled=True)]
    ppermute x14 -> x6, starting transfers between devices: 39.5 us -> 15.8 us  [the longest x3 10.4 us: swap_in(): return lax.ppermute(x, axis, [(0, 1), (1, 0)])]
    all_to_all x0 -> x1, starting transfers between devices: none -> 19.2 us  [exchanged(): return lax.all_to_all(x, axes, 0, 0, tiled=True)]
    ppermute x14 -> x6, waiting for transfers between devices: 13.9 us -> 2.02 us  [the longest x3 2.01 us: swap_in(): return lax.ppermute(x, axis, [(0, 1), (1, 0)])]
  transfers between devices with their start and end apart: 14 -> 7, of which waited for: 6 -> 3; matrix products, arithmetic and copies ran while one was open for 1% -> 0% of each run, Pallas kernels for 0% -> 0%
where the time goes in v2:
time: 115 us; the launch traced here: 114 us
  blocking collectives  63.6 us (55%)
  starting transfers between devices  35 us (30%)
  waiting for transfers between devices  5.98 us (5%)
  local copies, waits for them, and re-layouts  4.64 us (4%)
  Pallas kernels  3.74 us (3%)
    all_to_all x3, blocking collectives, exchanged(): return lax.all_to_all(x, axes, 0, 0, tiled=True)  63.6 us
    all_to_all x1, starting transfers between devices, exchanged(): return lax.all_to_all(x, axes, 0, 0, tiled=True)  19.2 us
    ppermute x3, starting transfers between devices, swap_in(): return lax.ppermute(x, axis, [(0, 1), (1, 0)])  10.4 us
    ppermute x3, starting transfers between devices, swap_over(): return lax.ppermute(x, axes, pairs + [(j, i) for i, j in pairs])  5.36 us
    unnamed x16, local copies, waits for them, and re-layouts  4.64 us
    all_to_all x1, waiting for transfers between devices, exchanged(): return lax.all_to_all(x, axes, 0, 0, tiled=True)  3.96 us
    pallas_call x6, Pallas kernels, call(): pl.pallas_call(kernel, out_shape=[jax.ShapeDtypeStruct(shape, jnp.float32...  3.74 us
  transfers between devices with their start and end apart: 7, of which 3 were waited for; matrix products, arithmetic and copies ran while one was open for 0% of the time, Pallas kernels for 0%

profile of v2, /device:TPU:1, one launch (start us, length us, event | category | flops | bytes accessed | tf_op | source)
XLA Modules:
  0.0 113.8 jit_solution(11287183963787249345)
XLA Ops:
  0.6 1.3 %copy-done = f32[40,32,256]{2,1,0:T(8,128)S(1)} copy-done((f32[40,32,256]{2,1,0:T(8,128)S(1)}, f32[40,32,256]{2,1,0:T(8,128)}, u32[]{:S(2)}) %copy-start) | copy-done | bytes 1310744
  1.9 0.8 copy-done.4
  2.7 0.8 copy-done.6
  3.5 0.7 copy-done.7
  4.1 1.4 %opening.1 = (f32[32,256]{1,0:T(8,128)S(1)}, f32[1,256]{1,0:T(1,128)S(1)}, f32[1,256]{1,0:T(1,128)S(1)}, f32[128,128]{1,0:T(8,128)}) custom-call(f32[4]{0:T(128)S(1)} %copy-done.7, f32[32,256]{1,0:T(8,128)S(1)} %copy-done.4, s32[32,256]{1,0:T(8,128)S(1)} %copy-done.6, f32[40,32,256]{2,1,0:T(8,128)S(1)} %copy-done), custom_call_target="tpu_custom_call" | custom-call | tf_op jit(solution)/shard_map/opening/pallas_call | solution.py:364
  5.5 19.2 %all-to-all-start = ((f32[128,1,128]{2,1,0:T(1,128)}), f32[128,1,128]{2,1,0:T(1,128)S(1)}, u32[]{:S(2)}, u32[]{:S(2)}) async-start(f32[128,1,128]{2,1,0:T(1,128)} %bitcast.1), calls=%async_computation | async-start | bytes 131072 | tf_op jit(solution)/shard_map/all_to_all | solution.py:376
  24.8 0.7 collective-permute-start
  25.4 5.0 %collective-permute-start.1 = (f32[1,256]{1,0:T(1,128)S(1)}, f32[1,256]{1,0:T(1,128)S(1)}, u32[]{:S(2)}, u32[]{:S(2)}) collective-permute-start(f32[1,256]{1,0:T(1,128)S(1)} %get-tuple-element.21), channel_id=1, source_target_pairs={{0,64},{64,0},{1,65},{65,1},{2,66},{66,2},{3,67},{67,3},{4,68},{68... | collective-permute-start | bytes 3080 | tf_op jit(solution)/shard_map/ppermute | solution.py:380
  30.4 0.9 collective-permute-done.1.in_ref
  31.4 4.0 %all-to-all-done = f32[128,1,128]{2,1,0:T(1,128)S(1)} async-done(((f32[128,1,128]{2,1,0:T(1,128)}), f32[128,1,128]{2,1,0:T(1,128)S(1)}, u32[]{:S(2)}, u32[]{:S(2)}) %all-to-all-start) | async-done | bytes 65568 | tf_op jit(solution)/shard_map/all_to_all | solution.py:376
  35.3 1.1 %copy-done.2 = f32[40,5120]{1,0:T(8,128)S(1)} copy-done((f32[40,5120]{1,0:T(8,128)S(1)}, f32[40,5120]{1,0:T(8,128)}, u32[]{:S(2)}) %copy-start.2) | copy-done | bytes 819224
  36.5 0.5 first.1
  37.0 0.8 collective-permute-start.2
  37.8 3.5 %collective-permute-start.3 = (f32[1,256]{1,0:T(1,128)S(1)}, f32[1,256]{1,0:T(1,128)S(1)}, u32[]{:S(2)}, u32[]{:S(2)}) collective-permute-start(f32[1,256]{1,0:T(1,128)S(1)} %get-tuple-element.24), channel_id=1, source_target_pairs={{0,64},{64,0},{1,65},{65,1},{2,66},{66,2},{3,67},{67,3},{4,68},{68... | collective-permute-start | bytes 3080 | tf_op jit(solution)/shard_map/ppermute | solution.py:380
  41.4 3.9 %collective-permute-start.4 = (f32[1,128]{1,0:T(1,128)S(1)}, f32[1,128]{1,0:T(1,128)S(1)}, u32[]{:S(2)}, u32[]{:S(2)}) collective-permute-start(f32[1,128]{1,0:T(1,128)S(1)} %get-tuple-element.25), channel_id=1, source_target_pairs={{1,2},{3,4},{5,6},{7,8},{9,10},{11,12},{13,14},{15,16},{17,18},{19... | collective-permute-start | bytes 1544 | tf_op jit(solution)/shard_map/ppermute | solution.py:386
  45.3 1.9 %collective-permute-start.5 = (f32[1,128]{1,0:T(1,128)S(1)}, f32[1,128]{1,0:T(1,128)S(1)}, u32[]{:S(2)}, u32[]{:S(2)}) collective-permute-start(f32[1,128]{1,0:T(1,128)S(1)} %get-tuple-element.26), channel_id=1, source_target_pairs={{0,1},{1,0},{2,3},{3,2},{4,5},{5,4},{6,7},{7,6},{8,9},{9,8},{10,11... | collective-permute-start | bytes 1544 | tf_op jit(solution)/shard_map/ppermute | solution.py:380
  47.2 1.1 collective-permute-done.5.y_in_ref
  48.3 0.4 second.1
  48.7 21.0 %all_to_all.36 = f32[128,1,128]{2,1,0:T(1,128)S(1)} all-to-all(f32[128,1,128]{2,1,0:T(1,128)S(1)} %bitcast.14), channel_id=1, replica_groups=mesh['zh'=8,'zl'=2,'xy'=32,'core'=2] {'zl','xy','core'}, dimensions={0} | all-to-all | bytes 131072 | tf_op jit(solution)/shard_map/all_to_all | solution.py:376
  69.7 0.5 third.1
  70.2 30.3 %all_to_all.37.got_ref = f32[32,8,128]{2,1,0:T(8,128)S(1)} all-to-all(f32[32,8,128]{2,1,0:T(8,128)S(1)} %get-tuple-element.31), channel_id=1, replica_groups=mesh['zh'=8,'zl'=2,'xy'=32,'core'=2] {'zh','zl','core'}, dimensions={0} | all-to-all | bytes 262144 | tf_op jit(solution)/shard_map/all_to_all | solution.py:376
  100.6 0.2 fourth.1
  100.7 12.3 %all_to_all.38 = f32[32,1,1152]{2,1,0:T(1,128)S(1)} all-to-all(f32[32,1,1152]{2,1,0:T(1,128)S(1)} %bitcast.13), channel_id=1, replica_groups=mesh['zh'=8,'zl'=2,'xy'=32,'core'=2] {'xy'}, dimensions={0} | all-to-all | bytes 294912 | tf_op jit(solution)/shard_map/all_to_all | solution.py:376
  113.0 0.8 closing.1
  (15 shorter events, 0.0 us)
Async XLA Ops:
  0.6 1.3 %copy-start = (f32[40,32,256]{2,1,0:T(8,128)S(1)}, f32[40,32,256]{2,1,0:T(8,128)}, u32[]{:S(2)}) copy-start(f32[40,32,256]{2,1,0:T(8,128)} %e_ref.7) | copy-start | bytes 3932164
  1.9 0.8 copy-start.4
  2.7 0.8 copy-start.6
  3.5 0.7 copy-start.7
  4.1 31.2 %copy-start.1 = (f32[40,32,256]{2,1,0:T(8,128)S(1)}, f32[40,32,256]{2,1,0:T(8,128)}, u32[]{:S(2)}) copy-start(f32[40,32,256]{2,1,0:T(8,128)} %e_ref.7) | copy-start | bytes 3932164
  4.1 31.2 %copy-start.5 = (f32[32,256]{1,0:T(8,128)S(1)}, f32[32,256]{1,0:T(8,128)}, u32[]{:S(2)}) copy-start(f32[32,256]{1,0:T(8,128)} %r_ref.7) | copy-start | bytes 98308
  5.5 29.8 %all-to-all-start = ((f32[128,1,128]{2,1,0:T(1,128)}), f32[128,1,128]{2,1,0:T(1,128)S(1)}, u32[]{:S(2)}, u32[]{:S(2)}) async-start(f32[128,1,128]{2,1,0:T(1,128)} %bitcast.1), calls=%async_computation | async-start | bytes 131072 | tf_op jit(solution)/shard_map/all_to_all | solution.py:376
  24.8 5.7 %collective-permute-start = (f32[1,256]{1,0:T(1,128)S(1)}, f32[1,256]{1,0:T(1,128)S(1)}, u32[]{:S(2)}, u32[]{:S(2)}) collective-permute-start(f32[1,256]{1,0:T(1,128)S(1)} %get-tuple-element.20), channel_id=1, source_target_pairs={{64,128},{192,256},{320,384},{448,512},{576,640},{704,768},{832,89... | collective-permute-start | bytes 3080 | tf_op jit(solution)/shard_map/ppermute | solution.py:386
  25.4 5.9 %collective-permute-start.1 = (f32[1,256]{1,0:T(1,128)S(1)}, f32[1,256]{1,0:T(1,128)S(1)}, u32[]{:S(2)}, u32[]{:S(2)}) collective-permute-start(f32[1,256]{1,0:T(1,128)S(1)} %get-tuple-element.21), channel_id=1, source_target_pairs={{0,64},{64,0},{1,65},{65,1},{2,66},{66,2},{3,67},{67,3},{4,68},{68... | collective-permute-start | bytes 3080 | tf_op jit(solution)/shard_map/ppermute | solution.py:380
  35.3 1.1 %copy-start.2 = (f32[40,5120]{1,0:T(8,128)S(1)}, f32[40,5120]{1,0:T(8,128)}, u32[]{:S(2)}) copy-start(f32[40,5120]{1,0:T(8,128)} %c_ref.3) | copy-start | bytes 2457604
  37.0 32.7 %copy-start.3 = (f32[40,5120]{1,0:T(8,128)S(1)}, f32[40,5120]{1,0:T(8,128)}, u32[]{:S(2)}) copy-start(f32[40,5120]{1,0:T(8,128)} %c_ref.3) | copy-start | bytes 2457604
  37.0 11.3 %collective-permute-start.2 = (f32[1,256]{1,0:T(1,128)S(1)}, f32[1,256]{1,0:T(1,128)S(1)}, u32[]{:S(2)}, u32[]{:S(2)}) collective-permute-start(f32[1,256]{1,0:T(1,128)S(1)} %get-tuple-element.23), channel_id=1, source_target_pairs={{64,128},{192,256},{320,384},{448,512},{576,640},{704,768},{832,89... | collective-permute-start | bytes 3080 | tf_op jit(solution)/shard_map/ppermute | solution.py:386
  37.8 10.5 %collective-permute-start.3 = (f32[1,256]{1,0:T(1,128)S(1)}, f32[1,256]{1,0:T(1,128)S(1)}, u32[]{:S(2)}, u32[]{:S(2)}) collective-permute-start(f32[1,256]{1,0:T(1,128)S(1)} %get-tuple-element.24), channel_id=1, source_target_pairs={{0,64},{64,0},{1,65},{65,1},{2,66},{66,2},{3,67},{67,3},{4,68},{68... | collective-permute-start | bytes 3080 | tf_op jit(solution)/shard_map/ppermute | solution.py:380
  41.4 5.8 %collective-permute-start.4 = (f32[1,128]{1,0:T(1,128)S(1)}, f32[1,128]{1,0:T(1,128)S(1)}, u32[]{:S(2)}, u32[]{:S(2)}) collective-permute-start(f32[1,128]{1,0:T(1,128)S(1)} %get-tuple-element.25), channel_id=1, source_target_pairs={{1,2},{3,4},{5,6},{7,8},{9,10},{11,12},{13,14},{15,16},{17,18},{19... | collective-permute-start | bytes 1544 | tf_op jit(solution)/shard_map/ppermute | solution.py:386
  45.3 3.0 %collective-permute-start.5 = (f32[1,128]{1,0:T(1,128)S(1)}, f32[1,128]{1,0:T(1,128)S(1)}, u32[]{:S(2)}, u32[]{:S(2)}) collective-permute-start(f32[1,128]{1,0:T(1,128)S(1)} %get-tuple-element.26), channel_id=1, source_target_pairs={{0,1},{1,0},{2,3},{3,2},{4,5},{5,4},{6,7},{7,6},{8,9},{9,8},{10,11... | collective-permute-start | bytes 1544 | tf_op jit(solution)/shard_map/ppermute | solution.py:380

commit v3 on v2

v3 whole, which is shorter than its diff:
```python
import jax
import jax.numpy as jnp
from jax import lax
from jax.experimental import pallas as pl
from jax.experimental.pallas import tpu as pltpu
from jax.sharding import Mesh, PartitionSpec as P

CHEB = 4
REACTION = 0.05
EIGEN_TOP = 2.0
EIGEN_LOW = 0.1
LANES = 128

ROWS = ("zh", "zl")
COLS = ("xy", "core")
GROUP = ("zl", "xy", "core")
STACK = ("zh", "zl", "core")
PLANE = ("xy",)
FINE = ("zh", "zl", "xy", "core")
VMEM_LIMIT = 24 * 1024 * 1024
PIECES = 5


def iota(shape, dim):
    return lax.broadcasted_iota(jnp.int32, shape, dim)


def harmonic(centre, beside):
    return jnp.where(beside > 0.0, 2.0 * centre * beside / (centre + beside), centre)


def shifts(v):
    rows, columns = v.shape
    return (
        pltpu.roll(v, 1, 0),
        pltpu.roll(v, rows - 1, 0),
        pltpu.roll(v, 1, 1),
        pltpu.roll(v, columns - 1, 1),
    )


def edges_of(shape):
    row, column = iota(shape, 0), iota(shape, 1)
    return (row == 0, row == shape[0] - 1, column == 0, column == shape[1] - 1)


class Stencil:
    def __init__(self, coef):
        self.faces = tuple(coef[k] for k in range(4))
        self.diagonal, self.inverse = coef[4], coef[5]
        self.edges = edges_of(self.diagonal.shape)
        self.inner = tuple(
            jnp.where(edge, 0.0, face) for edge, face in zip(self.edges, self.faces)
        )

    def apply(self, v):
        result = self.diagonal * v
        for weight, near in zip(self.inner, shifts(v)):
            result = result - weight * near
        return result

    def smooth(self, source):
        centre = 0.5 * (EIGEN_TOP + EIGEN_LOW)
        radius = 0.5 * (EIGEN_TOP - EIGEN_LOW)
        ratio_start = centre / radius
        factor = 1.0 / ratio_start
        update = source * self.inverse * (1.0 / centre)
        smoothed = update
        for _ in range(1, CHEB):
            defect = source - self.apply(smoothed)
            factor_next = 1.0 / (2.0 * ratio_start - factor)
            update = factor_next * factor * update + (2.0 * factor_next / radius) * (
                defect * self.inverse
            )
            smoothed = smoothed + update
            factor = factor_next
        return smoothed


def to_lanes(column, start):
    n = column.shape[0]
    want = lax.rem(iota((n, LANES), 1) - start + 8 * LANES, LANES)
    hit = want == iota((n, LANES), 0)
    return jnp.sum(jnp.where(hit, column, 0.0), axis=0, keepdims=True)


def to_column(row, start, n):
    want = lax.rem(iota((n, LANES), 1) - start + 8 * LANES, LANES)
    hit = want == iota((n, LANES), 0)
    return jnp.sum(jnp.where(hit, row, 0.0), axis=1, keepdims=True)


def project_one(own, v, rows_ref, e):
    rows, columns = v.shape
    p = own * v
    q = p[:, :LANES]
    for k in range(1, columns // LANES):
        q = q + p[:, k * LANES : (k + 1) * LANES]
    s = q[:8]
    for k in range(1, rows // 8):
        s = s + q[8 * k : 8 * k + 8]
    rows_ref[e : e + 1, :] = jnp.sum(s, axis=0, keepdims=True)


def project(e_ref, v, rows_ref):
    for e in range(e_ref.shape[0]):
        project_one(e_ref[e], v, rows_ref, e)
    return jnp.sum(rows_ref[...], axis=1, keepdims=True)


def coarse(c_ref, gathered_ref, nev):
    dofs = c_ref.shape[1]
    lane = iota((1, LANES), 1)
    total = None
    for r in range(dofs // LANES):
        low = r * LANES // nev
        high = (r * LANES + LANES - 1) // nev
        flat = gathered_ref[low : low + 1, :]
        for d in range(low + 1, high + 1):
            flat = jnp.where(lane >= d * nev - r * LANES, gathered_ref[d : d + 1, :], flat)
        term = c_ref[:, r * LANES : (r + 1) * LANES] * flat
        total = term if total is None else total + term
    return jnp.sum(total, axis=1, keepdims=True)


def prolong(e_ref, y, rows_ref):
    nev = e_ref.shape[0]
    rows_ref[...] = jnp.broadcast_to(y, (nev, LANES))
    reps = e_ref.shape[2] // LANES
    result = None
    for e in range(nev):
        weight = jnp.concatenate([rows_ref[e : e + 1, :]] * reps, axis=1)
        term = weight * e_ref[e]
        result = term if result is None else result + term
    return result


def total_of(v):
    return jnp.sum(jnp.sum(v, axis=0, keepdims=True), axis=1, keepdims=True)


def group_place():
    return (lax.axis_index("zl") * lax.axis_size("xy") + lax.axis_index("xy")) * 2 + lax.axis_index(
        "core"
    )


def column_place():
    return lax.axis_index("xy") * 2 + lax.axis_index("core")


def lane_start(place, nev):
    return lax.rem(place * nev, LANES)


def opening_kernel(
    kinds_hbm, r_hbm, map_hbm, e_hbm, c_hbm,
    perm_ref, over_ref, in_ref, e_over_ref, e_in_ref, out_ref, r_ref, e_ref, c_ref,
    kinds_ref, map_ref, rows_ref, sems,
):
    nev, rows, columns = e_ref.shape
    steps = sems.shape[0] - 4
    chunk = nev // steps
    small = [
        pltpu.make_async_copy(source, target, sems.at[k])
        for k, (source, target) in enumerate(
            ((kinds_hbm, kinds_ref), (map_hbm, map_ref), (r_hbm, r_ref))
        )
    ]
    parts = [
        pltpu.make_async_copy(
            e_hbm.at[pl.ds(k * chunk, chunk)], e_ref.at[pl.ds(k * chunk, chunk)], sems.at[4 + k]
        )
        for k in range(steps)
    ]
    matrix = pltpu.make_async_copy(c_hbm, c_ref, sems.at[3])
    for copy in small + parts + [matrix]:
        copy.start()
    for copy in small:
        copy.wait()
    classes = map_ref[...]
    perm = jnp.full(classes.shape, kinds_ref[0])
    for k in range(1, kinds_ref.shape[0]):
        perm = jnp.where(classes == k, kinds_ref[k], perm)
    perm_ref[...] = perm
    upper = lax.axis_index("zl") == 0
    first = lax.axis_index("core") == 0
    over_ref[...] = jnp.where(upper, perm[:1], perm[-1:])
    in_ref[...] = jnp.where(upper, perm[-1:], perm[:1])
    r = r_ref[...]
    lane = iota((rows, LANES), 1)
    lefts = jnp.zeros((rows, LANES), jnp.float32)
    rights = lefts
    for k in range(steps):
        parts[k].wait()
        for e in range(k * chunk, (k + 1) * chunk):
            own = e_ref[e]
            project_one(own, r, rows_ref, e)
            lefts = jnp.where(lane == e, own[:, :1], lefts)
            rights = jnp.where(lane == e, own[:, columns - 1 :], rights)
    e_over_ref[...] = jnp.where(first, lefts, rights)
    e_in_ref[...] = jnp.where(first, rights, lefts)
    c = jnp.sum(rows_ref[...], axis=1, keepdims=True)
    start = lane_start(group_place(), nev)
    message = to_lanes(c, start) + to_lanes(perm[:, :1], start + nev)
    message = message + to_lanes(perm[:, -1:], start + nev + rows)
    out_ref[...] = jnp.broadcast_to(message, out_ref.shape)
    matrix.wait()


def beside_columns(got_ref, stride, nev, rows):
    place, b, b_count = group_place(), column_place(), lax.axis_size("xy") * 2
    last = got_ref.shape[0] // stride - 1
    before, after = jnp.maximum(place - 1, 0), jnp.minimum(place + 1, last)
    left = to_column(
        got_ref[pl.ds(before * stride, 1), :], lane_start(before, nev) + nev + rows, rows
    )
    right = to_column(got_ref[pl.ds(after * stride, 1), :], lane_start(after, nev) + nev, rows)
    return jnp.where(b > 0, left, 0.0), jnp.where(b < b_count - 1, right, 0.0)


def first_kernel(
    got_ref, over_ref, in_ref, perm_ref, r_ref, e_ref, c_ref,
    z_ref, coef_ref, z_over_ref, z_in_ref, rows_ref,
):
    nev, rows, columns = e_ref.shape
    upper = lax.axis_index("zl") == 0
    left, right = beside_columns(got_ref, 1, nev, rows)
    over, within = over_ref[...], in_ref[...]
    halo = (jnp.where(upper, over, within), jnp.where(upper, within, over), left, right)
    perm = perm_ref[...]
    edges = edges_of(perm.shape)
    faces = []
    for edge, near, outside in zip(edges, shifts(perm), halo):
        faces.append(harmonic(perm, jnp.where(edge, outside, near)))
    diagonal = REACTION + faces[0] + faces[1] + faces[2] + faces[3]
    coef = faces + [diagonal, 1.0 / diagonal]
    for k in range(6):
        coef_ref[k] = coef[k]
    stencil = Stencil(coef)
    y = coarse(c_ref, got_ref, nev)
    z = stencil.smooth(r_ref[...]) + prolong(e_ref, y, rows_ref)
    z_ref[...] = z
    top, low = (faces[0] * z)[:1], (faces[1] * z)[-1:]
    z_over_ref[...] = jnp.where(upper, top, low)
    z_in_ref[...] = jnp.where(upper, low, top)


def second_kernel(
    z_over_ref, z_in_ref, e_over_ref, e_in_ref, z_ref, coef_ref, e_ref, q_ref, out_ref, rows_ref
):
    nev, rows, _ = e_ref.shape
    upper = lax.axis_index("zl") == 0
    first = lax.axis_index("core") == 0
    stencil = Stencil(coef_ref)
    over, within = z_over_ref[...], z_in_ref[...]
    z = z_ref[...]
    q = stencil.apply(z)
    q = q - jnp.where(stencil.edges[0], jnp.where(upper, over, within), 0.0)
    q = q - jnp.where(stencil.edges[1], jnp.where(upper, within, over), 0.0)
    q_ref[...] = q
    left, right = (stencil.faces[2] * z)[:, :1], (stencil.faces[3] * z)[:, -1:]
    start = lane_start(group_place(), nev)
    own = to_lanes(project(e_ref, q, rows_ref), start)
    own = own + to_lanes(left, start + nev) + to_lanes(right, start + nev + rows)
    e_over, e_in = e_over_ref[...], e_in_ref[...]
    to_left = jnp.sum(jnp.where(first, e_over, e_in) * left, axis=0, keepdims=True)
    to_right = jnp.sum(jnp.where(first, e_in, e_over) * right, axis=0, keepdims=True)
    added = pltpu.roll(to_left, lax.rem(start - nev + LANES, LANES), 1)
    added = added + pltpu.roll(to_right, lax.rem(start + nev, LANES), 1)
    sub = iota((8, LANES), 0)
    pair = jnp.where(lax.rem(sub, 2) == 0, own, -added)
    for k in range(out_ref.shape[0] // 8):
        out_ref[8 * k : 8 * k + 8, :] = pair


def third_kernel(
    got_ref, q_ref, z_ref, r_ref, coef_ref, e_ref, c_ref,
    q_out_ref, w_ref, v_ref, out_ref, rows_ref, block_ref, group_ref,
):
    nev, rows, columns = e_ref.shape
    half = columns // LANES
    count = group_ref.shape[0]
    stencil = Stencil(coef_ref)
    z, r = z_ref[...], r_ref[...]
    left, right = beside_columns(got_ref, 2, nev, rows)
    q = q_ref[...] - jnp.where(stencil.edges[2], left, 0.0)
    q = q - jnp.where(stencil.edges[3], right, 0.0)
    q_out_ref[...] = q
    added = got_ref[pl.ds(1, count, stride=2), :]
    group_ref[...] = (
        got_ref[pl.ds(0, count, stride=2), :]
        + pltpu.roll(added, 1, 0)
        + pltpu.roll(added, count - 1, 0)
    )
    y = coarse(c_ref, group_ref, nev)
    w = stencil.smooth(q) + prolong(e_ref, y, rows_ref)
    v = stencil.apply(w)
    w_ref[...] = w
    v_ref[...] = v
    low = (stencil.faces[1] * w)[-1:]
    for k in range(half):
        block_ref[k : k + 1, :] = low[:, k * LANES : (k + 1) * LANES]
        block_ref[half + k : half + k + 1, :] = w[:1, k * LANES : (k + 1) * LANES]
    last = to_lanes(w[:, :1], 0) + to_lanes((stencil.faces[3] * w)[:, -1:], rows)
    lane = iota((1, LANES), 1)
    for k, product in enumerate((r * z, z * q, r * w, q * w, w * v)):
        last = jnp.where(lane == 2 * rows + k, total_of(product), last)
    size = block_ref.shape[0]
    block_ref[size - 1 : size, :] = last
    message = block_ref[...]
    for i in range(out_ref.shape[0] // size):
        out_ref[i * size : (i + 1) * size, :] = message


def fourth_kernel(got_ref, v_ref, coef_ref, v_out_ref, out_ref, block_ref):
    rows, columns = v_ref.shape
    half = columns // LANES
    size = 2 * half + 1
    count = got_ref.shape[0] // size
    z_count = count // 2
    z = lax.axis_index("zh") * 2 + lax.axis_index("zl")
    core = lax.axis_index("core")
    flat = jnp.zeros((half, LANES), jnp.float32)
    for i in range(count - 2):
        at, below = i * size, (i + 2) * size
        flat = flat + got_ref[at : at + half, :] * got_ref[below + half : below + 2 * half, :]
    west = got_ref[pl.ds(2 * half, z_count, stride=2 * size), :]
    east = got_ref[pl.ds(2 * half + size, z_count, stride=2 * size), :]
    facing = jnp.where(iota((z_count, LANES), 1) < rows, pltpu.roll(west, LANES - rows, 1) * east, 0.0)
    between = total_of(flat) + total_of(facing)
    lane = iota((1, LANES), 1)
    sums = jnp.sum(west + east, axis=0, keepdims=True)
    sums = jnp.where(lane == 2 * rows + 4, sums - 2.0 * between, sums)
    pack = LANES // rows
    zr = z_count // pack
    wide = iota((zr, LANES), 1)
    lefts = jnp.zeros((zr, LANES), jnp.float32)
    rights = lefts
    for j in range(pack):
        a = got_ref[pl.ds(2 * half + 2 * size * j, zr, stride=2 * size * pack), :]
        d = got_ref[pl.ds(2 * half + size + 2 * size * j, zr, stride=2 * size * pack), :]
        a = jnp.where(wide < rows, a, 0.0)
        d = jnp.where((wide >= rows) & (wide < 2 * rows), d, 0.0)
        if j > 0:
            a = pltpu.roll(a, rows * j, 1)
        if j != 1:
            d = pltpu.roll(d, (rows * (j - 1)) % LANES, 1)
        lefts, rights = lefts + a, rights + d
    block_ref[:zr, :] = lefts
    block_ref[zr : 2 * zr, :] = rights
    block_ref[2 * zr : 2 * zr + 1, :] = sums
    message = block_ref[...]
    height = block_ref.shape[0]
    for i in range(out_ref.shape[0] // height):
        out_ref[i * height : (i + 1) * height, :] = message

    above = jnp.maximum(2 * z - 2 + core, 0) * size
    below = jnp.minimum(2 * z + 2 + core, count - 1) * size + half
    up = jnp.concatenate([got_ref[pl.ds(above + k, 1), :] for k in range(half)], axis=1)
    down = jnp.concatenate([got_ref[pl.ds(below + k, 1), :] for k in range(half)], axis=1)
    up = jnp.where(z > 0, up, 0.0)
    down = jnp.where(z < z_count - 1, down, 0.0) * coef_ref[1, rows - 1 : rows, :]
    partner = got_ref[pl.ds((2 * z + 1 - core) * size + 2 * half, 1), :]
    left, right = to_column(partner, rows, rows), to_column(partner, 0, rows)
    edges = edges_of((rows, columns))
    v = v_ref[...]
    v = v - jnp.where(edges[0], up, 0.0) - jnp.where(edges[1], down, 0.0)
    v = v - jnp.where(edges[2], jnp.where(core == 1, left, 0.0), 0.0)
    v = v - jnp.where(edges[3], jnp.where(core == 0, right, 0.0) * coef_ref[3], 0.0)
    v_out_ref[...] = v


def closing_kernel(got_ref, v_ref, z_ref, w_ref, q_ref, r_ref, coef_ref, x_ref, res_ref):
    rows, columns = v_ref.shape
    pack = LANES // rows
    zr = lax.axis_size("zh") * 2 // pack
    size = 2 * zr + 1
    count = got_ref.shape[0] // size
    z = lax.axis_index("zh") * 2 + lax.axis_index("zl")
    xy, core = lax.axis_index("xy"), lax.axis_index("core")
    sums = got_ref[2 * zr : 2 * zr + 1, :]
    flat = jnp.zeros((zr, LANES), jnp.float32)
    for i in range(1, count):
        at = i * size
        sums = sums + got_ref[at + 2 * zr : at + 2 * zr + 1, :]
        flat = flat + got_ref[at - size + zr : at - size + 2 * zr, :] * got_ref[at : at + zr, :]
    across = total_of(flat)
    lane = iota((1, LANES), 1)
    rz, zq, rw, qw, wv = (
        jnp.sum(jnp.where(lane == 2 * rows + k, sums, 0.0), axis=1, keepdims=True)
        for k in range(5)
    )
    wv = wv - 2.0 * across
    step = rz / zq
    rz_new = rz - step * ((rw + zq) - step * qw)
    grow = 1.0 + rz_new / rz
    curve = grow * grow * zq - 2.0 * grow * step * qw + step * step * wv
    step_next = rz_new / curve
    on_z = step + step_next * grow
    on_w = step_next * step

    left_of, right_of = jnp.maximum(xy - 1, 0), jnp.minimum(xy + 1, count - 1)
    row = z // pack
    position = lax.rem(z, pack) * rows
    left = to_column(got_ref[pl.ds(left_of * size + zr + row, 1), :], position, rows)
    right = to_column(got_ref[pl.ds(right_of * size + row, 1), :], position, rows)
    left = jnp.where((core == 0) & (xy > 0), left, 0.0)
    right = jnp.where((core == 1) & (xy < count - 1), right, 0.0)
    edges = edges_of((rows, columns))
    v = v_ref[...]
    v = v - jnp.where(edges[2], left, 0.0) - jnp.where(edges[3], right * coef_ref[3], 0.0)
    x_ref[...] = on_z * z_ref[...] - on_w * w_ref[...]
    res_ref[...] = r_ref[...] - on_z * q_ref[...] + on_w * v


def call(kernel, name, args, outs, scratch=(), by_hand=False):
    whole = pl.BlockSpec(memory_space=pltpu.VMEM)
    scratch = [pltpu.VMEM(x, jnp.float32) if isinstance(x, tuple) else x for x in scratch]
    return pl.pallas_call(
        kernel,
        out_shape=[jax.ShapeDtypeStruct(shape, jnp.float32) for shape in outs],
        in_specs=[pl.BlockSpec(memory_space=pl.ANY) if by_hand else whole] * len(args),
        out_specs=[whole] * len(outs),
        scratch_shapes=scratch,
        compiler_params=pltpu.CompilerParams(vmem_limit_bytes=VMEM_LIMIT),
        name=name,
    )(*args)


def exchanged(x, axes, rows):
    flat = x.reshape(x.shape[0] // rows, rows * LANES)
    return lax.all_to_all(flat, axes, 0, 0, tiled=True).reshape(x.shape)


def swap_in(x, axis):
    return lax.ppermute(x, axis, [(0, 1), (1, 0)])


def swap_over(x, axes):
    count = lax.axis_size(axes)
    pairs = [(i, i + 1) for i in range(1, count - 1, 2)]
    return lax.ppermute(x, axes, pairs + [(j, i) for i, j in pairs])


def local(right_side, class_map, class_perm, eigenvectors, coarse_inverse):
    rows, columns = right_side.shape
    nev = eigenvectors.shape[0]
    field = (rows, columns)
    group = 2 * lax.axis_size(COLS)
    z_count, chips = lax.axis_size(ROWS), lax.axis_size("xy")
    size = 2 * (columns // LANES) + 1
    size_next = 2 * (z_count * rows // LANES) + 1
    per_vector = (nev, LANES)

    perm, over, within, e_over, e_in, message, r, vectors, matrix = call(
        opening_kernel, "opening",
        (class_perm, right_side, class_map, eigenvectors, coarse_inverse),
        [field, (1, columns), (1, columns), (rows, LANES), (rows, LANES), (group, LANES),
         field, eigenvectors.shape, coarse_inverse.shape],
        [pltpu.SMEM(class_perm.shape, jnp.float32), pltpu.VMEM(field, jnp.int32), per_vector,
         pltpu.SemaphoreType.DMA((4 + PIECES,))],
        by_hand=True,
    )
    over, within = swap_over(over, ROWS), swap_in(within, "zl")
    e_over, e_in = swap_over(e_over, COLS), swap_in(e_in, "core")
    got = exchanged(message, GROUP, 1)
    z0, coef, z_over, z_in = call(
        first_kernel, "first", (got, over, within, perm, r, vectors, matrix),
        [field, (6,) + field, (1, columns), (1, columns)], [per_vector],
    )
    z_over, z_in = swap_over(z_over, ROWS), swap_in(z_in, "zl")
    q0, message = call(
        second_kernel, "second", (z_over, z_in, e_over, e_in, z0, coef, vectors),
        [field, (2 * group, LANES)], [per_vector],
    )
    got = exchanged(message, GROUP, 2)
    q0, w, v, message = call(
        third_kernel, "third", (got, q0, z0, r, coef, vectors, matrix),
        [field, field, field, (2 * z_count * size, LANES)],
        [per_vector, (size, LANES), (group, LANES)],
    )
    got = exchanged(message, STACK, size)
    v, message = call(
        fourth_kernel, "fourth", (got, v, coef),
        [field, (chips * size_next, LANES)], [(size_next, LANES)],
    )
    got = exchanged(message, PLANE, size_next)
    return tuple(call(closing_kernel, "closing", (got, v, z0, w, q0, r, coef), [field, field]))


def solution(mesh):
    n_gx, n_gy = mesh.devices.shape
    fine = Mesh(mesh.devices.reshape(n_gx // 2, 2, n_gy // 2, 2), FINE)
    in_specs = (P(ROWS, COLS), P(ROWS, COLS), P(), P(None, ROWS, COLS), P(FINE, None))
    out_specs = (P(ROWS, COLS), P(ROWS, COLS))
    return jax.shard_map(local, mesh=fine, in_specs=in_specs, out_specs=out_specs, check_vma=False)
```

time: 115 us -> 116 us (level)
  waiting for transfers between devices: 5.98 us -> 1.86 us
  starting transfers between devices: 35 us -> 36.9 us
  blocking collectives: 63.6 us -> 65.3 us
    all_to_all x1, waiting for transfers between devices: 3.96 us -> 0.01 us  [exchanged(): return lax.all_to_all(flat, axes, 0, 0, tiled=True).reshape(x.shape)]
    ppermute x3, starting transfers between devices: 10.4 us -> 12.8 us  [swap_in(): return lax.ppermute(x, axis, [(0, 1), (1, 0)])]
    all_to_all x3, blocking collectives: 63.6 us -> 65.3 us  [exchanged(): return lax.all_to_all(flat, axes, 0, 0, tiled=True).reshape(x.shape)]
    unnamed x16 -> x10, local copies, waits for them, and re-layouts: 4.64 us -> 4.62 us
  transfers between devices with their start and end apart: 7 -> 7, of which waited for: 3 -> 2; matrix products, arithmetic and copies ran while one was open for 0% -> 0% of each run, Pallas kernels for 0% -> 0%
where the time goes in v3:
time: 116 us; the launch traced here: 114 us
  blocking collectives  65.3 us (56%)
  starting transfers between devices  36.9 us (32%)
  local copies, waits for them, and re-layouts  4.62 us (4%)
  Pallas kernels  4.39 us (4%)
  waiting for transfers between devices  1.86 us (2%)
    all_to_all x3, blocking collectives, exchanged(): return lax.all_to_all(flat, axes, 0, 0, tiled=True).reshape(x.shape)  65.3 us
    all_to_all x1, starting transfers between devices, exchanged(): return lax.all_to_all(flat, axes, 0, 0, tiled=True).reshape(x.shape)  19.2 us
    ppermute x3, starting transfers between devices, swap_in(): return lax.ppermute(x, axis, [(0, 1), (1, 0)])  12.8 us
    ppermute x3, starting transfers between devices, swap_over(): return lax.ppermute(x, axes, pairs + [(j, i) for i, j in pairs])  4.87 us
    unnamed x10, local copies, waits for them, and re-layouts  4.62 us
    pallas_call x6, Pallas kernels, call(): pl.pallas_call(kernel, out_shape=[jax.ShapeDtypeStruct(shape, jnp.float32...  4.39 us
  transfers between devices with their start and end apart: 7, of which 2 were waited for; matrix products, arithmetic and copies ran while one was open for 0% of the time, Pallas kernels for 0%

profile of v3, /device:TPU:1, one launch (start us, length us, event | category | flops | bytes accessed | tf_op | source)
XLA Modules:
  0.0 113.8 jit_solution(17581369918339441578)
XLA Ops:
  0.6 1.3 %copy-done = f32[40,32,256]{2,1,0:T(8,128)S(1)} copy-done((f32[40,32,256]{2,1,0:T(8,128)S(1)}, f32[40,32,256]{2,1,0:T(8,128)}, u32[]{:S(2)}) %copy-start) | copy-done | bytes 1310744
  2.0 1.1 %copy-done.1 = f32[40,5120]{1,0:T(8,128)S(1)} copy-done((f32[40,5120]{1,0:T(8,128)S(1)}, f32[40,5120]{1,0:T(8,128)}, u32[]{:S(2)}) %copy-start.1) | copy-done | bytes 819224
  3.1 0.8 copy-done.2
  3.9 0.8 copy-done.3
  4.6 0.7 copy-done.4
  5.3 2.1 %opening.1 = (f32[32,256]{1,0:T(8,128)S(1)}, f32[1,256]{1,0:T(1,128)S(1)}, f32[1,256]{1,0:T(1,128)S(1)}, f32[32,128]{1,0:T(8,128)S(1)}, f32[32,128]{1,0:T(8,128)...) custom-call(f32[4]{0:T(128)S(1)} %copy-done.4, ...), custom_call_target="tpu_custom_call" | custom-call | tf_op jit(solution)/shard_map/opening/pallas_call | solution.py:420
  7.4 19.2 %all-to-all-start = ((f32[128,1,128]{2,1,0:T(1,128)}), f32[128,1,128]{2,1,0:T(1,128)S(1)}, u32[]{:S(2)}, u32[]{:S(2)}) async-start(f32[128,1,128]{2,1,0:T(1,128)} %bitcast.1), calls=%async_computation | async-start | bytes 131072 | tf_op jit(solution)/shard_map/all_to_all | solution.py:433
  26.6 3.5 %collective-permute-start.4 = (f32[32,128]{1,0:T(8,128)S(1)}, f32[32,128]{1,0:T(8,128)S(1)}, u32[]{:S(2)}, u32[]{:S(2)}) collective-permute-start(f32[32,128]{1,0:T(8,128)S(1)} %get-tuple-element.32), channel_id=1, source_target_pairs={{1,2},{3,4},{5,6},{7,8},{9,10},{11,12},{13,14},{15,16},{17,18},{19... | collective-permute-start | bytes 49160 | tf_op jit(solution)/shard_map/ppermute | solution.py:443
  30.2 1.9 %collective-permute-start.5 = (f32[32,128]{1,0:T(8,128)S(1)}, f32[32,128]{1,0:T(8,128)S(1)}, u32[]{:S(2)}, u32[]{:S(2)}) collective-permute-start(f32[32,128]{1,0:T(8,128)S(1)} %get-tuple-element.33), channel_id=1, source_target_pairs={{0,1},{1,0},{2,3},{3,2},{4,5},{5,4},{6,7},{7,6},{8,9},{9,8},{10,11... | collective-permute-start | bytes 49160 | tf_op jit(solution)/shard_map/ppermute | solution.py:437
  32.1 0.7 collective-permute-start
  32.8 4.8 %collective-permute-start.1 = (f32[1,256]{1,0:T(1,128)S(1)}, f32[1,256]{1,0:T(1,128)S(1)}, u32[]{:S(2)}, u32[]{:S(2)}) collective-permute-start(f32[1,256]{1,0:T(1,128)S(1)} %get-tuple-element.25), channel_id=1, source_target_pairs={{0,64},{64,0},{1,65},{65,1},{2,66},{66,2},{3,67},{67,3},{4,68},{68... | collective-permute-start | bytes 3080 | tf_op jit(solution)/shard_map/ppermute | solution.py:437
  37.6 0.9 collective-permute-done.1.in_ref
  38.5 0.0 all-to-all-done
  38.5 0.4 first.1
  38.9 0.7 collective-permute-start.2
  39.6 6.1 %collective-permute-start.3 = (f32[1,256]{1,0:T(1,128)S(1)}, f32[1,256]{1,0:T(1,128)S(1)}, u32[]{:S(2)}, u32[]{:S(2)}) collective-permute-start(f32[1,256]{1,0:T(1,128)S(1)} %get-tuple-element.31), channel_id=1, source_target_pairs={{0,64},{64,0},{1,65},{65,1},{2,66},{66,2},{3,67},{67,3},{4,68},{68... | collective-permute-start | bytes 3080 | tf_op jit(solution)/shard_map/ppermute | solution.py:437
  45.7 0.9 collective-permute-done.3.z_in_ref
  46.7 0.3 second.1
  47.0 25.1 %all_to_all.38 = f32[128,1,256]{2,1,0:T(1,128)S(1)} all-to-all(f32[128,1,256]{2,1,0:T(1,128)S(1)} %bitcast.15), channel_id=1, replica_groups=mesh['zh'=8,'zl'=2,'xy'=32,'core'=2] {'zl','xy','core'}, dimensions={0} | all-to-all | bytes 262144 | tf_op jit(solution)/shard_map/all_to_all | solution.py:433
  72.1 0.6 third.1
  72.7 28.0 %all_to_all.39 = f32[32,1,640]{2,1,0:T(1,128)S(1)} all-to-all(f32[32,1,640]{2,1,0:T(1,128)S(1)} %bitcast.16), channel_id=1, replica_groups=mesh['zh'=8,'zl'=2,'xy'=32,'core'=2] {'zh','zl','core'}, dimensions={0} | all-to-all | bytes 163840 | tf_op jit(solution)/shard_map/all_to_all | solution.py:433
  100.7 0.2 fourth.1
  100.9 12.2 %all_to_all.40 = f32[32,1,1152]{2,1,0:T(1,128)S(1)} all-to-all(f32[32,1,1152]{2,1,0:T(1,128)S(1)} %bitcast.14), channel_id=1, replica_groups=mesh['zh'=8,'zl'=2,'xy'=32,'core'=2] {'xy'}, dimensions={0} | all-to-all | bytes 294912 | tf_op jit(solution)/shard_map/all_to_all | solution.py:433
  113.0 0.8 closing.1
  (9 shorter events, 0.0 us)
Async XLA Ops:
  0.6 1.3 %copy-start = (f32[40,32,256]{2,1,0:T(8,128)S(1)}, f32[40,32,256]{2,1,0:T(8,128)}, u32[]{:S(2)}) copy-start(f32[40,32,256]{2,1,0:T(8,128)} %e_hbm.1) | copy-start | bytes 3932164
  1.9 1.1 %copy-start.1 = (f32[40,5120]{1,0:T(8,128)S(1)}, f32[40,5120]{1,0:T(8,128)}, u32[]{:S(2)}) copy-start(f32[40,5120]{1,0:T(8,128)} %c_hbm.1) | copy-start | bytes 2457604
  3.1 0.8 copy-start.2
  3.9 0.8 copy-start.3
  4.6 0.7 copy-start.4
  7.4 31.1 %all-to-all-start = ((f32[128,1,128]{2,1,0:T(1,128)}), f32[128,1,128]{2,1,0:T(1,128)S(1)}, u32[]{:S(2)}, u32[]{:S(2)}) async-start(f32[128,1,128]{2,1,0:T(1,128)} %bitcast.1), calls=%async_computation | async-start | bytes 131072 | tf_op jit(solution)/shard_map/all_to_all | solution.py:433
  26.6 19.1 %collective-permute-start.4 = (f32[32,128]{1,0:T(8,128)S(1)}, f32[32,128]{1,0:T(8,128)S(1)}, u32[]{:S(2)}, u32[]{:S(2)}) collective-permute-start(f32[32,128]{1,0:T(8,128)S(1)} %get-tuple-element.32), channel_id=1, source_target_pairs={{1,2},{3,4},{5,6},{7,8},{9,10},{11,12},{13,14},{15,16},{17,18},{19... | collective-permute-start | bytes 49160 | tf_op jit(solution)/shard_map/ppermute | solution.py:443
  30.2 15.5 %collective-permute-start.5 = (f32[32,128]{1,0:T(8,128)S(1)}, f32[32,128]{1,0:T(8,128)S(1)}, u32[]{:S(2)}, u32[]{:S(2)}) collective-permute-start(f32[32,128]{1,0:T(8,128)S(1)} %get-tuple-element.33), channel_id=1, source_target_pairs={{0,1},{1,0},{2,3},{3,2},{4,5},{5,4},{6,7},{7,6},{8,9},{9,8},{10,11... | collective-permute-start | bytes 49160 | tf_op jit(solution)/shard_map/ppermute | solution.py:437
  32.1 5.5 %collective-permute-start = (f32[1,256]{1,0:T(1,128)S(1)}, f32[1,256]{1,0:T(1,128)S(1)}, u32[]{:S(2)}, u32[]{:S(2)}) collective-permute-start(f32[1,256]{1,0:T(1,128)S(1)} %get-tuple-element.24), channel_id=1, source_target_pairs={{64,128},{192,256},{320,384},{448,512},{576,640},{704,768},{832,89... | collective-permute-start | bytes 3080 | tf_op jit(solution)/shard_map/ppermute | solution.py:443
  32.8 5.7 %collective-permute-start.1 = (f32[1,256]{1,0:T(1,128)S(1)}, f32[1,256]{1,0:T(1,128)S(1)}, u32[]{:S(2)}, u32[]{:S(2)}) collective-permute-start(f32[1,256]{1,0:T(1,128)S(1)} %get-tuple-element.25), channel_id=1, source_target_pairs={{0,64},{64,0},{1,65},{65,1},{2,66},{66,2},{3,67},{67,3},{4,68},{68... | collective-permute-start | bytes 3080 | tf_op jit(solution)/shard_map/ppermute | solution.py:437
  38.9 6.8 %collective-permute-start.2 = (f32[1,256]{1,0:T(1,128)S(1)}, f32[1,256]{1,0:T(1,128)S(1)}, u32[]{:S(2)}, u32[]{:S(2)}) collective-permute-start(f32[1,256]{1,0:T(1,128)S(1)} %get-tuple-element.30), channel_id=1, source_target_pairs={{64,128},{192,256},{320,384},{448,512},{576,640},{704,768},{832,89... | collective-permute-start | bytes 3080 | tf_op jit(solution)/shard_map/ppermute | solution.py:443
  39.6 7.0 %collective-permute-start.3 = (f32[1,256]{1,0:T(1,128)S(1)}, f32[1,256]{1,0:T(1,128)S(1)}, u32[]{:S(2)}, u32[]{:S(2)}) collective-permute-start(f32[1,256]{1,0:T(1,128)S(1)} %get-tuple-element.31), channel_id=1, source_target_pairs={{0,64},{64,0},{1,65},{65,1},{2,66},{66,2},{3,67},{67,3},{4,68},{68... | collective-permute-start | bytes 3080 | tf_op jit(solution)/shard_map/ppermute | solution.py:437

commit v4 on v3

--- a/solution.py
+++ b/solution.py
@@ -108,16 +108,17 @@
     return jnp.sum(rows_ref[...], axis=1, keepdims=True)
 
 
-def coarse(c_ref, gathered_ref, nev):
+def coarse(c_ref, gathered_ref, nev, stride):
     dofs = c_ref.shape[1]
     lane = iota((1, LANES), 1)
     total = None
     for r in range(dofs // LANES):
         low = r * LANES // nev
         high = (r * LANES + LANES - 1) // nev
-        flat = gathered_ref[low : low + 1, :]
+        flat = gathered_ref[low * stride : low * stride + 1, :]
         for d in range(low + 1, high + 1):
-            flat = jnp.where(lane >= d * nev - r * LANES, gathered_ref[d : d + 1, :], flat)
+            row = gathered_ref[d * stride : d * stride + 1, :]
+            flat = jnp.where(lane >= d * nev - r * LANES, row, flat)
         term = c_ref[:, r * LANES : (r + 1) * LANES] * flat
         total = term if total is None else total + term
     return jnp.sum(total, axis=1, keepdims=True)
@@ -155,8 +156,8 @@
 
 def opening_kernel(
     kinds_hbm, r_hbm, map_hbm, e_hbm, c_hbm,
-    perm_ref, over_ref, in_ref, e_over_ref, e_in_ref, out_ref, r_ref, e_ref, c_ref,
-    kinds_ref, map_ref, rows_ref, sems,
+    perm_ref, over_ref, out_ref, r_ref, e_ref, c_ref,
+    kinds_ref, map_ref, rows_ref, block_ref, sems,
 ):
     nev, rows, columns = e_ref.shape
     steps = sems.shape[0] - 4
@@ -184,27 +185,26 @@
         perm = jnp.where(classes == k, kinds_ref[k], perm)
     perm_ref[...] = perm
     upper = lax.axis_index("zl") == 0
-    first = lax.axis_index("core") == 0
     over_ref[...] = jnp.where(upper, perm[:1], perm[-1:])
-    in_ref[...] = jnp.where(upper, perm[-1:], perm[:1])
+    within = jnp.where(upper, perm[-1:], perm[:1])
     r = r_ref[...]
-    lane = iota((rows, LANES), 1)
-    lefts = jnp.zeros((rows, LANES), jnp.float32)
-    rights = lefts
     for k in range(steps):
         parts[k].wait()
         for e in range(k * chunk, (k + 1) * chunk):
-            own = e_ref[e]
-            project_one(own, r, rows_ref, e)
-            lefts = jnp.where(lane == e, own[:, :1], lefts)
-            rights = jnp.where(lane == e, own[:, columns - 1 :], rights)
-    e_over_ref[...] = jnp.where(first, lefts, rights)
-    e_in_ref[...] = jnp.where(first, rights, lefts)
+            project_one(e_ref[e], r, rows_ref, e)
     c = jnp.sum(rows_ref[...], axis=1, keepdims=True)
     start = lane_start(group_place(), nev)
-    message = to_lanes(c, start) + to_lanes(perm[:, :1], start + nev)
-    message = message + to_lanes(perm[:, -1:], start + nev + rows)
-    out_ref[...] = jnp.broadcast_to(message, out_ref.shape)
+    size = block_ref.shape[0]
+    block_ref[:1, :] = (
+        to_lanes(c, start)
+        + to_lanes(perm[:, :1], start + nev)
+        + to_lanes(perm[:, -1:], start + nev + rows)
+    )
+    for k in range(size - 1):
+        block_ref[k + 1 : k + 2, :] = within[:, k * LANES : (k + 1) * LANES]
+    message = block_ref[...]
+    for i in range(out_ref.shape[0] // size):
+        out_ref[i * size : (i + 1) * size, :] = message
     matrix.wait()
 
 
@@ -220,13 +220,20 @@
 
 
 def first_kernel(
-    got_ref, over_ref, in_ref, perm_ref, r_ref, e_ref, c_ref,
-    z_ref, coef_ref, z_over_ref, z_in_ref, rows_ref,
+    got_ref, over_ref, perm_ref, r_ref, e_ref, c_ref,
+    z_ref, coef_ref, z_over_ref, z_in_ref, y_over_ref, y_in_ref, rows_ref,
 ):
     nev, rows, columns = e_ref.shape
+    size = columns // LANES + 1
     upper = lax.axis_index("zl") == 0
-    left, right = beside_columns(got_ref, 1, nev, rows)
-    over, within = over_ref[...], in_ref[...]
+    first = lax.axis_index("core") == 0
+    left, right = beside_columns(got_ref, size, nev, rows)
+    across = lax.axis_size("xy") * 2
+    partner = (group_place() + jnp.where(upper, across, -across)) * size
+    over = over_ref[...]
+    within = jnp.concatenate(
+        [got_ref[pl.ds(partner + 1 + k, 1), :] for k in range(size - 1)], axis=1
+    )
     halo = (jnp.where(upper, over, within), jnp.where(upper, within, over), left, right)
     perm = perm_ref[...]
     edges = edges_of(perm.shape)
@@ -238,62 +245,49 @@
     for k in range(6):
         coef_ref[k] = coef[k]
     stencil = Stencil(coef)
-    y = coarse(c_ref, got_ref, nev)
+    y = coarse(c_ref, got_ref, nev, size)
     z = stencil.smooth(r_ref[...]) + prolong(e_ref, y, rows_ref)
     z_ref[...] = z
     top, low = (faces[0] * z)[:1], (faces[1] * z)[-1:]
     z_over_ref[...] = jnp.where(upper, top, low)
     z_in_ref[...] = jnp.where(upper, low, top)
+    lefts, rights = to_lanes((faces[2] * z)[:, :1], 0), to_lanes((faces[3] * z)[:, -1:], 0)
+    y_over_ref[...] = jnp.where(first, lefts, rights)
+    y_in_ref[...] = jnp.where(first, rights, lefts)
 
 
 def second_kernel(
-    z_over_ref, z_in_ref, e_over_ref, e_in_ref, z_ref, coef_ref, e_ref, q_ref, out_ref, rows_ref
+    z_in_ref, y_over_ref, y_in_ref, z_over_ref, z_ref, coef_ref, e_ref, q_ref, out_ref, rows_ref
 ):
     nev, rows, _ = e_ref.shape
     upper = lax.axis_index("zl") == 0
     first = lax.axis_index("core") == 0
     stencil = Stencil(coef_ref)
     over, within = z_over_ref[...], z_in_ref[...]
-    z = z_ref[...]
-    q = stencil.apply(z)
-    q = q - jnp.where(stencil.edges[0], jnp.where(upper, over, within), 0.0)
-    q = q - jnp.where(stencil.edges[1], jnp.where(upper, within, over), 0.0)
+    y_over, y_in = to_column(y_over_ref[...], 0, rows), to_column(y_in_ref[...], 0, rows)
+    halo = (
+        jnp.where(upper, over, within),
+        jnp.where(upper, within, over),
+        jnp.where(first, y_over, y_in),
+        jnp.where(first, y_in, y_over),
+    )
+    q = stencil.apply(z_ref[...])
+    for edge, outside in zip(stencil.edges, halo):
+        q = q - jnp.where(edge, outside, 0.0)
     q_ref[...] = q
-    left, right = (stencil.faces[2] * z)[:, :1], (stencil.faces[3] * z)[:, -1:]
-    start = lane_start(group_place(), nev)
-    own = to_lanes(project(e_ref, q, rows_ref), start)
-    own = own + to_lanes(left, start + nev) + to_lanes(right, start + nev + rows)
-    e_over, e_in = e_over_ref[...], e_in_ref[...]
-    to_left = jnp.sum(jnp.where(first, e_over, e_in) * left, axis=0, keepdims=True)
-    to_right = jnp.sum(jnp.where(first, e_in, e_over) * right, axis=0, keepdims=True)
-    added = pltpu.roll(to_left, lax.rem(start - nev + LANES, LANES), 1)
-    added = added + pltpu.roll(to_right, lax.rem(start + nev, LANES), 1)
-    sub = iota((8, LANES), 0)
-    pair = jnp.where(lax.rem(sub, 2) == 0, own, -added)
-    for k in range(out_ref.shape[0] // 8):
-        out_ref[8 * k : 8 * k + 8, :] = pair
+    message = to_lanes(project(e_ref, q, rows_ref), lane_start(group_place(), nev))
+    out_ref[...] = jnp.broadcast_to(message, out_ref.shape)
 
 
 def third_kernel(
     got_ref, q_ref, z_ref, r_ref, coef_ref, e_ref, c_ref,
-    q_out_ref, w_ref, v_ref, out_ref, rows_ref, block_ref, group_ref,
+    w_ref, v_ref, out_ref, rows_ref, block_ref,
 ):
     nev, rows, columns = e_ref.shape
     half = columns // LANES
-    count = group_ref.shape[0]
     stencil = Stencil(coef_ref)
-    z, r = z_ref[...], r_ref[...]
-    left, right = beside_columns(got_ref, 2, nev, rows)
-    q = q_ref[...] - jnp.where(stencil.edges[2], left, 0.0)
-    q = q - jnp.where(stencil.edges[3], right, 0.0)
-    q_out_ref[...] = q
-    added = got_ref[pl.ds(1, count, stride=2), :]
-    group_ref[...] = (
-        got_ref[pl.ds(0, count, stride=2), :]
-        + pltpu.roll(added, 1, 0)
-        + pltpu.roll(added, count - 1, 0)
-    )
-    y = coarse(c_ref, group_ref, nev)
+    q, z, r = q_ref[...], z_ref[...], r_ref[...]
+    y = coarse(c_ref, got_ref, nev, 1)
     w = stencil.smooth(q) + prolong(e_ref, y, rows_ref)
     v = stencil.apply(w)
     w_ref[...] = w
@@ -453,32 +447,33 @@
     size_next = 2 * (z_count * rows // LANES) + 1
     per_vector = (nev, LANES)
 
-    perm, over, within, e_over, e_in, message, r, vectors, matrix = call(
+    size_first = columns // LANES + 1
+    given = (class_perm, right_side, class_map, eigenvectors, coarse_inverse)
+    perm, over, message, r, vectors, matrix = call(
         opening_kernel, "opening",
-        (class_perm, right_side, class_map, eigenvectors, coarse_inverse),
-        [field, (1, columns), (1, columns), (rows, LANES), (rows, LANES), (group, LANES),
+        tuple(pltpu.with_memory_space_constraint(x, pltpu.HBM) for x in given),
+        [field, (1, columns), (size_first * group, LANES),
          field, eigenvectors.shape, coarse_inverse.shape],
         [pltpu.SMEM(class_perm.shape, jnp.float32), pltpu.VMEM(field, jnp.int32), per_vector,
-         pltpu.SemaphoreType.DMA((4 + PIECES,))],
+         (size_first, LANES), pltpu.SemaphoreType.DMA((4 + PIECES,))],
         by_hand=True,
     )
-    over, within = swap_over(over, ROWS), swap_in(within, "zl")
-    e_over, e_in = swap_over(e_over, COLS), swap_in(e_in, "core")
+    over = swap_over(over, ROWS)
+    got = exchanged(message, GROUP, size_first)
+    z0, coef, z_over, z_in, y_over, y_in = call(
+        first_kernel, "first", (got, over, perm, r, vectors, matrix),
+        [field, (6,) + field, (1, columns), (1, columns), (1, LANES), (1, LANES)], [per_vector],
+    )
+    y_over, z_in = swap_over(y_over, COLS), swap_in(z_in, "zl")
+    y_in, z_over = swap_in(y_in, "core"), swap_over(z_over, ROWS)
+    q0, message = call(
+        second_kernel, "second", (z_in, y_over, y_in, z_over, z0, coef, vectors),
+        [field, (group, LANES)], [per_vector],
+    )
     got = exchanged(message, GROUP, 1)
-    z0, coef, z_over, z_in = call(
-        first_kernel, "first", (got, over, within, perm, r, vectors, matrix),
-        [field, (6,) + field, (1, columns), (1, columns)], [per_vector],
-    )
-    z_over, z_in = swap_over(z_over, ROWS), swap_in(z_in, "zl")
-    q0, message = call(
-        second_kernel, "second", (z_over, z_in, e_over, e_in, z0, coef, vectors),
-        [field, (2 * group, LANES)], [per_vector],
-    )
-    got = exchanged(message, GROUP, 2)
-    q0, w, v, message = call(
+    w, v, message = call(
         third_kernel, "third", (got, q0, z0, r, coef, vectors, matrix),
-        [field, field, field, (2 * z_count * size, LANES)],
-        [per_vector, (size, LANES), (group, LANES)],
+        [field, field, (2 * z_count * size, LANES)], [per_vector, (size, LANES)],
     )
     got = exchanged(message, STACK, size)
     v, message = call(

time: 116 us -> 108 us (0.931)
  waiting for transfers between devices: 1.86 us -> 12.6 us
  starting transfers between devices: 36.9 us -> 28.7 us
  blocking collectives: 65.3 us -> 59.4 us
  local copies, waits for them, and re-layouts: 4.62 us -> 0 us
    all_to_all x1, waiting for transfers between devices: 0.01 us -> 11.5 us  [exchanged(): return lax.all_to_all(flat, axes, 0, 0, tiled=True).reshape(x.shape)]
    ppermute x3 -> x2, starting transfers between devices: 12.8 us -> 4.52 us  [swap_in(): return lax.ppermute(x, axis, [(0, 1), (1, 0)])]
    all_to_all x3, blocking collectives: 65.3 us -> 59.4 us  [exchanged(): return lax.all_to_all(flat, axes, 0, 0, tiled=True).reshape(x.shape)]
    unnamed x10 -> x0, local copies, waits for them, and re-layouts: 4.62 us -> none
  transfers between devices with their start and end apart: 7 -> 6, of which waited for: 2 -> 2; matrix products, arithmetic and copies ran while one was open for 0% -> 0% of each run, Pallas kernels for 0% -> 0%
where the time goes in v4:
time: 108 us; the launch traced here: 106 us
  blocking collectives  59.4 us (55%)
  starting transfers between devices  28.7 us (27%)
  waiting for transfers between devices  12.6 us (12%)
  Pallas kernels  4.67 us (4%)
    all_to_all x3, blocking collectives, exchanged(): return lax.all_to_all(flat, axes, 0, 0, tiled=True).reshape(x.shape)  59.4 us
    all_to_all x1, starting transfers between devices, exchanged(): return lax.all_to_all(flat, axes, 0, 0, tiled=True).reshape(x.shape)  19.3 us
    all_to_all x1, waiting for transfers between devices, exchanged(): return lax.all_to_all(flat, axes, 0, 0, tiled=True).reshape(x.shape)  11.5 us
    ppermute x3, starting transfers between devices, swap_over(): return lax.ppermute(x, axes, pairs + [(j, i) for i, j in pairs])  4.87 us
    pallas_call x6, Pallas kernels, call(): pl.pallas_call(kernel, out_shape=[jax.ShapeDtypeStruct(shape, jnp.float32...  4.67 us
    ppermute x2, starting transfers between devices, swap_in(): return lax.ppermute(x, axis, [(0, 1), (1, 0)])  4.52 us
  transfers between devices with their start and end apart: 6, of which 2 were waited for; matrix products, arithmetic and copies ran while one was open for 0% of the time, Pallas kernels for 0%

profile of v4, /device:TPU:1, one launch (start us, length us, event | category | flops | bytes accessed | tf_op | source)
XLA Modules:
  0.0 106.1 jit_solution(11751472508647020985)
XLA Ops:
  0.6 2.3 %opening.1 = (f32[32,256]{1,0:T(8,128)S(1)}, f32[1,256]{1,0:T(1,128)S(1)}, f32[384,128]{1,0:T(8,128)}, f32[32,256]{1,0:T(8,128)S(1)}, f32[40,32,256]{2,1,0:T(8,128)S(1)}, /*index=5*/f32[40,5120]{1,0:T(8,128)S(1)}) custom-call(f32[4]{0:T(128)} %kinds_hbm.1, f32[32,256]{1,0:T(8,128)} %r_hbm.1, s32[32,256]{1,0:T(8,128)} %map_hbm.1, f32[40,32,256]{2,1,0:T(8,128)} %e_hbm.1, ...), custom_call_target="tpu_custom_call" | custom-call | tf_op jit(solution)/shard_map/opening/pallas_call | solution.py:414
  3.0 19.3 %all-to-all-start = ((f32[128,1,384]{2,1,0:T(1,128)}), f32[128,1,384]{2,1,0:T(1,128)S(1)}, u32[]{:S(2)}, u32[]{:S(2)}) async-start(f32[128,1,384]{2,1,0:T(1,128)} %bitcast), calls=%async_computation | async-start | bytes 393216 | tf_op jit(solution)/shard_map/all_to_all | solution.py:427
  22.3 0.7 collective-permute-start
  23.0 0.0 collective-permute-done.over_ref
  23.0 11.5 %all-to-all-done = f32[128,1,384]{2,1,0:T(1,128)S(1)} async-done(((f32[128,1,384]{2,1,0:T(1,128)}), f32[128,1,384]{2,1,0:T(1,128)S(1)}, u32[]{:S(2)}, u32[]{:S(2)}) %all-to-all-start) | async-done | bytes 196640 | tf_op jit(solution)/shard_map/all_to_all | solution.py:427
  34.5 0.5 first.1
  35.0 2.6 %collective-permute-start.1 = (f32[1,256]{1,0:T(1,128)S(1)}, f32[1,256]{1,0:T(1,128)S(1)}, u32[]{:S(2)}, u32[]{:S(2)}) collective-permute-start(f32[1,256]{1,0:T(1,128)S(1)} %get-tuple-element.27), channel_id=1, source_target_pairs={{0,64},{64,0},{1,65},{65,1},{2,66},{66,2},{3,67},{67,3},{4,68},{68... | collective-permute-start | bytes 3080 | tf_op jit(solution)/shard_map/ppermute | solution.py:431
  37.7 0.7 collective-permute-start.4
  38.3 3.5 %collective-permute-start.2 = (f32[1,128]{1,0:T(1,128)S(1)}, f32[1,128]{1,0:T(1,128)S(1)}, u32[]{:S(2)}, u32[]{:S(2)}) collective-permute-start(f32[1,128]{1,0:T(1,128)S(1)} %get-tuple-element.28), channel_id=1, source_target_pairs={{1,2},{3,4},{5,6},{7,8},{9,10},{11,12},{13,14},{15,16},{17,18},{19... | collective-permute-start | bytes 1544 | tf_op jit(solution)/shard_map/ppermute | solution.py:437
  41.9 1.9 %collective-permute-start.3 = (f32[1,128]{1,0:T(1,128)S(1)}, f32[1,128]{1,0:T(1,128)S(1)}, u32[]{:S(2)}, u32[]{:S(2)}) collective-permute-start(f32[1,128]{1,0:T(1,128)S(1)} %get-tuple-element.29), channel_id=1, source_target_pairs={{0,1},{1,0},{2,3},{3,2},{4,5},{5,4},{6,7},{7,6},{8,9},{9,8},{10,11... | collective-permute-start | bytes 1544 | tf_op jit(solution)/shard_map/ppermute | solution.py:431
  43.8 0.0 collective-permute-done.2.y_over_ref
  43.8 1.1 %collective-permute-done.3.y_in_ref = f32[1,128]{1,0:T(1,128)S(1)} collective-permute-done((f32[1,128]{1,0:T(1,128)S(1)}, f32[1,128]{1,0:T(1,128)S(1)}, u32[]{:S(2)}, u32[]{:S(2)}) %collective-permute-start.3) | collective-permute-done | bytes 544 | tf_op jit(solution)/shard_map/ppermute | solution.py:431
  44.9 0.0 collective-permute-done.1.z_in_ref
  44.9 0.0 collective-permute-done.4.z_over_ref
  44.9 0.4 second.1
  45.3 18.2 %all_to_all.38 = f32[128,1,128]{2,1,0:T(1,128)S(1)} all-to-all(f32[128,1,128]{2,1,0:T(1,128)S(1)} %bitcast.16), channel_id=1, replica_groups=mesh['zh'=8,'zl'=2,'xy'=32,'core'=2] {'zl','xy','core'}, dimensions={0} | all-to-all | bytes 131072 | tf_op jit(solution)/shard_map/all_to_all | solution.py:427
  63.4 0.5 third.1
  63.9 29.1 %all_to_all.39 = f32[32,1,640]{2,1,0:T(1,128)S(1)} all-to-all(f32[32,1,640]{2,1,0:T(1,128)S(1)} %bitcast.15), channel_id=1, replica_groups=mesh['zh'=8,'zl'=2,'xy'=32,'core'=2] {'zh','zl','core'}, dimensions={0} | all-to-all | bytes 163840 | tf_op jit(solution)/shard_map/all_to_all | solution.py:427
  93.0 0.2 fourth.1
  93.2 12.2 %all_to_all.40 = f32[32,1,1152]{2,1,0:T(1,128)S(1)} all-to-all(f32[32,1,1152]{2,1,0:T(1,128)S(1)} %bitcast.14), channel_id=1, replica_groups=mesh['zh'=8,'zl'=2,'xy'=32,'core'=2] {'xy'}, dimensions={0} | all-to-all | bytes 294912 | tf_op jit(solution)/shard_map/all_to_all | solution.py:427
  105.3 0.8 closing.1
Async XLA Ops:
  3.0 31.5 %all-to-all-start = ((f32[128,1,384]{2,1,0:T(1,128)}), f32[128,1,384]{2,1,0:T(1,128)S(1)}, u32[]{:S(2)}, u32[]{:S(2)}) async-start(f32[128,1,384]{2,1,0:T(1,128)} %bitcast), calls=%async_computation | async-start | bytes 393216 | tf_op jit(solution)/shard_map/all_to_all | solution.py:427
  22.3 0.7 collective-permute-start
  35.0 9.9 %collective-permute-start.1 = (f32[1,256]{1,0:T(1,128)S(1)}, f32[1,256]{1,0:T(1,128)S(1)}, u32[]{:S(2)}, u32[]{:S(2)}) collective-permute-start(f32[1,256]{1,0:T(1,128)S(1)} %get-tuple-element.27), channel_id=1, source_target_pairs={{0,64},{64,0},{1,65},{65,1},{2,66},{66,2},{3,67},{67,3},{4,68},{68... | collective-permute-start | bytes 3080 | tf_op jit(solution)/shard_map/ppermute | solution.py:431
  37.7 7.2 %collective-permute-start.4 = (f32[1,256]{1,0:T(1,128)S(1)}, f32[1,256]{1,0:T(1,128)S(1)}, u32[]{:S(2)}, u32[]{:S(2)}) collective-permute-start(f32[1,256]{1,0:T(1,128)S(1)} %get-tuple-element.30), channel_id=1, source_target_pairs={{64,128},{192,256},{320,384},{448,512},{576,640},{704,768},{832,89... | collective-permute-start | bytes 3080 | tf_op jit(solution)/shard_map/ppermute | solution.py:437
  38.3 5.5 %collective-permute-start.2 = (f32[1,128]{1,0:T(1,128)S(1)}, f32[1,128]{1,0:T(1,128)S(1)}, u32[]{:S(2)}, u32[]{:S(2)}) collective-permute-start(f32[1,128]{1,0:T(1,128)S(1)} %get-tuple-element.28), channel_id=1, source_target_pairs={{1,2},{3,4},{5,6},{7,8},{9,10},{11,12},{13,14},{15,16},{17,18},{19... | collective-permute-start | bytes 1544 | tf_op jit(solution)/shard_map/ppermute | solution.py:437
  41.9 3.0 %collective-permute-start.3 = (f32[1,128]{1,0:T(1,128)S(1)}, f32[1,128]{1,0:T(1,128)S(1)}, u32[]{:S(2)}, u32[]{:S(2)}) collective-permute-start(f32[1,128]{1,0:T(1,128)S(1)} %get-tuple-element.29), channel_id=1, source_target_pairs={{0,1},{1,0},{2,3},{3,2},{4,5},{5,4},{6,7},{7,6},{8,9},{9,8},{10,11... | collective-permute-start | bytes 1544 | tf_op jit(solution)/shard_map/ppermute | solution.py:431

commit v5 on v4

--- a/solution.py
+++ b/solution.py
@@ -140,6 +140,17 @@
     return jnp.sum(jnp.sum(v, axis=0, keepdims=True), axis=1, keepdims=True)
 
 
+def fill(out_ref, message):
+    size = message.shape[0]
+    count = out_ref.shape[0] // size
+    batch = min(8, count)
+    for i in range(batch):
+        out_ref[i * size : (i + 1) * size, :] = message
+    pattern = out_ref[: batch * size, :]
+    for k in range(1, count // batch):
+        out_ref[k * batch * size : (k + 1) * batch * size, :] = pattern
+
+
 def group_place():
     return (lax.axis_index("zl") * lax.axis_size("xy") + lax.axis_index("xy")) * 2 + lax.axis_index(
         "core"
@@ -156,7 +167,7 @@
 
 def opening_kernel(
     kinds_hbm, r_hbm, map_hbm, e_hbm, c_hbm,
-    perm_ref, over_ref, out_ref, r_ref, e_ref, c_ref,
+    perm_ref, over_ref, facing_ref, out_ref, r_ref, e_ref, c_ref,
     kinds_ref, map_ref, rows_ref, block_ref, sems,
 ):
     nev, rows, columns = e_ref.shape
@@ -188,10 +199,18 @@
     over_ref[...] = jnp.where(upper, perm[:1], perm[-1:])
     within = jnp.where(upper, perm[-1:], perm[:1])
     r = r_ref[...]
+    first = lax.axis_index("core") == 0
+    block = pl.multiple_of(jnp.where(first, 0, columns - LANES), LANES)
+    turn = jnp.where(first, 0, 1)
+    lane = iota((rows, LANES), 1)
+    facing = jnp.zeros((rows, LANES), jnp.float32)
     for k in range(steps):
         parts[k].wait()
         for e in range(k * chunk, (k + 1) * chunk):
             project_one(e_ref[e], r, rows_ref, e)
+            edge = pltpu.roll(e_ref[e, :, pl.ds(block, LANES)], e + turn, 1)
+            facing = jnp.where(lane == e, edge, facing)
+    facing_ref[...] = facing
     c = jnp.sum(rows_ref[...], axis=1, keepdims=True)
     start = lane_start(group_place(), nev)
     size = block_ref.shape[0]
@@ -202,9 +221,7 @@
     )
     for k in range(size - 1):
         block_ref[k + 1 : k + 2, :] = within[:, k * LANES : (k + 1) * LANES]
-    message = block_ref[...]
-    for i in range(out_ref.shape[0] // size):
-        out_ref[i * size : (i + 1) * size, :] = message
+    fill(out_ref, block_ref[...])
     matrix.wait()
 
 
@@ -221,7 +238,7 @@
 
 def first_kernel(
     got_ref, over_ref, perm_ref, r_ref, e_ref, c_ref,
-    z_ref, coef_ref, z_over_ref, z_in_ref, y_over_ref, y_in_ref, rows_ref,
+    z_ref, coef_ref, z_over_ref, z_in_ref, y_in_ref, rows_ref,
 ):
     nev, rows, columns = e_ref.shape
     size = columns // LANES + 1
@@ -252,42 +269,66 @@
     z_over_ref[...] = jnp.where(upper, top, low)
     z_in_ref[...] = jnp.where(upper, low, top)
     lefts, rights = to_lanes((faces[2] * z)[:, :1], 0), to_lanes((faces[3] * z)[:, -1:], 0)
-    y_over_ref[...] = jnp.where(first, lefts, rights)
     y_in_ref[...] = jnp.where(first, rights, lefts)
 
 
 def second_kernel(
-    z_in_ref, y_over_ref, y_in_ref, z_over_ref, z_ref, coef_ref, e_ref, q_ref, out_ref, rows_ref
+    z_in_ref, y_in_ref, z_over_ref, facing_ref, z_ref, coef_ref, e_ref, q_ref, out_ref, rows_ref
 ):
     nev, rows, _ = e_ref.shape
     upper = lax.axis_index("zl") == 0
     first = lax.axis_index("core") == 0
     stencil = Stencil(coef_ref)
     over, within = z_over_ref[...], z_in_ref[...]
-    y_over, y_in = to_column(y_over_ref[...], 0, rows), to_column(y_in_ref[...], 0, rows)
+    y_in = to_column(y_in_ref[...], 0, rows)
     halo = (
         jnp.where(upper, over, within),
         jnp.where(upper, within, over),
-        jnp.where(first, y_over, y_in),
-        jnp.where(first, y_in, y_over),
-    )
-    q = stencil.apply(z_ref[...])
+        jnp.where(first, 0.0, y_in),
+        jnp.where(first, y_in, 0.0),
+    )
+    z = z_ref[...]
+    q = stencil.apply(z)
     for edge, outside in zip(stencil.edges, halo):
         q = q - jnp.where(edge, outside, 0.0)
     q_ref[...] = q
-    message = to_lanes(project(e_ref, q, rows_ref), lane_start(group_place(), nev))
-    out_ref[...] = jnp.broadcast_to(message, out_ref.shape)
+    left, right = (stencil.faces[2] * z)[:, :1], (stencil.faces[3] * z)[:, -1:]
+    edge = jnp.where(first, left, right)
+    start = lane_start(group_place(), nev)
+    own = to_lanes(project(e_ref, q, rows_ref), start) + to_lanes(edge, start + nev)
+    added = jnp.sum(facing_ref[...] * edge, axis=0, keepdims=True)
+    step = jnp.where(first, LANES - nev, nev)
+    added = pltpu.roll(added, lax.rem(start + step, LANES), 1)
+    sub = iota((8, LANES), 0)
+    pair = jnp.where(lax.rem(sub, 2) == 0, own, -added)
+    for k in range(out_ref.shape[0] // 8):
+        out_ref[8 * k : 8 * k + 8, :] = pair
 
 
 def third_kernel(
     got_ref, q_ref, z_ref, r_ref, coef_ref, e_ref, c_ref,
-    w_ref, v_ref, out_ref, rows_ref, block_ref,
+    q_out_ref, w_ref, v_ref, out_ref, rows_ref, block_ref, group_ref,
 ):
     nev, rows, columns = e_ref.shape
     half = columns // LANES
     stencil = Stencil(coef_ref)
-    q, z, r = q_ref[...], z_ref[...], r_ref[...]
-    y = coarse(c_ref, got_ref, nev, 1)
+    z, r = z_ref[...], r_ref[...]
+    first = lax.axis_index("core") == 0
+    place, b, count = group_place(), column_place(), group_ref.shape[0]
+    near = jnp.where(first, jnp.maximum(place - 1, 0), jnp.minimum(place + 1, count - 1))
+    edge = to_column(got_ref[pl.ds(2 * near, 1), :], lane_start(near, nev) + nev, rows)
+    left = jnp.where(first & (b > 0), edge, 0.0)
+    right = jnp.where((~first) & (b < lax.axis_size("xy") * 2 - 1), edge, 0.0)
+    q = q_ref[...] - jnp.where(stencil.edges[2], left, 0.0)
+    q = q - jnp.where(stencil.edges[3], right, 0.0)
+    q_out_ref[...] = q
+    added = got_ref[pl.ds(1, count, stride=2), :]
+    group_ref[...] = (
+        got_ref[pl.ds(0, count, stride=2), :]
+        + pltpu.roll(added, 1, 0)
+        + pltpu.roll(added, count - 1, 0)
+    )
+    y = coarse(c_ref, group_ref, nev, 1)
     w = stencil.smooth(q) + prolong(e_ref, y, rows_ref)
     v = stencil.apply(w)
     w_ref[...] = w
@@ -302,9 +343,7 @@
         last = jnp.where(lane == 2 * rows + k, total_of(product), last)
     size = block_ref.shape[0]
     block_ref[size - 1 : size, :] = last
-    message = block_ref[...]
-    for i in range(out_ref.shape[0] // size):
-        out_ref[i * size : (i + 1) * size, :] = message
+    fill(out_ref, block_ref[...])
 
 
 def fourth_kernel(got_ref, v_ref, coef_ref, v_out_ref, out_ref, block_ref):
@@ -344,10 +383,7 @@
     block_ref[:zr, :] = lefts
     block_ref[zr : 2 * zr, :] = rights
     block_ref[2 * zr : 2 * zr + 1, :] = sums
-    message = block_ref[...]
-    height = block_ref.shape[0]
-    for i in range(out_ref.shape[0] // height):
-        out_ref[i * height : (i + 1) * height, :] = message
+    fill(out_ref, block_ref[...])
 
     above = jnp.maximum(2 * z - 2 + core, 0) * size
     below = jnp.minimum(2 * z + 2 + core, count - 1) * size + half
@@ -449,31 +485,32 @@
 
     size_first = columns // LANES + 1
     given = (class_perm, right_side, class_map, eigenvectors, coarse_inverse)
-    perm, over, message, r, vectors, matrix = call(
+    perm, over, facing, message, r, vectors, matrix = call(
         opening_kernel, "opening",
         tuple(pltpu.with_memory_space_constraint(x, pltpu.HBM) for x in given),
-        [field, (1, columns), (size_first * group, LANES),
+        [field, (1, columns), (rows, LANES), (size_first * group, LANES),
          field, eigenvectors.shape, coarse_inverse.shape],
         [pltpu.SMEM(class_perm.shape, jnp.float32), pltpu.VMEM(field, jnp.int32), per_vector,
          (size_first, LANES), pltpu.SemaphoreType.DMA((4 + PIECES,))],
         by_hand=True,
     )
-    over = swap_over(over, ROWS)
+    over, facing = swap_over(over, ROWS), swap_over(facing, COLS)
     got = exchanged(message, GROUP, size_first)
-    z0, coef, z_over, z_in, y_over, y_in = call(
+    z0, coef, z_over, z_in, y_in = call(
         first_kernel, "first", (got, over, perm, r, vectors, matrix),
-        [field, (6,) + field, (1, columns), (1, columns), (1, LANES), (1, LANES)], [per_vector],
-    )
-    y_over, z_in = swap_over(y_over, COLS), swap_in(z_in, "zl")
-    y_in, z_over = swap_in(y_in, "core"), swap_over(z_over, ROWS)
+        [field, (6,) + field, (1, columns), (1, columns), (1, LANES)], [per_vector],
+    )
+    z_in, y_in = swap_in(z_in, "zl"), swap_in(y_in, "core")
+    z_over = swap_over(z_over, ROWS)
     q0, message = call(
-        second_kernel, "second", (z_in, y_over, y_in, z_over, z0, coef, vectors),
-        [field, (group, LANES)], [per_vector],
-    )
-    got = exchanged(message, GROUP, 1)
-    w, v, message = call(
+        second_kernel, "second", (z_in, y_in, z_over, facing, z0, coef, vectors),
+        [field, (2 * group, LANES)], [per_vector],
+    )
+    got = exchanged(message, GROUP, 2)
+    q0, w, v, message = call(
         third_kernel, "third", (got, q0, z0, r, coef, vectors, matrix),
-        [field, field, (2 * z_count * size, LANES)], [per_vector, (size, LANES)],
+        [field, field, field, (2 * z_count * size, LANES)],
+        [per_vector, (size, LANES), (group, LANES)],
     )
     got = exchanged(message, STACK, size)
     v, message = call(

time: 108 us -> 107 us (level)
  waiting for transfers between devices: 12.6 us -> 8.85 us
  blocking collectives: 59.4 us -> 62.1 us
    all_to_all x1, waiting for transfers between devices: 11.5 us -> 8.05 us  [exchanged(): return lax.all_to_all(flat, axes, 0, 0, tiled=True).reshape(x.shape)]
    all_to_all x3, blocking collectives: 59.4 us -> 62.1 us  [exchanged(): return lax.all_to_all(flat, axes, 0, 0, tiled=True).reshape(x.shape)]
  transfers between devices with their start and end apart: 6 -> 6, of which waited for: 2 -> 2; matrix products, arithmetic and copies ran while one was open for 0% -> 0% of each run, Pallas kernels for 0% -> 1%
where the time goes in v5:
time: 107 us; the launch traced here: 106 us
  blocking collectives  62.1 us (58%)
  starting transfers between devices  29.3 us (27%)
  waiting for transfers between devices  8.85 us (8%)
  Pallas kernels  4.81 us (4%)
    all_to_all x3, blocking collectives, exchanged(): return lax.all_to_all(flat, axes, 0, 0, tiled=True).reshape(x.shape)  62.1 us
    all_to_all x1, starting transfers between devices, exchanged(): return lax.all_to_all(flat, axes, 0, 0, tiled=True).reshape(x.shape)  19.3 us
    all_to_all x1, waiting for transfers between devices, exchanged(): return lax.all_to_all(flat, axes, 0, 0, tiled=True).reshape(x.shape)  8.05 us
    ppermute x2, starting transfers between devices, swap_in(): return lax.ppermute(x, axis, [(0, 1), (1, 0)])  5.11 us
    ppermute x3, starting transfers between devices, swap_over(): return lax.ppermute(x, axes, pairs + [(j, i) for i, j in pairs])  4.87 us
    pallas_call x6, Pallas kernels, call(): pl.pallas_call(kernel, out_shape=[jax.ShapeDtypeStruct(shape, jnp.float32...  4.81 us
  transfers between devices with their start and end apart: 6, of which 2 were waited for; matrix products, arithmetic and copies ran while one was open for 0% of the time, Pallas kernels for 1%

profile of v5, /device:TPU:1, one launch (start us, length us, event | category | flops | bytes accessed | tf_op | source)
XLA Modules:
  0.0 105.8 jit_solution(3921033884340477130)
XLA Ops:
  0.6 2.4 %opening.1 = (f32[32,256]{1,0:T(8,128)S(1)}, f32[1,256]{1,0:T(1,128)S(1)}, f32[32,128]{1,0:T(8,128)S(1)}, f32[384,128]{1,0:T(8,128)}, f32[32,256]{1,0:T(8,128)S(...) custom-call(f32[4]{0:T(128)} %kinds_hbm.1, f32[32,256]{1,0:T(8,128)} %r_hbm.1, s32[32,256]{1,0:T(8,128)} %map_hbm.1, ...), custom_call_target="tpu_custom_call" | custom-call | tf_op jit(solution)/shard_map/opening/pallas_call | solution.py:450
  3.0 19.3 %all-to-all-start = ((f32[128,1,384]{2,1,0:T(1,128)}), f32[128,1,384]{2,1,0:T(1,128)S(1)}, u32[]{:S(2)}, u32[]{:S(2)}) async-start(f32[128,1,384]{2,1,0:T(1,128)} %bitcast), calls=%async_computation | async-start | bytes 393216 | tf_op jit(solution)/shard_map/all_to_all | solution.py:463
  22.3 3.5 %collective-permute-start.4 = (f32[32,128]{1,0:T(8,128)S(1)}, f32[32,128]{1,0:T(8,128)S(1)}, u32[]{:S(2)}, u32[]{:S(2)}) collective-permute-start(f32[32,128]{1,0:T(8,128)S(1)} %get-tuple-element.31), channel_id=1, source_target_pairs={{1,2},{3,4},{5,6},{7,8},{9,10},{11,12},{13,14},{15,16},{17,18},{19... | collective-permute-start | bytes 49160 | tf_op jit(solution)/shard_map/ppermute | solution.py:473
  25.9 0.7 collective-permute-start
  26.5 0.0 collective-permute-done.over_ref
  26.6 8.1 %all-to-all-done = f32[128,1,384]{2,1,0:T(1,128)S(1)} async-done(((f32[128,1,384]{2,1,0:T(1,128)}), f32[128,1,384]{2,1,0:T(1,128)S(1)}, u32[]{:S(2)}, u32[]{:S(2)}) %all-to-all-start) | async-done | bytes 196640 | tf_op jit(solution)/shard_map/all_to_all | solution.py:463
  34.6 0.5 first.1
  35.1 2.5 %collective-permute-start.1 = (f32[1,256]{1,0:T(1,128)S(1)}, f32[1,256]{1,0:T(1,128)S(1)}, u32[]{:S(2)}, u32[]{:S(2)}) collective-permute-start(f32[1,256]{1,0:T(1,128)S(1)} %get-tuple-element.28), channel_id=1, source_target_pairs={{0,64},{64,0},{1,65},{65,1},{2,66},{66,2},{3,67},{67,3},{4,68},{68... | collective-permute-start | bytes 3080 | tf_op jit(solution)/shard_map/ppermute | solution.py:467
  37.7 0.7 collective-permute-start.3
  38.3 2.6 %collective-permute-start.2 = (f32[1,128]{1,0:T(1,128)S(1)}, f32[1,128]{1,0:T(1,128)S(1)}, u32[]{:S(2)}, u32[]{:S(2)}) collective-permute-start(f32[1,128]{1,0:T(1,128)S(1)} %get-tuple-element.29), channel_id=1, source_target_pairs={{0,1},{1,0},{2,3},{3,2},{4,5},{5,4},{6,7},{7,6},{8,9},{9,8},{10,11... | collective-permute-start | bytes 1544 | tf_op jit(solution)/shard_map/ppermute | solution.py:467
  40.9 0.0 collective-permute-done.4.facing_ref
  40.9 0.8 collective-permute-done.2.y_in_ref
  41.7 0.0 collective-permute-done.1.z_in_ref
  41.7 0.0 collective-permute-done.3.z_over_ref
  41.7 0.4 second.1
  42.1 20.7 %all_to_all.36 = f32[128,1,256]{2,1,0:T(1,128)S(1)} all-to-all(f32[128,1,256]{2,1,0:T(1,128)S(1)} %bitcast.13), channel_id=1, replica_groups=mesh['zh'=8,'zl'=2,'xy'=32,'core'=2] {'zl','xy','core'}, dimensions={0} | all-to-all | bytes 262144 | tf_op jit(solution)/shard_map/all_to_all | solution.py:463
  62.8 0.6 third.1
  63.4 29.3 %all_to_all.37 = f32[32,1,640]{2,1,0:T(1,128)S(1)} all-to-all(f32[32,1,640]{2,1,0:T(1,128)S(1)} %bitcast.14), channel_id=1, replica_groups=mesh['zh'=8,'zl'=2,'xy'=32,'core'=2] {'zh','zl','core'}, dimensions={0} | all-to-all | bytes 163840 | tf_op jit(solution)/shard_map/all_to_all | solution.py:463
  92.6 0.2 fourth.1
  92.8 12.2 %all_to_all.38 = f32[32,1,1152]{2,1,0:T(1,128)S(1)} all-to-all(f32[32,1,1152]{2,1,0:T(1,128)S(1)} %bitcast.12), channel_id=1, replica_groups=mesh['zh'=8,'zl'=2,'xy'=32,'core'=2] {'xy'}, dimensions={0} | all-to-all | bytes 294912 | tf_op jit(solution)/shard_map/all_to_all | solution.py:463
  105.0 0.8 closing.1
Async XLA Ops:
  3.0 31.6 %all-to-all-start = ((f32[128,1,384]{2,1,0:T(1,128)}), f32[128,1,384]{2,1,0:T(1,128)S(1)}, u32[]{:S(2)}, u32[]{:S(2)}) async-start(f32[128,1,384]{2,1,0:T(1,128)} %bitcast), calls=%async_computation | async-start | bytes 393216 | tf_op jit(solution)/shard_map/all_to_all | solution.py:463
  22.3 18.6 %collective-permute-start.4 = (f32[32,128]{1,0:T(8,128)S(1)}, f32[32,128]{1,0:T(8,128)S(1)}, u32[]{:S(2)}, u32[]{:S(2)}) collective-permute-start(f32[32,128]{1,0:T(8,128)S(1)} %get-tuple-element.31), channel_id=1, source_target_pairs={{1,2},{3,4},{5,6},{7,8},{9,10},{11,12},{13,14},{15,16},{17,18},{19... | collective-permute-start | bytes 49160 | tf_op jit(solution)/shard_map/ppermute | solution.py:473
  25.9 0.7 collective-permute-start
  35.1 6.6 %collective-permute-start.1 = (f32[1,256]{1,0:T(1,128)S(1)}, f32[1,256]{1,0:T(1,128)S(1)}, u32[]{:S(2)}, u32[]{:S(2)}) collective-permute-start(f32[1,256]{1,0:T(1,128)S(1)} %get-tuple-element.28), channel_id=1, source_target_pairs={{0,64},{64,0},{1,65},{65,1},{2,66},{66,2},{3,67},{67,3},{4,68},{68... | collective-permute-start | bytes 3080 | tf_op jit(solution)/shard_map/ppermute | solution.py:467
  37.7 4.1 %collective-permute-start.3 = (f32[1,256]{1,0:T(1,128)S(1)}, f32[1,256]{1,0:T(1,128)S(1)}, u32[]{:S(2)}, u32[]{:S(2)}) collective-permute-start(f32[1,256]{1,0:T(1,128)S(1)} %get-tuple-element.30), channel_id=1, source_target_pairs={{64,128},{192,256},{320,384},{448,512},{576,640},{704,768},{832,89... | collective-permute-start | bytes 3080 | tf_op jit(solution)/shard_map/ppermute | solution.py:473
  38.3 3.4 %collective-permute-start.2 = (f32[1,128]{1,0:T(1,128)S(1)}, f32[1,128]{1,0:T(1,128)S(1)}, u32[]{:S(2)}, u32[]{:S(2)}) collective-permute-start(f32[1,128]{1,0:T(1,128)S(1)} %get-tuple-element.29), channel_id=1, source_target_pairs={{0,1},{1,0},{2,3},{3,2},{4,5},{5,4},{6,7},{7,6},{8,9},{9,8},{10,11... | collective-permute-start | bytes 1544 | tf_op jit(solution)/shard_map/ppermute | solution.py:467

commit v6 on v5

--- a/solution.py
+++ b/solution.py
@@ -186,7 +186,7 @@
         for k in range(steps)
     ]
     matrix = pltpu.make_async_copy(c_hbm, c_ref, sems.at[3])
-    for copy in small + parts + [matrix]:
+    for copy in parts[:2] + small + parts[2:] + [matrix]:
         copy.start()
     for copy in small:
         copy.wait()
@@ -237,7 +237,7 @@
 
 
 def first_kernel(
-    got_ref, over_ref, perm_ref, r_ref, e_ref, c_ref,
+    got_ref, over_ref, _, perm_ref, r_ref, e_ref, c_ref,
     z_ref, coef_ref, z_over_ref, z_in_ref, y_in_ref, rows_ref,
 ):
     nev, rows, columns = e_ref.shape
@@ -497,7 +497,7 @@
     over, facing = swap_over(over, ROWS), swap_over(facing, COLS)
     got = exchanged(message, GROUP, size_first)
     z0, coef, z_over, z_in, y_in = call(
-        first_kernel, "first", (got, over, perm, r, vectors, matrix),
+        first_kernel, "first", (got, over, facing, perm, r, vectors, matrix),
         [field, (6,) + field, (1, columns), (1, columns), (1, LANES)], [per_vector],
     )
     z_in, y_in = swap_in(z_in, "zl"), swap_in(y_in, "core")

time: 107 us -> 107 us (level)
    all_to_all x1, waiting for transfers between devices: 8.05 us -> 5.99 us  [exchanged(): return lax.all_to_all(flat, axes, 0, 0, tiled=True).reshape(x.shape)]
    ppermute x3, waiting for transfers between devices: 0.01 us -> 2.07 us  [swap_over(): return lax.ppermute(x, axes, pairs + [(j, i) for i, j in pairs])]
  transfers between devices with their start and end apart: 6 -> 6, of which waited for: 2 -> 3; matrix products, arithmetic and copies ran while one was open for 0% -> 0% of each run, Pallas kernels for 1% -> 0%
where the time goes in v6:
time: 107 us; the launch traced here: 106 us
  blocking collectives  62.1 us (58%)
  starting transfers between devices  29.3 us (27%)
  waiting for transfers between devices  8.85 us (8%)
  Pallas kernels  4.78 us (4%)
    all_to_all x3, blocking collectives, exchanged(): return lax.all_to_all(flat, axes, 0, 0, tiled=True).reshape(x.shape)  62.1 us
    all_to_all x1, starting transfers between devices, exchanged(): return lax.all_to_all(flat, axes, 0, 0, tiled=True).reshape(x.shape)  19.3 us
    all_to_all x1, waiting for transfers between devices, exchanged(): return lax.all_to_all(flat, axes, 0, 0, tiled=True).reshape(x.shape)  5.99 us
    ppermute x2, starting transfers between devices, swap_in(): return lax.ppermute(x, axis, [(0, 1), (1, 0)])  5.11 us
    ppermute x3, starting transfers between devices, swap_over(): return lax.ppermute(x, axes, pairs + [(j, i) for i, j in pairs])  4.87 us
    pallas_call x6, Pallas kernels, call(): pl.pallas_call(kernel, out_shape=[jax.ShapeDtypeStruct(shape, jnp.float32...  4.78 us
  transfers between devices with their start and end apart: 6, of which 3 were waited for; matrix products, arithmetic and copies ran while one was open for 0% of the time, Pallas kernels for 0%

profile of v6, /device:TPU:1, one launch (start us, length us, event | category | flops | bytes accessed | tf_op | source)
XLA Modules:
  0.0 105.7 jit_solution(8282841778151802023)
XLA Ops:
  0.6 2.3 %opening.1 = (f32[32,256]{1,0:T(8,128)S(1)}, f32[1,256]{1,0:T(1,128)S(1)}, f32[32,128]{1,0:T(8,128)S(1)}, f32[384,128]{1,0:T(8,128)}, f32[32,256]{1,0:T(8,128)S(...) custom-call(f32[4]{0:T(128)} %kinds_hbm.1, f32[32,256]{1,0:T(8,128)} %r_hbm.1, s32[32,256]{1,0:T(8,128)} %map_hbm.1, ...), custom_call_target="tpu_custom_call" | custom-call | tf_op jit(solution)/shard_map/opening/pallas_call | solution.py:450
  3.0 19.3 %all-to-all-start = ((f32[128,1,384]{2,1,0:T(1,128)}), f32[128,1,384]{2,1,0:T(1,128)S(1)}, u32[]{:S(2)}, u32[]{:S(2)}) async-start(f32[128,1,384]{2,1,0:T(1,128)} %bitcast), calls=%async_computation | async-start | bytes 393216 | tf_op jit(solution)/shard_map/all_to_all | solution.py:463
  22.3 3.5 %collective-permute-start.1 = (f32[32,128]{1,0:T(8,128)S(1)}, f32[32,128]{1,0:T(8,128)S(1)}, u32[]{:S(2)}, u32[]{:S(2)}) collective-permute-start(f32[32,128]{1,0:T(8,128)S(1)} %get-tuple-element.24), channel_id=1, source_target_pairs={{1,2},{3,4},{5,6},{7,8},{9,10},{11,12},{13,14},{15,16},{17,18},{19... | collective-permute-start | bytes 49160 | tf_op jit(solution)/shard_map/ppermute | solution.py:473
  25.9 0.7 collective-permute-start
  26.5 0.0 collective-permute-done.over_ref
  26.5 2.1 %collective-permute-done.1._.facing_ref = f32[32,128]{1,0:T(8,128)S(1)} collective-permute-done((f32[32,128]{1,0:T(8,128)S(1)}, f32[32,128]{1,0:T(8,128)S(1)}, u32[]{:S(2)}, u32[]{:S(2)}) %collective-permute-start.1) | collective-permute-done | bytes 16416 | tf_op jit(solution)/shard_map/ppermute | solution.py:473
  28.6 6.0 %all-to-all-done = f32[128,1,384]{2,1,0:T(1,128)S(1)} async-done(((f32[128,1,384]{2,1,0:T(1,128)}), f32[128,1,384]{2,1,0:T(1,128)S(1)}, u32[]{:S(2)}, u32[]{:S(2)}) %all-to-all-start) | async-done | bytes 196640 | tf_op jit(solution)/shard_map/all_to_all | solution.py:463
  34.6 0.5 first.1
  35.1 2.5 %collective-permute-start.2 = (f32[1,256]{1,0:T(1,128)S(1)}, f32[1,256]{1,0:T(1,128)S(1)}, u32[]{:S(2)}, u32[]{:S(2)}) collective-permute-start(f32[1,256]{1,0:T(1,128)S(1)} %get-tuple-element.29), channel_id=1, source_target_pairs={{0,64},{64,0},{1,65},{65,1},{2,66},{66,2},{3,67},{67,3},{4,68},{68... | collective-permute-start | bytes 3080 | tf_op jit(solution)/shard_map/ppermute | solution.py:467
  37.7 0.7 collective-permute-start.4
  38.3 2.6 %collective-permute-start.3 = (f32[1,128]{1,0:T(1,128)S(1)}, f32[1,128]{1,0:T(1,128)S(1)}, u32[]{:S(2)}, u32[]{:S(2)}) collective-permute-start(f32[1,128]{1,0:T(1,128)S(1)} %get-tuple-element.30), channel_id=1, source_target_pairs={{0,1},{1,0},{2,3},{3,2},{4,5},{5,4},{6,7},{7,6},{8,9},{9,8},{10,11... | collective-permute-start | bytes 1544 | tf_op jit(solution)/shard_map/ppermute | solution.py:467
  40.9 0.8 collective-permute-done.3.y_in_ref
  41.7 0.0 collective-permute-done.2.z_in_ref
  41.7 0.0 collective-permute-done.4.z_over_ref
  41.7 0.4 second.1
  42.1 20.7 %all_to_all.36 = f32[128,1,256]{2,1,0:T(1,128)S(1)} all-to-all(f32[128,1,256]{2,1,0:T(1,128)S(1)} %bitcast.13), channel_id=1, replica_groups=mesh['zh'=8,'zl'=2,'xy'=32,'core'=2] {'zl','xy','core'}, dimensions={0} | all-to-all | bytes 262144 | tf_op jit(solution)/shard_map/all_to_all | solution.py:463
  62.7 0.6 third.1
  63.3 29.3 %all_to_all.37 = f32[32,1,640]{2,1,0:T(1,128)S(1)} all-to-all(f32[32,1,640]{2,1,0:T(1,128)S(1)} %bitcast.14), channel_id=1, replica_groups=mesh['zh'=8,'zl'=2,'xy'=32,'core'=2] {'zh','zl','core'}, dimensions={0} | all-to-all | bytes 163840 | tf_op jit(solution)/shard_map/all_to_all | solution.py:463
  92.6 0.2 fourth.1
  92.8 12.2 %all_to_all.38 = f32[32,1,1152]{2,1,0:T(1,128)S(1)} all-to-all(f32[32,1,1152]{2,1,0:T(1,128)S(1)} %bitcast.12), channel_id=1, replica_groups=mesh['zh'=8,'zl'=2,'xy'=32,'core'=2] {'xy'}, dimensions={0} | all-to-all | bytes 294912 | tf_op jit(solution)/shard_map/all_to_all | solution.py:463
  105.0 0.8 closing.1
Async XLA Ops:
  3.0 31.6 %all-to-all-start = ((f32[128,1,384]{2,1,0:T(1,128)}), f32[128,1,384]{2,1,0:T(1,128)S(1)}, u32[]{:S(2)}, u32[]{:S(2)}) async-start(f32[128,1,384]{2,1,0:T(1,128)} %bitcast), calls=%async_computation | async-start | bytes 393216 | tf_op jit(solution)/shard_map/all_to_all | solution.py:463
  22.3 6.3 %collective-permute-start.1 = (f32[32,128]{1,0:T(8,128)S(1)}, f32[32,128]{1,0:T(8,128)S(1)}, u32[]{:S(2)}, u32[]{:S(2)}) collective-permute-start(f32[32,128]{1,0:T(8,128)S(1)} %get-tuple-element.24), channel_id=1, source_target_pairs={{1,2},{3,4},{5,6},{7,8},{9,10},{11,12},{13,14},{15,16},{17,18},{19... | collective-permute-start | bytes 49160 | tf_op jit(solution)/shard_map/ppermute | solution.py:473
  25.9 0.7 collective-permute-start
  35.1 6.6 %collective-permute-start.2 = (f32[1,256]{1,0:T(1,128)S(1)}, f32[1,256]{1,0:T(1,128)S(1)}, u32[]{:S(2)}, u32[]{:S(2)}) collective-permute-start(f32[1,256]{1,0:T(1,128)S(1)} %get-tuple-element.29), channel_id=1, source_target_pairs={{0,64},{64,0},{1,65},{65,1},{2,66},{66,2},{3,67},{67,3},{4,68},{68... | collective-permute-start | bytes 3080 | tf_op jit(solution)/shard_map/ppermute | solution.py:467
  37.7 4.1 %collective-permute-start.4 = (f32[1,256]{1,0:T(1,128)S(1)}, f32[1,256]{1,0:T(1,128)S(1)}, u32[]{:S(2)}, u32[]{:S(2)}) collective-permute-start(f32[1,256]{1,0:T(1,128)S(1)} %get-tuple-element.31), channel_id=1, source_target_pairs={{64,128},{192,256},{320,384},{448,512},{576,640},{704,768},{832,89... | collective-permute-start | bytes 3080 | tf_op jit(solution)/shard_map/ppermute | solution.py:473
  38.3 3.4 %collective-permute-start.3 = (f32[1,128]{1,0:T(1,128)S(1)}, f32[1,128]{1,0:T(1,128)S(1)}, u32[]{:S(2)}, u32[]{:S(2)}) collective-permute-start(f32[1,128]{1,0:T(1,128)S(1)} %get-tuple-element.30), channel_id=1, source_target_pairs={{0,1},{1,0},{2,3},{3,2},{4,5},{5,4},{6,7},{7,6},{8,9},{9,8},{10,11... | collective-permute-start | bytes 1544 | tf_op jit(solution)/shard_map/ppermute | solution.py:467

commit v7 on v5

--- a/solution.py
+++ b/solution.py
@@ -186,7 +186,7 @@
         for k in range(steps)
     ]
     matrix = pltpu.make_async_copy(c_hbm, c_ref, sems.at[3])
-    for copy in small + parts + [matrix]:
+    for copy in parts[:2] + small + parts[2:] + [matrix]:
         copy.start()
     for copy in small:
         copy.wait()
@@ -196,8 +196,11 @@
         perm = jnp.where(classes == k, kinds_ref[k], perm)
     perm_ref[...] = perm
     upper = lax.axis_index("zl") == 0
-    over_ref[...] = jnp.where(upper, perm[:1], perm[-1:])
+    over = jnp.where(upper, perm[:1], perm[-1:])
     within = jnp.where(upper, perm[-1:], perm[:1])
+    over_ref[...] = jnp.zeros_like(over_ref)
+    for k in range(columns // LANES):
+        over_ref[k : k + 1, :] = over[:, k * LANES : (k + 1) * LANES]
     r = r_ref[...]
     first = lax.axis_index("core") == 0
     block = pl.multiple_of(jnp.where(first, 0, columns - LANES), LANES)
@@ -247,7 +250,7 @@
     left, right = beside_columns(got_ref, size, nev, rows)
     across = lax.axis_size("xy") * 2
     partner = (group_place() + jnp.where(upper, across, -across)) * size
-    over = over_ref[...]
+    over = jnp.concatenate([over_ref[k : k + 1, :] for k in range(size - 1)], axis=1)
     within = jnp.concatenate(
         [got_ref[pl.ds(partner + 1 + k, 1), :] for k in range(size - 1)], axis=1
     )
@@ -488,7 +491,7 @@
     perm, over, facing, message, r, vectors, matrix = call(
         opening_kernel, "opening",
         tuple(pltpu.with_memory_space_constraint(x, pltpu.HBM) for x in given),
-        [field, (1, columns), (rows, LANES), (size_first * group, LANES),
+        [field, (rows + 8, LANES), (rows, LANES), (size_first * group, LANES),
          field, eigenvectors.shape, coarse_inverse.shape],
         [pltpu.SMEM(class_perm.shape, jnp.float32), pltpu.VMEM(field, jnp.int32), per_vector,
          (size_first, LANES), pltpu.SemaphoreType.DMA((4 + PIECES,))],

time: 107 us -> 105 us (0.981)
  blocking collectives: 62.1 us -> 60.1 us
    all_to_all x3, blocking collectives: 62.1 us -> 60.1 us  [exchanged(): return lax.all_to_all(flat, axes, 0, 0, tiled=True).reshape(x.shape)]
where the time goes in v7:
time: 105 us; the launch traced here: 104 us
  blocking collectives  60.1 us (57%)
  starting transfers between devices  29.4 us (28%)
  waiting for transfers between devices  8.76 us (8%)
  Pallas kernels  4.79 us (5%)
    all_to_all x3, blocking collectives, exchanged(): return lax.all_to_all(flat, axes, 0, 0, tiled=True).reshape(x.shape)  60.1 us
    all_to_all x1, starting transfers between devices, exchanged(): return lax.all_to_all(flat, axes, 0, 0, tiled=True).reshape(x.shape)  19.3 us
    all_to_all x1, waiting for transfers between devices, exchanged(): return lax.all_to_all(flat, axes, 0, 0, tiled=True).reshape(x.shape)  7.97 us
    ppermute x2, starting transfers between devices, swap_in(): return lax.ppermute(x, axis, [(0, 1), (1, 0)])  5.18 us
    ppermute x3, starting transfers between devices, swap_over(): return lax.ppermute(x, axes, pairs + [(j, i) for i, j in pairs])  4.87 us
    pallas_call x6, Pallas kernels, call(): pl.pallas_call(kernel, out_shape=[jax.ShapeDtypeStruct(shape, jnp.float32...  4.79 us
  transfers between devices with their start and end apart: 6, of which 2 were waited for; matrix products, arithmetic and copies ran while one was open for 0% of the time, Pallas kernels for 1%

profile of v7, /device:TPU:1, one launch (start us, length us, event | category | flops | bytes accessed | tf_op | source)
XLA Modules:
  0.0 103.7 jit_solution(4933298160953965673)
XLA Ops:
  0.6 2.3 %opening.1 = (f32[32,256]{1,0:T(8,128)S(1)}, f32[40,128]{1,0:T(8,128)S(1)}, f32[32,128]{1,0:T(8,128)S(1)}, f32[384,128]{1,0:T(8,128)}, f32[32,256]{1,0:T(8,128)S...) custom-call(f32[4]{0:T(128)} %kinds_hbm.1, f32[32,256]{1,0:T(8,128)} %r_hbm.1, s32[32,256]{1,0:T(8,128)} %map_hbm.1, ...), custom_call_target="tpu_custom_call" | custom-call | tf_op jit(solution)/shard_map/opening/pallas_call | solution.py:453
  3.0 19.3 %all-to-all-start = ((f32[128,1,384]{2,1,0:T(1,128)}), f32[128,1,384]{2,1,0:T(1,128)S(1)}, u32[]{:S(2)}, u32[]{:S(2)}) async-start(f32[128,1,384]{2,1,0:T(1,128)} %bitcast), calls=%async_computation | async-start | bytes 393216 | tf_op jit(solution)/shard_map/all_to_all | solution.py:466
  22.3 0.7 collective-permute-start
  23.0 3.5 %collective-permute-start.4 = (f32[32,128]{1,0:T(8,128)S(1)}, f32[32,128]{1,0:T(8,128)S(1)}, u32[]{:S(2)}, u32[]{:S(2)}) collective-permute-start(f32[32,128]{1,0:T(8,128)S(1)} %get-tuple-element.31), channel_id=1, source_target_pairs={{1,2},{3,4},{5,6},{7,8},{9,10},{11,12},{13,14},{15,16},{17,18},{19... | collective-permute-start | bytes 49160 | tf_op jit(solution)/shard_map/ppermute | solution.py:476
  26.5 0.0 collective-permute-done.over_ref
  26.5 8.0 %all-to-all-done = f32[128,1,384]{2,1,0:T(1,128)S(1)} async-done(((f32[128,1,384]{2,1,0:T(1,128)}), f32[128,1,384]{2,1,0:T(1,128)S(1)}, u32[]{:S(2)}, u32[]{:S(2)}) %all-to-all-start) | async-done | bytes 196640 | tf_op jit(solution)/shard_map/all_to_all | solution.py:466
  34.5 0.5 first.1
  35.1 2.6 %collective-permute-start.1 = (f32[1,256]{1,0:T(1,128)S(1)}, f32[1,256]{1,0:T(1,128)S(1)}, u32[]{:S(2)}, u32[]{:S(2)}) collective-permute-start(f32[1,256]{1,0:T(1,128)S(1)} %get-tuple-element.28), channel_id=1, source_target_pairs={{0,64},{64,0},{1,65},{65,1},{2,66},{66,2},{3,67},{67,3},{4,68},{68... | collective-permute-start | bytes 3080 | tf_op jit(solution)/shard_map/ppermute | solution.py:470
  37.7 0.7 collective-permute-start.3
  38.3 2.6 %collective-permute-start.2 = (f32[1,128]{1,0:T(1,128)S(1)}, f32[1,128]{1,0:T(1,128)S(1)}, u32[]{:S(2)}, u32[]{:S(2)}) collective-permute-start(f32[1,128]{1,0:T(1,128)S(1)} %get-tuple-element.29), channel_id=1, source_target_pairs={{0,1},{1,0},{2,3},{3,2},{4,5},{5,4},{6,7},{7,6},{8,9},{9,8},{10,11... | collective-permute-start | bytes 1544 | tf_op jit(solution)/shard_map/ppermute | solution.py:470
  40.9 0.0 collective-permute-done.4.facing_ref
  40.9 0.8 collective-permute-done.2.y_in_ref
  41.7 0.0 collective-permute-done.1.z_in_ref
  41.7 0.0 collective-permute-done.3.z_over_ref
  41.7 0.4 second.1
  42.1 18.9 %all_to_all.36 = f32[128,1,256]{2,1,0:T(1,128)S(1)} all-to-all(f32[128,1,256]{2,1,0:T(1,128)S(1)} %bitcast.13), channel_id=1, replica_groups=mesh['zh'=8,'zl'=2,'xy'=32,'core'=2] {'zl','xy','core'}, dimensions={0} | all-to-all | bytes 262144 | tf_op jit(solution)/shard_map/all_to_all | solution.py:466
  61.0 0.6 third.1
  61.6 29.0 %all_to_all.37 = f32[32,1,640]{2,1,0:T(1,128)S(1)} all-to-all(f32[32,1,640]{2,1,0:T(1,128)S(1)} %bitcast.14), channel_id=1, replica_groups=mesh['zh'=8,'zl'=2,'xy'=32,'core'=2] {'zh','zl','core'}, dimensions={0} | all-to-all | bytes 163840 | tf_op jit(solution)/shard_map/all_to_all | solution.py:466
  90.6 0.2 fourth.1
  90.8 12.2 %all_to_all.38 = f32[32,1,1152]{2,1,0:T(1,128)S(1)} all-to-all(f32[32,1,1152]{2,1,0:T(1,128)S(1)} %bitcast.12), channel_id=1, replica_groups=mesh['zh'=8,'zl'=2,'xy'=32,'core'=2] {'xy'}, dimensions={0} | all-to-all | bytes 294912 | tf_op jit(solution)/shard_map/all_to_all | solution.py:466
  102.9 0.8 closing.1
Async XLA Ops:
  3.0 31.5 %all-to-all-start = ((f32[128,1,384]{2,1,0:T(1,128)}), f32[128,1,384]{2,1,0:T(1,128)S(1)}, u32[]{:S(2)}, u32[]{:S(2)}) async-start(f32[128,1,384]{2,1,0:T(1,128)} %bitcast), calls=%async_computation | async-start | bytes 393216 | tf_op jit(solution)/shard_map/all_to_all | solution.py:466
  22.3 4.2 %collective-permute-start = (f32[40,128]{1,0:T(8,128)S(1)}, f32[40,128]{1,0:T(8,128)S(1)}, u32[]{:S(2)}, u32[]{:S(2)}) collective-permute-start(f32[40,128]{1,0:T(8,128)S(1)} %get-tuple-element.23), channel_id=1, source_target_pairs={{64,128},{192,256},{320,384},{448,512},{576,640},{704,768},{832,89... | collective-permute-start | bytes 61448 | tf_op jit(solution)/shard_map/ppermute | solution.py:476
  23.0 17.9 %collective-permute-start.4 = (f32[32,128]{1,0:T(8,128)S(1)}, f32[32,128]{1,0:T(8,128)S(1)}, u32[]{:S(2)}, u32[]{:S(2)}) collective-permute-start(f32[32,128]{1,0:T(8,128)S(1)} %get-tuple-element.31), channel_id=1, source_target_pairs={{1,2},{3,4},{5,6},{7,8},{9,10},{11,12},{13,14},{15,16},{17,18},{19... | collective-permute-start | bytes 49160 | tf_op jit(solution)/shard_map/ppermute | solution.py:476
  35.1 6.7 %collective-permute-start.1 = (f32[1,256]{1,0:T(1,128)S(1)}, f32[1,256]{1,0:T(1,128)S(1)}, u32[]{:S(2)}, u32[]{:S(2)}) collective-permute-start(f32[1,256]{1,0:T(1,128)S(1)} %get-tuple-element.28), channel_id=1, source_target_pairs={{0,64},{64,0},{1,65},{65,1},{2,66},{66,2},{3,67},{67,3},{4,68},{68... | collective-permute-start | bytes 3080 | tf_op jit(solution)/shard_map/ppermute | solution.py:470
  37.7 4.1 %collective-permute-start.3 = (f32[1,256]{1,0:T(1,128)S(1)}, f32[1,256]{1,0:T(1,128)S(1)}, u32[]{:S(2)}, u32[]{:S(2)}) collective-permute-start(f32[1,256]{1,0:T(1,128)S(1)} %get-tuple-element.30), channel_id=1, source_target_pairs={{64,128},{192,256},{320,384},{448,512},{576,640},{704,768},{832,89... | collective-permute-start | bytes 3080 | tf_op jit(solution)/shard_map/ppermute | solution.py:476
  38.3 3.4 %collective-permute-start.2 = (f32[1,128]{1,0:T(1,128)S(1)}, f32[1,128]{1,0:T(1,128)S(1)}, u32[]{:S(2)}, u32[]{:S(2)}) collective-permute-start(f32[1,128]{1,0:T(1,128)S(1)} %get-tuple-element.29), channel_id=1, source_target_pairs={{0,1},{1,0},{2,3},{3,2},{4,5},{5,4},{6,7},{7,6},{8,9},{9,8},{10,11... | collective-permute-start | bytes 1544 | tf_op jit(solution)/shard_map/ppermute | solution.py:470

commit v8 on v7

--- a/solution.py
+++ b/solution.py
@@ -272,7 +272,7 @@
     z_over_ref[...] = jnp.where(upper, top, low)
     z_in_ref[...] = jnp.where(upper, low, top)
     lefts, rights = to_lanes((faces[2] * z)[:, :1], 0), to_lanes((faces[3] * z)[:, -1:], 0)
-    y_in_ref[...] = jnp.where(first, rights, lefts)
+    y_in_ref[...] = jnp.broadcast_to(jnp.where(first, rights, lefts), y_in_ref.shape)
 
 
 def second_kernel(
@@ -283,7 +283,7 @@
     first = lax.axis_index("core") == 0
     stencil = Stencil(coef_ref)
     over, within = z_over_ref[...], z_in_ref[...]
-    y_in = to_column(y_in_ref[...], 0, rows)
+    y_in = to_column(y_in_ref[:1, :], 0, rows)
     halo = (
         jnp.where(upper, over, within),
         jnp.where(upper, within, over),
@@ -501,7 +501,7 @@
     got = exchanged(message, GROUP, size_first)
     z0, coef, z_over, z_in, y_in = call(
         first_kernel, "first", (got, over, perm, r, vectors, matrix),
-        [field, (6,) + field, (1, columns), (1, columns), (1, LANES)], [per_vector],
+        [field, (6,) + field, (1, columns), (1, columns), (8, LANES)], [per_vector],
     )
     z_in, y_in = swap_in(z_in, "zl"), swap_in(y_in, "core")
     z_over = swap_over(z_over, ROWS)

time: 105 us -> 106 us (level)
  no operation moved by 1% of the time
where the time goes in v8:
time: 106 us; the launch traced here: 104 us
  blocking collectives  60.9 us (57%)
  starting transfers between devices  29.1 us (27%)
  waiting for transfers between devices  9 us (8%)
  Pallas kernels  4.79 us (5%)
    all_to_all x3, blocking collectives, exchanged(): return lax.all_to_all(flat, axes, 0, 0, tiled=True).reshape(x.shape)  60.9 us
    all_to_all x1, starting transfers between devices, exchanged(): return lax.all_to_all(flat, axes, 0, 0, tiled=True).reshape(x.shape)  19.3 us
    all_to_all x1, waiting for transfers between devices, exchanged(): return lax.all_to_all(flat, axes, 0, 0, tiled=True).reshape(x.shape)  7.97 us
    ppermute x2, starting transfers between devices, swap_in(): return lax.ppermute(x, axis, [(0, 1), (1, 0)])  4.9 us
    ppermute x3, starting transfers between devices, swap_over(): return lax.ppermute(x, axes, pairs + [(j, i) for i, j in pairs])  4.87 us
    pallas_call x6, Pallas kernels, call(): pl.pallas_call(kernel, out_shape=[jax.ShapeDtypeStruct(shape, jnp.float32...  4.79 us
  transfers between devices with their start and end apart: 6, of which 2 were waited for; matrix products, arithmetic and copies ran while one was open for 0% of the time, Pallas kernels for 1%

profile of v8, /device:TPU:1, one launch (start us, length us, event | category | flops | bytes accessed | tf_op | source)
XLA Modules:
  0.0 104.5 jit_solution(7737662262883383504)
XLA Ops:
  0.6 2.3 %opening.1 = (f32[32,256]{1,0:T(8,128)S(1)}, f32[40,128]{1,0:T(8,128)S(1)}, f32[32,128]{1,0:T(8,128)S(1)}, f32[384,128]{1,0:T(8,128)}, f32[32,256]{1,0:T(8,128)S...) custom-call(f32[4]{0:T(128)} %kinds_hbm.1, f32[32,256]{1,0:T(8,128)} %r_hbm.1, s32[32,256]{1,0:T(8,128)} %map_hbm.1, ...), custom_call_target="tpu_custom_call" | custom-call | tf_op jit(solution)/shard_map/opening/pallas_call | solution.py:453
  3.0 19.3 %all-to-all-start = ((f32[128,1,384]{2,1,0:T(1,128)}), f32[128,1,384]{2,1,0:T(1,128)S(1)}, u32[]{:S(2)}, u32[]{:S(2)}) async-start(f32[128,1,384]{2,1,0:T(1,128)} %bitcast), calls=%async_computation | async-start | bytes 393216 | tf_op jit(solution)/shard_map/all_to_all | solution.py:466
  22.3 0.7 collective-permute-start
  23.0 3.5 %collective-permute-start.4 = (f32[32,128]{1,0:T(8,128)S(1)}, f32[32,128]{1,0:T(8,128)S(1)}, u32[]{:S(2)}, u32[]{:S(2)}) collective-permute-start(f32[32,128]{1,0:T(8,128)S(1)} %get-tuple-element.31), channel_id=1, source_target_pairs={{1,2},{3,4},{5,6},{7,8},{9,10},{11,12},{13,14},{15,16},{17,18},{19... | collective-permute-start | bytes 49160 | tf_op jit(solution)/shard_map/ppermute | solution.py:476
  26.5 0.0 collective-permute-done.over_ref
  26.5 8.0 %all-to-all-done = f32[128,1,384]{2,1,0:T(1,128)S(1)} async-done(((f32[128,1,384]{2,1,0:T(1,128)}), f32[128,1,384]{2,1,0:T(1,128)S(1)}, u32[]{:S(2)}, u32[]{:S(2)}) %all-to-all-start) | async-done | bytes 196640 | tf_op jit(solution)/shard_map/all_to_all | solution.py:466
  34.5 0.5 first.1
  35.1 2.3 %collective-permute-start.2 = (f32[8,128]{1,0:T(8,128)S(1)}, f32[8,128]{1,0:T(8,128)S(1)}, u32[]{:S(2)}, u32[]{:S(2)}) collective-permute-start(f32[8,128]{1,0:T(8,128)S(1)} %get-tuple-element.29), channel_id=1, source_target_pairs={{0,1},{1,0},{2,3},{3,2},{4,5},{5,4},{6,7},{7,6},{8,9},{9,8},{10,11... | collective-permute-start | bytes 12296 | tf_op jit(solution)/shard_map/ppermute | solution.py:470
  37.4 2.6 %collective-permute-start.1 = (f32[1,256]{1,0:T(1,128)S(1)}, f32[1,256]{1,0:T(1,128)S(1)}, u32[]{:S(2)}, u32[]{:S(2)}) collective-permute-start(f32[1,256]{1,0:T(1,128)S(1)} %get-tuple-element.28), channel_id=1, source_target_pairs={{0,64},{64,0},{1,65},{65,1},{2,66},{66,2},{3,67},{67,3},{4,68},{68... | collective-permute-start | bytes 3080 | tf_op jit(solution)/shard_map/ppermute | solution.py:470
  40.0 0.7 collective-permute-start.3
  40.6 0.0 collective-permute-done.4.facing_ref
  40.6 1.0 collective-permute-done.1.z_in_ref
  41.7 0.0 collective-permute-done.3.z_over_ref
  41.7 0.0 collective-permute-done.2.y_in_ref
  41.7 0.4 second.1
  42.0 20.0 %all_to_all.36 = f32[128,1,256]{2,1,0:T(1,128)S(1)} all-to-all(f32[128,1,256]{2,1,0:T(1,128)S(1)} %bitcast.13), channel_id=1, replica_groups=mesh['zh'=8,'zl'=2,'xy'=32,'core'=2] {'zl','xy','core'}, dimensions={0} | all-to-all | bytes 262144 | tf_op jit(solution)/shard_map/all_to_all | solution.py:466
  62.0 0.6 third.1
  62.6 28.7 %all_to_all.37 = f32[32,1,640]{2,1,0:T(1,128)S(1)} all-to-all(f32[32,1,640]{2,1,0:T(1,128)S(1)} %bitcast.14), channel_id=1, replica_groups=mesh['zh'=8,'zl'=2,'xy'=32,'core'=2] {'zh','zl','core'}, dimensions={0} | all-to-all | bytes 163840 | tf_op jit(solution)/shard_map/all_to_all | solution.py:466
  91.3 0.2 fourth.1
  91.5 12.2 %all_to_all.38 = f32[32,1,1152]{2,1,0:T(1,128)S(1)} all-to-all(f32[32,1,1152]{2,1,0:T(1,128)S(1)} %bitcast.12), channel_id=1, replica_groups=mesh['zh'=8,'zl'=2,'xy'=32,'core'=2] {'xy'}, dimensions={0} | all-to-all | bytes 294912 | tf_op jit(solution)/shard_map/all_to_all | solution.py:466
  103.7 0.8 closing.1
Async XLA Ops:
  3.0 31.5 %all-to-all-start = ((f32[128,1,384]{2,1,0:T(1,128)}), f32[128,1,384]{2,1,0:T(1,128)S(1)}, u32[]{:S(2)}, u32[]{:S(2)}) async-start(f32[128,1,384]{2,1,0:T(1,128)} %bitcast), calls=%async_computation | async-start | bytes 393216 | tf_op jit(solution)/shard_map/all_to_all | solution.py:466
  22.3 4.2 %collective-permute-start = (f32[40,128]{1,0:T(8,128)S(1)}, f32[40,128]{1,0:T(8,128)S(1)}, u32[]{:S(2)}, u32[]{:S(2)}) collective-permute-start(f32[40,128]{1,0:T(8,128)S(1)} %get-tuple-element.23), channel_id=1, source_target_pairs={{64,128},{192,256},{320,384},{448,512},{576,640},{704,768},{832,89... | collective-permute-start | bytes 61448 | tf_op jit(solution)/shard_map/ppermute | solution.py:476
  23.0 17.7 %collective-permute-start.4 = (f32[32,128]{1,0:T(8,128)S(1)}, f32[32,128]{1,0:T(8,128)S(1)}, u32[]{:S(2)}, u32[]{:S(2)}) collective-permute-start(f32[32,128]{1,0:T(8,128)S(1)} %get-tuple-element.31), channel_id=1, source_target_pairs={{1,2},{3,4},{5,6},{7,8},{9,10},{11,12},{13,14},{15,16},{17,18},{19... | collective-permute-start | bytes 49160 | tf_op jit(solution)/shard_map/ppermute | solution.py:476
  35.1 6.6 %collective-permute-start.2 = (f32[8,128]{1,0:T(8,128)S(1)}, f32[8,128]{1,0:T(8,128)S(1)}, u32[]{:S(2)}, u32[]{:S(2)}) collective-permute-start(f32[8,128]{1,0:T(8,128)S(1)} %get-tuple-element.29), channel_id=1, source_target_pairs={{0,1},{1,0},{2,3},{3,2},{4,5},{5,4},{6,7},{7,6},{8,9},{9,8},{10,11... | collective-permute-start | bytes 12296 | tf_op jit(solution)/shard_map/ppermute | solution.py:470
  37.4 4.3 %collective-permute-start.1 = (f32[1,256]{1,0:T(1,128)S(1)}, f32[1,256]{1,0:T(1,128)S(1)}, u32[]{:S(2)}, u32[]{:S(2)}) collective-permute-start(f32[1,256]{1,0:T(1,128)S(1)} %get-tuple-element.28), channel_id=1, source_target_pairs={{0,64},{64,0},{1,65},{65,1},{2,66},{66,2},{3,67},{67,3},{4,68},{68... | collective-permute-start | bytes 3080 | tf_op jit(solution)/shard_map/ppermute | solution.py:470
  40.0 1.7 %collective-permute-start.3 = (f32[1,256]{1,0:T(1,128)S(1)}, f32[1,256]{1,0:T(1,128)S(1)}, u32[]{:S(2)}, u32[]{:S(2)}) collective-permute-start(f32[1,256]{1,0:T(1,128)S(1)} %get-tuple-element.30), channel_id=1, source_target_pairs={{64,128},{192,256},{320,384},{448,512},{576,640},{704,768},{832,89... | collective-permute-start | bytes 3080 | tf_op jit(solution)/shard_map/ppermute | solution.py:476

commit v9 on v8

--- a/solution.py
+++ b/solution.py
@@ -167,7 +167,7 @@
 
 def opening_kernel(
     kinds_hbm, r_hbm, map_hbm, e_hbm, c_hbm,
-    perm_ref, over_ref, facing_ref, out_ref, r_ref, e_ref, c_ref,
+    perm_ref, over_ref, facing_ref, inside_ref, out_ref, r_ref, e_ref, c_ref,
     kinds_ref, map_ref, rows_ref, block_ref, sems,
 ):
     nev, rows, columns = e_ref.shape
@@ -204,16 +204,21 @@
     r = r_ref[...]
     first = lax.axis_index("core") == 0
     block = pl.multiple_of(jnp.where(first, 0, columns - LANES), LANES)
+    other = pl.multiple_of(jnp.where(first, columns - LANES, 0), LANES)
     turn = jnp.where(first, 0, 1)
     lane = iota((rows, LANES), 1)
     facing = jnp.zeros((rows, LANES), jnp.float32)
+    inside = facing
     for k in range(steps):
         parts[k].wait()
         for e in range(k * chunk, (k + 1) * chunk):
             project_one(e_ref[e], r, rows_ref, e)
             edge = pltpu.roll(e_ref[e, :, pl.ds(block, LANES)], e + turn, 1)
             facing = jnp.where(lane == e, edge, facing)
+            edge = pltpu.roll(e_ref[e, :, pl.ds(other, LANES)], e + 1 - turn, 1)
+            inside = jnp.where(lane == e, edge, inside)
     facing_ref[...] = facing
+    inside_ref[...] = inside
     c = jnp.sum(rows_ref[...], axis=1, keepdims=True)
     start = lane_start(group_place(), nev)
     size = block_ref.shape[0]
@@ -241,12 +246,11 @@
 
 def first_kernel(
     got_ref, over_ref, perm_ref, r_ref, e_ref, c_ref,
-    z_ref, coef_ref, z_over_ref, z_in_ref, y_in_ref, rows_ref,
+    z_ref, coef_ref, z_over_ref, z_in_ref, rows_ref,
 ):
     nev, rows, columns = e_ref.shape
     size = columns // LANES + 1
     upper = lax.axis_index("zl") == 0
-    first = lax.axis_index("core") == 0
     left, right = beside_columns(got_ref, size, nev, rows)
     across = lax.axis_size("xy") * 2
     partner = (group_place() + jnp.where(upper, across, -across)) * size
@@ -271,37 +275,30 @@
     top, low = (faces[0] * z)[:1], (faces[1] * z)[-1:]
     z_over_ref[...] = jnp.where(upper, top, low)
     z_in_ref[...] = jnp.where(upper, low, top)
-    lefts, rights = to_lanes((faces[2] * z)[:, :1], 0), to_lanes((faces[3] * z)[:, -1:], 0)
-    y_in_ref[...] = jnp.broadcast_to(jnp.where(first, rights, lefts), y_in_ref.shape)
 
 
 def second_kernel(
-    z_in_ref, y_in_ref, z_over_ref, facing_ref, z_ref, coef_ref, e_ref, q_ref, out_ref, rows_ref
+    z_over_ref, z_in_ref, facing_ref, inside_ref, z_ref, coef_ref, e_ref, q_ref, out_ref, rows_ref
 ):
     nev, rows, _ = e_ref.shape
     upper = lax.axis_index("zl") == 0
     first = lax.axis_index("core") == 0
     stencil = Stencil(coef_ref)
     over, within = z_over_ref[...], z_in_ref[...]
-    y_in = to_column(y_in_ref[:1, :], 0, rows)
-    halo = (
-        jnp.where(upper, over, within),
-        jnp.where(upper, within, over),
-        jnp.where(first, 0.0, y_in),
-        jnp.where(first, y_in, 0.0),
-    )
     z = z_ref[...]
     q = stencil.apply(z)
-    for edge, outside in zip(stencil.edges, halo):
-        q = q - jnp.where(edge, outside, 0.0)
+    q = q - jnp.where(stencil.edges[0], jnp.where(upper, over, within), 0.0)
+    q = q - jnp.where(stencil.edges[1], jnp.where(upper, within, over), 0.0)
     q_ref[...] = q
     left, right = (stencil.faces[2] * z)[:, :1], (stencil.faces[3] * z)[:, -1:]
-    edge = jnp.where(first, left, right)
     start = lane_start(group_place(), nev)
-    own = to_lanes(project(e_ref, q, rows_ref), start) + to_lanes(edge, start + nev)
-    added = jnp.sum(facing_ref[...] * edge, axis=0, keepdims=True)
-    step = jnp.where(first, LANES - nev, nev)
-    added = pltpu.roll(added, lax.rem(start + step, LANES), 1)
+    own = to_lanes(project(e_ref, q, rows_ref), start)
+    own = own + to_lanes(left, start + nev) + to_lanes(right, start + nev + rows)
+    facing, inside = facing_ref[...], inside_ref[...]
+    to_left = jnp.sum(jnp.where(first, facing, inside) * left, axis=0, keepdims=True)
+    to_right = jnp.sum(jnp.where(first, inside, facing) * right, axis=0, keepdims=True)
+    added = pltpu.roll(to_left, lax.rem(start - nev + LANES, LANES), 1)
+    added = added + pltpu.roll(to_right, lax.rem(start + nev, LANES), 1)
     sub = iota((8, LANES), 0)
     pair = jnp.where(lax.rem(sub, 2) == 0, own, -added)
     for k in range(out_ref.shape[0] // 8):
@@ -316,12 +313,8 @@
     half = columns // LANES
     stencil = Stencil(coef_ref)
     z, r = z_ref[...], r_ref[...]
-    first = lax.axis_index("core") == 0
-    place, b, count = group_place(), column_place(), group_ref.shape[0]
-    near = jnp.where(first, jnp.maximum(place - 1, 0), jnp.minimum(place + 1, count - 1))
-    edge = to_column(got_ref[pl.ds(2 * near, 1), :], lane_start(near, nev) + nev, rows)
-    left = jnp.where(first & (b > 0), edge, 0.0)
-    right = jnp.where((~first) & (b < lax.axis_size("xy") * 2 - 1), edge, 0.0)
+    count = group_ref.shape[0]
+    left, right = beside_columns(got_ref, 2, nev, rows)
     q = q_ref[...] - jnp.where(stencil.edges[2], left, 0.0)
     q = q - jnp.where(stencil.edges[3], right, 0.0)
     q_out_ref[...] = q
@@ -488,25 +481,25 @@
 
     size_first = columns // LANES + 1
     given = (class_perm, right_side, class_map, eigenvectors, coarse_inverse)
-    perm, over, facing, message, r, vectors, matrix = call(
+    perm, over, facing, inside, message, r, vectors, matrix = call(
         opening_kernel, "opening",
         tuple(pltpu.with_memory_space_constraint(x, pltpu.HBM) for x in given),
-        [field, (rows + 8, LANES), (rows, LANES), (size_first * group, LANES),
+        [field, (rows + 8, LANES), (rows, LANES), (rows, LANES), (size_first * group, LANES),
          field, eigenvectors.shape, coarse_inverse.shape],
         [pltpu.SMEM(class_perm.shape, jnp.float32), pltpu.VMEM(field, jnp.int32), per_vector,
          (size_first, LANES), pltpu.SemaphoreType.DMA((4 + PIECES,))],
         by_hand=True,
     )
     over, facing = swap_over(over, ROWS), swap_over(facing, COLS)
+    inside = swap_in(inside, "core")
     got = exchanged(message, GROUP, size_first)
-    z0, coef, z_over, z_in, y_in = call(
+    z0, coef, z_over, z_in = call(
         first_kernel, "first", (got, over, perm, r, vectors, matrix),
-        [field, (6,) + field, (1, columns), (1, columns), (8, LANES)], [per_vector],
-    )
-    z_in, y_in = swap_in(z_in, "zl"), swap_in(y_in, "core")
-    z_over = swap_over(z_over, ROWS)
+        [field, (6,) + field, (1, columns), (1, columns)], [per_vector],
+    )
+    z_over, z_in = swap_over(z_over, ROWS), swap_in(z_in, "zl")
     q0, message = call(
-        second_kernel, "second", (z_in, y_in, z_over, facing, z0, coef, vectors),
+        second_kernel, "second", (z_over, z_in, facing, inside, z0, coef, vectors),
         [field, (2 * group, LANES)], [per_vector],
     )
     got = exchanged(message, GROUP, 2)

time: 106 us -> 106 us (level)
  waiting for transfers between devices: 9 us -> 6.96 us
    all_to_all x1, waiting for transfers between devices: 7.97 us -> 6.04 us  [exchanged(): return lax.all_to_all(flat, axes, 0, 0, tiled=True).reshape(x.shape)]
  transfers between devices with their start and end apart: 6 -> 6, of which waited for: 2 -> 2; matrix products, arithmetic and copies ran while one was open for 0% -> 0% of each run, Pallas kernels for 1% -> 0%
where the time goes in v9:
time: 106 us; the launch traced here: 104 us
  blocking collectives  61.7 us (58%)
  starting transfers between devices  30 us (28%)
  waiting for transfers between devices  6.96 us (7%)
  Pallas kernels  4.78 us (5%)
    all_to_all x3, blocking collectives, exchanged(): return lax.all_to_all(flat, axes, 0, 0, tiled=True).reshape(x.shape)  61.7 us
    all_to_all x1, starting transfers between devices, exchanged(): return lax.all_to_all(flat, axes, 0, 0, tiled=True).reshape(x.shape)  19.3 us
    all_to_all x1, waiting for transfers between devices, exchanged(): return lax.all_to_all(flat, axes, 0, 0, tiled=True).reshape(x.shape)  6.04 us
    ppermute x2, starting transfers between devices, swap_in(): return lax.ppermute(x, axis, [(0, 1), (1, 0)])  5.78 us
    ppermute x3, starting transfers between devices, swap_over(): return lax.ppermute(x, axes, pairs + [(j, i) for i, j in pairs])  4.87 us
    pallas_call x6, Pallas kernels, call(): pl.pallas_call(kernel, out_shape=[jax.ShapeDtypeStruct(shape, jnp.float32...  4.78 us
  transfers between devices with their start and end apart: 6, of which 2 were waited for; matrix products, arithmetic and copies ran while one was open for 0% of the time, Pallas kernels for 0%

profile of v9, /device:TPU:1, one launch (start us, length us, event | category | flops | bytes accessed | tf_op | source)
XLA Modules:
  0.0 104.1 jit_solution(252398025741310232)
XLA Ops:
  0.6 2.5 %opening.1 = (f32[32,256]{1,0:T(8,128)S(1)}, f32[40,128]{1,0:T(8,128)S(1)}, f32[32,128]{1,0:T(8,128)S(1)}, f32[32,128]{1,0:T(8,128)S(1)}, f32[384,128]{1,0:T(8,1...) custom-call(f32[4]{0:T(128)} %kinds_hbm.1, f32[32,256]{1,0:T(8,128)} %r_hbm.1, ...), custom_call_target="tpu_custom_call" | custom-call | tf_op jit(solution)/shard_map/opening/pallas_call | solution.py:446
  3.1 19.3 %all-to-all-start = ((f32[128,1,384]{2,1,0:T(1,128)}), f32[128,1,384]{2,1,0:T(1,128)S(1)}, u32[]{:S(2)}, u32[]{:S(2)}) async-start(f32[128,1,384]{2,1,0:T(1,128)} %bitcast), calls=%async_computation | async-start | bytes 393216 | tf_op jit(solution)/shard_map/all_to_all | solution.py:459
  22.5 0.7 collective-permute-start
  23.1 3.5 %collective-permute-start.3 = (f32[32,128]{1,0:T(8,128)S(1)}, f32[32,128]{1,0:T(8,128)S(1)}, u32[]{:S(2)}, u32[]{:S(2)}) collective-permute-start(f32[32,128]{1,0:T(8,128)S(1)} %get-tuple-element.30), channel_id=1, source_target_pairs={{1,2},{3,4},{5,6},{7,8},{9,10},{11,12},{13,14},{15,16},{17,18},{19... | collective-permute-start | bytes 49160 | tf_op jit(solution)/shard_map/ppermute | solution.py:469
  26.7 1.9 %collective-permute-start.4 = (f32[32,128]{1,0:T(8,128)S(1)}, f32[32,128]{1,0:T(8,128)S(1)}, u32[]{:S(2)}, u32[]{:S(2)}) collective-permute-start(f32[32,128]{1,0:T(8,128)S(1)} %get-tuple-element.31), channel_id=1, source_target_pairs={{0,1},{1,0},{2,3},{3,2},{4,5},{5,4},{6,7},{7,6},{8,9},{9,8},{10,11... | collective-permute-start | bytes 49160 | tf_op jit(solution)/shard_map/ppermute | solution.py:463
  28.6 0.0 collective-permute-done.over_ref
  28.6 6.0 %all-to-all-done = f32[128,1,384]{2,1,0:T(1,128)S(1)} async-done(((f32[128,1,384]{2,1,0:T(1,128)}), f32[128,1,384]{2,1,0:T(1,128)S(1)}, u32[]{:S(2)}, u32[]{:S(2)}) %all-to-all-start) | async-done | bytes 196640 | tf_op jit(solution)/shard_map/all_to_all | solution.py:459
  34.7 0.4 first.1
  35.1 0.7 collective-permute-start.1
  35.8 3.9 %collective-permute-start.2 = (f32[1,256]{1,0:T(1,128)S(1)}, f32[1,256]{1,0:T(1,128)S(1)}, u32[]{:S(2)}, u32[]{:S(2)}) collective-permute-start(f32[1,256]{1,0:T(1,128)S(1)} %get-tuple-element.29), channel_id=1, source_target_pairs={{0,64},{64,0},{1,65},{65,1},{2,66},{66,2},{3,67},{67,3},{4,68},{68... | collective-permute-start | bytes 3080 | tf_op jit(solution)/shard_map/ppermute | solution.py:463
  39.6 0.0 collective-permute-done.3.facing_ref
  39.6 0.0 collective-permute-done.4.inside_ref
  39.6 0.0 collective-permute-done.1.z_over_ref
  39.7 0.9 collective-permute-done.2.z_in_ref
  40.6 0.3 second.1
  40.9 21.6 %all_to_all.36 = f32[128,1,256]{2,1,0:T(1,128)S(1)} all-to-all(f32[128,1,256]{2,1,0:T(1,128)S(1)} %bitcast.13), channel_id=1, replica_groups=mesh['zh'=8,'zl'=2,'xy'=32,'core'=2] {'zl','xy','core'}, dimensions={0} | all-to-all | bytes 262144 | tf_op jit(solution)/shard_map/all_to_all | solution.py:459
  62.5 0.6 third.1
  63.1 27.9 %all_to_all.37 = f32[32,1,640]{2,1,0:T(1,128)S(1)} all-to-all(f32[32,1,640]{2,1,0:T(1,128)S(1)} %bitcast.14), channel_id=1, replica_groups=mesh['zh'=8,'zl'=2,'xy'=32,'core'=2] {'zh','zl','core'}, dimensions={0} | all-to-all | bytes 163840 | tf_op jit(solution)/shard_map/all_to_all | solution.py:459
  91.0 0.2 fourth.1
  91.2 12.2 %all_to_all.38 = f32[32,1,1152]{2,1,0:T(1,128)S(1)} all-to-all(f32[32,1,1152]{2,1,0:T(1,128)S(1)} %bitcast.12), channel_id=1, replica_groups=mesh['zh'=8,'zl'=2,'xy'=32,'core'=2] {'xy'}, dimensions={0} | all-to-all | bytes 294912 | tf_op jit(solution)/shard_map/all_to_all | solution.py:459
  103.3 0.8 closing.1
Async XLA Ops:
  3.1 31.5 %all-to-all-start = ((f32[128,1,384]{2,1,0:T(1,128)}), f32[128,1,384]{2,1,0:T(1,128)S(1)}, u32[]{:S(2)}, u32[]{:S(2)}) async-start(f32[128,1,384]{2,1,0:T(1,128)} %bitcast), calls=%async_computation | async-start | bytes 393216 | tf_op jit(solution)/shard_map/all_to_all | solution.py:459
  22.5 6.2 %collective-permute-start = (f32[40,128]{1,0:T(8,128)S(1)}, f32[40,128]{1,0:T(8,128)S(1)}, u32[]{:S(2)}, u32[]{:S(2)}) collective-permute-start(f32[40,128]{1,0:T(8,128)S(1)} %get-tuple-element.23), channel_id=1, source_target_pairs={{64,128},{192,256},{320,384},{448,512},{576,640},{704,768},{832,89... | collective-permute-start | bytes 61448 | tf_op jit(solution)/shard_map/ppermute | solution.py:469
  23.1 16.5 %collective-permute-start.3 = (f32[32,128]{1,0:T(8,128)S(1)}, f32[32,128]{1,0:T(8,128)S(1)}, u32[]{:S(2)}, u32[]{:S(2)}) collective-permute-start(f32[32,128]{1,0:T(8,128)S(1)} %get-tuple-element.30), channel_id=1, source_target_pairs={{1,2},{3,4},{5,6},{7,8},{9,10},{11,12},{13,14},{15,16},{17,18},{19... | collective-permute-start | bytes 49160 | tf_op jit(solution)/shard_map/ppermute | solution.py:469
  26.7 13.0 %collective-permute-start.4 = (f32[32,128]{1,0:T(8,128)S(1)}, f32[32,128]{1,0:T(8,128)S(1)}, u32[]{:S(2)}, u32[]{:S(2)}) collective-permute-start(f32[32,128]{1,0:T(8,128)S(1)} %get-tuple-element.31), channel_id=1, source_target_pairs={{0,1},{1,0},{2,3},{3,2},{4,5},{5,4},{6,7},{7,6},{8,9},{9,8},{10,11... | collective-permute-start | bytes 49160 | tf_op jit(solution)/shard_map/ppermute | solution.py:463
  35.1 4.6 %collective-permute-start.1 = (f32[1,256]{1,0:T(1,128)S(1)}, f32[1,256]{1,0:T(1,128)S(1)}, u32[]{:S(2)}, u32[]{:S(2)}) collective-permute-start(f32[1,256]{1,0:T(1,128)S(1)} %get-tuple-element.28), channel_id=1, source_target_pairs={{64,128},{192,256},{320,384},{448,512},{576,640},{704,768},{832,89... | collective-permute-start | bytes 3080 | tf_op jit(solution)/shard_map/ppermute | solution.py:469
  35.8 4.8 %collective-permute-start.2 = (f32[1,256]{1,0:T(1,128)S(1)}, f32[1,256]{1,0:T(1,128)S(1)}, u32[]{:S(2)}, u32[]{:S(2)}) collective-permute-start(f32[1,256]{1,0:T(1,128)S(1)} %get-tuple-element.29), channel_id=1, source_target_pairs={{0,64},{64,0},{1,65},{65,1},{2,66},{66,2},{3,67},{67,3},{4,68},{68... | collective-permute-start | bytes 3080 | tf_op jit(solution)/shard_map/ppermute | solution.py:463

commit v10 on v7

--- a/solution.py
+++ b/solution.py
@@ -167,7 +167,7 @@
 
 def opening_kernel(
     kinds_hbm, r_hbm, map_hbm, e_hbm, c_hbm,
-    perm_ref, over_ref, facing_ref, out_ref, r_ref, e_ref, c_ref,
+    perm_ref, over_ref, facing_ref, row_ref, out_ref, r_ref, e_ref, c_ref,
     kinds_ref, map_ref, rows_ref, block_ref, sems,
 ):
     nev, rows, columns = e_ref.shape
@@ -210,7 +210,9 @@
     for k in range(steps):
         parts[k].wait()
         for e in range(k * chunk, (k + 1) * chunk):
-            project_one(e_ref[e], r, rows_ref, e)
+            own = e_ref[e]
+            project_one(own, r, rows_ref, e)
+            row_ref[e : e + 1, :] = jnp.where(upper, own[rows - 1 :], own[:1])
             edge = pltpu.roll(e_ref[e, :, pl.ds(block, LANES)], e + turn, 1)
             facing = jnp.where(lane == e, edge, facing)
     facing_ref[...] = facing
@@ -241,7 +243,7 @@
 
 def first_kernel(
     got_ref, over_ref, perm_ref, r_ref, e_ref, c_ref,
-    z_ref, coef_ref, z_over_ref, z_in_ref, y_in_ref, rows_ref,
+    z_ref, coef_ref, z_over_ref, y_in_ref, rows_ref,
 ):
     nev, rows, columns = e_ref.shape
     size = columns // LANES + 1
@@ -270,23 +272,23 @@
     z_ref[...] = z
     top, low = (faces[0] * z)[:1], (faces[1] * z)[-1:]
     z_over_ref[...] = jnp.where(upper, top, low)
-    z_in_ref[...] = jnp.where(upper, low, top)
     lefts, rights = to_lanes((faces[2] * z)[:, :1], 0), to_lanes((faces[3] * z)[:, -1:], 0)
     y_in_ref[...] = jnp.where(first, rights, lefts)
 
 
 def second_kernel(
-    z_in_ref, y_in_ref, z_over_ref, facing_ref, z_ref, coef_ref, e_ref, q_ref, out_ref, rows_ref
+    z_over_ref, y_in_ref, facing_ref, row_ref, z_ref, coef_ref, e_ref,
+    q_ref, z_in_ref, out_ref, rows_ref,
 ):
     nev, rows, _ = e_ref.shape
     upper = lax.axis_index("zl") == 0
     first = lax.axis_index("core") == 0
     stencil = Stencil(coef_ref)
-    over, within = z_over_ref[...], z_in_ref[...]
+    over = z_over_ref[...]
     y_in = to_column(y_in_ref[...], 0, rows)
     halo = (
-        jnp.where(upper, over, within),
-        jnp.where(upper, within, over),
+        jnp.where(upper, over, 0.0),
+        jnp.where(upper, 0.0, over),
         jnp.where(first, 0.0, y_in),
         jnp.where(first, y_in, 0.0),
     )
@@ -295,6 +297,8 @@
     for edge, outside in zip(stencil.edges, halo):
         q = q - jnp.where(edge, outside, 0.0)
     q_ref[...] = q
+    within = jnp.where(upper, (stencil.faces[1] * z)[-1:], (stencil.faces[0] * z)[:1])
+    z_in_ref[...] = within
     left, right = (stencil.faces[2] * z)[:, :1], (stencil.faces[3] * z)[:, -1:]
     edge = jnp.where(first, left, right)
     start = lane_start(group_place(), nev)
@@ -302,6 +306,10 @@
     added = jnp.sum(facing_ref[...] * edge, axis=0, keepdims=True)
     step = jnp.where(first, LANES - nev, nev)
     added = pltpu.roll(added, lax.rem(start + step, LANES), 1)
+    across = lax.axis_size("xy") * 2
+    partner = group_place() + jnp.where(upper, across, -across)
+    below = jnp.sum(row_ref[...] * within, axis=1, keepdims=True)
+    added = added + to_lanes(below, lane_start(partner, nev))
     sub = iota((8, LANES), 0)
     pair = jnp.where(lax.rem(sub, 2) == 0, own, -added)
     for k in range(out_ref.shape[0] // 8):
@@ -309,7 +317,7 @@
 
 
 def third_kernel(
-    got_ref, q_ref, z_ref, r_ref, coef_ref, e_ref, c_ref,
+    got_ref, z_in_ref, q_ref, z_ref, r_ref, coef_ref, e_ref, c_ref,
     q_out_ref, w_ref, v_ref, out_ref, rows_ref, block_ref, group_ref,
 ):
     nev, rows, columns = e_ref.shape
@@ -324,12 +332,17 @@
     right = jnp.where((~first) & (b < lax.axis_size("xy") * 2 - 1), edge, 0.0)
     q = q_ref[...] - jnp.where(stencil.edges[2], left, 0.0)
     q = q - jnp.where(stencil.edges[3], right, 0.0)
+    upper = lax.axis_index("zl") == 0
+    within = z_in_ref[...]
+    q = q - jnp.where(stencil.edges[0], jnp.where(upper, 0.0, within), 0.0)
+    q = q - jnp.where(stencil.edges[1], jnp.where(upper, within, 0.0), 0.0)
     q_out_ref[...] = q
     added = got_ref[pl.ds(1, count, stride=2), :]
     group_ref[...] = (
         got_ref[pl.ds(0, count, stride=2), :]
         + pltpu.roll(added, 1, 0)
         + pltpu.roll(added, count - 1, 0)
+        + pltpu.roll(added, count // 2, 0)
     )
     y = coarse(c_ref, group_ref, nev, 1)
     w = stencil.smooth(q) + prolong(e_ref, y, rows_ref)
@@ -488,30 +501,31 @@
 
     size_first = columns // LANES + 1
     given = (class_perm, right_side, class_map, eigenvectors, coarse_inverse)
-    perm, over, facing, message, r, vectors, matrix = call(
+    perm, over, facing, row, message, r, vectors, matrix = call(
         opening_kernel, "opening",
         tuple(pltpu.with_memory_space_constraint(x, pltpu.HBM) for x in given),
-        [field, (rows + 8, LANES), (rows, LANES), (size_first * group, LANES),
+        [field, (2 * nev + 8, LANES), (rows, LANES), (nev, columns), (size_first * group, LANES),
          field, eigenvectors.shape, coarse_inverse.shape],
         [pltpu.SMEM(class_perm.shape, jnp.float32), pltpu.VMEM(field, jnp.int32), per_vector,
          (size_first, LANES), pltpu.SemaphoreType.DMA((4 + PIECES,))],
         by_hand=True,
     )
-    over, facing = swap_over(over, ROWS), swap_over(facing, COLS)
+    over, row = swap_over(over, ROWS), swap_in(row, "zl")
+    facing = swap_over(facing, COLS)
     got = exchanged(message, GROUP, size_first)
-    z0, coef, z_over, z_in, y_in = call(
+    z0, coef, z_over, y_in = call(
         first_kernel, "first", (got, over, perm, r, vectors, matrix),
-        [field, (6,) + field, (1, columns), (1, columns), (1, LANES)], [per_vector],
-    )
-    z_in, y_in = swap_in(z_in, "zl"), swap_in(y_in, "core")
-    z_over = swap_over(z_over, ROWS)
-    q0, message = call(
-        second_kernel, "second", (z_in, y_in, z_over, facing, z0, coef, vectors),
-        [field, (2 * group, LANES)], [per_vector],
-    )
+        [field, (6,) + field, (1, columns), (1, LANES)], [per_vector],
+    )
+    z_over, y_in = swap_over(z_over, ROWS), swap_in(y_in, "core")
+    q0, z_in, message = call(
+        second_kernel, "second", (z_over, y_in, facing, row, z0, coef, vectors),
+        [field, (1, columns), (2 * group, LANES)], [per_vector],
+    )
+    z_in = swap_in(z_in, "zl")
     got = exchanged(message, GROUP, 2)
     q0, w, v, message = call(
-        third_kernel, "third", (got, q0, z0, r, coef, vectors, matrix),
+        third_kernel, "third", (got, z_in, q0, z0, r, coef, vectors, matrix),
         [field, field, field, (2 * z_count * size, LANES)],
         [per_vector, (size, LANES), (group, LANES)],
     )

time: 105 us -> 106 us (level)
  blocking collectives: 60.1 us -> 40.5 us
  starting transfers between devices: 29.4 us -> 46.2 us
  waiting for transfers between devices: 8.76 us -> 11 us
    all_to_all x3 -> x2, blocking collectives: 60.1 us -> 40.5 us  [exchanged(): return lax.all_to_all(flat, axes, 0, 0, tiled=True).reshape(x.shape)]
    all_to_all x1 -> x2, starting transfers between devices: 19.3 us -> 30.3 us  [exchanged(): return lax.all_to_all(flat, axes, 0, 0, tiled=True).reshape(x.shape)]
    ppermute x2 -> x3, starting transfers between devices: 5.18 us -> 10.9 us  [swap_in(): return lax.ppermute(x, axis, [(0, 1), (1, 0)])]
    ppermute x2 -> x3, waiting for transfers between devices: 0.79 us -> 2.02 us  [swap_in(): return lax.ppermute(x, axis, [(0, 1), (1, 0)])]
    all_to_all x1 -> x2, waiting for transfers between devices: 7.97 us -> 8.98 us  [exchanged(): return lax.all_to_all(flat, axes, 0, 0, tiled=True).reshape(x.shape)]
  transfers between devices with their start and end apart: 6 -> 8, of which waited for: 2 -> 4; matrix products, arithmetic and copies ran while one was open for 0% -> 0% of each run, Pallas kernels for 1% -> 1%
where the time goes in v10:
time: 106 us; the launch traced here: 104 us
  starting transfers between devices  46.2 us (44%)
  blocking collectives  40.5 us (38%)
  waiting for transfers between devices  11 us (10%)
  Pallas kernels  5.44 us (5%)
    all_to_all x2, blocking collectives, exchanged(): return lax.all_to_all(flat, axes, 0, 0, tiled=True).reshape(x.shape)  40.5 us
    all_to_all x2, starting transfers between devices, exchanged(): return lax.all_to_all(flat, axes, 0, 0, tiled=True).reshape(x.shape)  30.3 us
    ppermute x3, starting transfers between devices, swap_in(): return lax.ppermute(x, axis, [(0, 1), (1, 0)])  10.9 us
    all_to_all x2, waiting for transfers between devices, exchanged(): return lax.all_to_all(flat, axes, 0, 0, tiled=True).reshape(x.shape)  8.98 us
    pallas_call x6, Pallas kernels, call(): pl.pallas_call(kernel, out_shape=[jax.ShapeDtypeStruct(shape, jnp.float32...  5.44 us
    ppermute x3, starting transfers between devices, swap_over(): return lax.ppermute(x, axes, pairs + [(j, i) for i, j in pairs])  4.96 us
  transfers between devices with their start and end apart: 8, of which 4 were waited for; matrix products, arithmetic and copies ran while one was open for 0% of the time, Pallas kernels for 1%

profile of v10, /device:TPU:1, one launch (start us, length us, event | category | flops | bytes accessed | tf_op | source)
XLA Modules:
  0.0 103.9 jit_solution(11218713499585848624)
XLA Ops:
  0.6 2.3 %opening.1 = (f32[32,256]{1,0:T(8,128)S(1)}, f32[88,128]{1,0:T(8,128)S(1)}, f32[32,128]{1,0:T(8,128)S(1)}, f32[40,256]{1,0:T(8,128)S(1)}, f32[384,128]{1,0:T(8,1...) custom-call(f32[4]{0:T(128)} %kinds_hbm.1, f32[32,256]{1,0:T(8,128)} %r_hbm.1, ...), custom_call_target="tpu_custom_call" | custom-call | tf_op jit(solution)/shard_map/opening/pallas_call | solution.py:466
  3.0 19.3 %all-to-all-start = ((f32[128,1,384]{2,1,0:T(1,128)}), f32[128,1,384]{2,1,0:T(1,128)S(1)}, u32[]{:S(2)}, u32[]{:S(2)}) async-start(f32[128,1,384]{2,1,0:T(1,128)} %bitcast), calls=%async_computation | async-start | bytes 393216 | tf_op jit(solution)/shard_map/all_to_all | solution.py:479
  22.3 0.7 collective-permute-start
  23.0 5.0 %collective-permute-start.4 = (f32[40,256]{1,0:T(8,128)S(1)}, f32[40,256]{1,0:T(8,128)S(1)}, u32[]{:S(2)}, u32[]{:S(2)}) collective-permute-start(f32[40,256]{1,0:T(8,128)S(1)} %get-tuple-element.32), channel_id=1, source_target_pairs={{0,64},{64,0},{1,65},{65,1},{2,66},{66,2},{3,67},{67,3},{4,68},{68... | collective-permute-start | bytes 122888 | tf_op jit(solution)/shard_map/ppermute | solution.py:483
  27.9 3.6 %collective-permute-start.3 = (f32[32,128]{1,0:T(8,128)S(1)}, f32[32,128]{1,0:T(8,128)S(1)}, u32[]{:S(2)}, u32[]{:S(2)}) collective-permute-start(f32[32,128]{1,0:T(8,128)S(1)} %get-tuple-element.31), channel_id=1, source_target_pairs={{1,2},{3,4},{5,6},{7,8},{9,10},{11,12},{13,14},{15,16},{17,18},{19... | collective-permute-start | bytes 49160 | tf_op jit(solution)/shard_map/ppermute | solution.py:489
  31.6 0.0 collective-permute-done.over_ref
  31.6 2.9 %all-to-all-done = f32[128,1,384]{2,1,0:T(1,128)S(1)} async-done(((f32[128,1,384]{2,1,0:T(1,128)}), f32[128,1,384]{2,1,0:T(1,128)S(1)}, u32[]{:S(2)}, u32[]{:S(2)}) %all-to-all-start) | async-done | bytes 196640 | tf_op jit(solution)/shard_map/all_to_all | solution.py:479
  34.5 0.5 first.1
  35.0 0.7 collective-permute-start.1
  35.7 2.3 %collective-permute-start.2 = (f32[1,128]{1,0:T(1,128)S(1)}, f32[1,128]{1,0:T(1,128)S(1)}, u32[]{:S(2)}, u32[]{:S(2)}) collective-permute-start(f32[1,128]{1,0:T(1,128)S(1)} %get-tuple-element.30), channel_id=1, source_target_pairs={{0,1},{1,0},{2,3},{3,2},{4,5},{5,4},{6,7},{7,6},{8,9},{9,8},{10,11... | collective-permute-start | bytes 1544 | tf_op jit(solution)/shard_map/ppermute | solution.py:483
  38.0 0.0 collective-permute-done.3.facing_ref
  38.0 0.0 collective-permute-done.4.row_ref
  38.0 0.8 collective-permute-done.2.y_in_ref
  38.8 0.0 collective-permute-done.1.z_over_ref
  38.8 1.0 second.1
  39.8 11.0 %all-to-all-start.1 = ((f32[128,1,256]{2,1,0:T(1,128)}), f32[128,1,256]{2,1,0:T(1,128)S(1)}, u32[]{:S(2)}, u32[]{:S(2)}) async-start(f32[128,1,256]{2,1,0:T(1,128)} %bitcast.2), calls=%async_computation.1 | async-start | bytes 262144 | tf_op jit(solution)/shard_map/all_to_all | solution.py:479
  50.8 3.6 %collective-permute-start.5 = (f32[1,256]{1,0:T(1,128)S(1)}, f32[1,256]{1,0:T(1,128)S(1)}, u32[]{:S(2)}, u32[]{:S(2)}) collective-permute-start(f32[1,256]{1,0:T(1,128)S(1)} %get-tuple-element.36), channel_id=1, source_target_pairs={{0,64},{64,0},{1,65},{65,1},{2,66},{66,2},{3,67},{67,3},{4,68},{68... | collective-permute-start | bytes 3080 | tf_op jit(solution)/shard_map/ppermute | solution.py:483
  54.5 1.2 %collective-permute-done.5.z_in_ref = f32[1,256]{1,0:T(1,128)S(1)} collective-permute-done((f32[1,256]{1,0:T(1,128)S(1)}, f32[1,256]{1,0:T(1,128)S(1)}, u32[]{:S(2)}, u32[]{:S(2)}) %collective-permute-start.5) | collective-permute-done | bytes 1056 | tf_op jit(solution)/shard_map/ppermute | solution.py:483
  55.7 6.1 %all-to-all-done.1 = f32[128,1,256]{2,1,0:T(1,128)S(1)} async-done(((f32[128,1,256]{2,1,0:T(1,128)}), f32[128,1,256]{2,1,0:T(1,128)S(1)}, u32[]{:S(2)}, u32[]{:S(2)}) %all-to-all-start.1) | async-done | bytes 131104 | tf_op jit(solution)/shard_map/all_to_all | solution.py:479
  61.8 0.6 third.1
  62.4 27.1 %all_to_all.36 = f32[32,1,640]{2,1,0:T(1,128)S(1)} all-to-all(f32[32,1,640]{2,1,0:T(1,128)S(1)} %bitcast.13), channel_id=1, replica_groups=mesh['zh'=8,'zl'=2,'xy'=32,'core'=2] {'zh','zl','core'}, dimensions={0} | all-to-all | bytes 163840 | tf_op jit(solution)/shard_map/all_to_all | solution.py:479
  89.5 0.2 fourth.1
  89.7 13.4 %all_to_all.37 = f32[32,1,1152]{2,1,0:T(1,128)S(1)} all-to-all(f32[32,1,1152]{2,1,0:T(1,128)S(1)} %bitcast.12), channel_id=1, replica_groups=mesh['zh'=8,'zl'=2,'xy'=32,'core'=2] {'xy'}, dimensions={0} | all-to-all | bytes 294912 | tf_op jit(solution)/shard_map/all_to_all | solution.py:479
  103.1 0.8 closing.1
Async XLA Ops:
  3.0 31.5 %all-to-all-start = ((f32[128,1,384]{2,1,0:T(1,128)}), f32[128,1,384]{2,1,0:T(1,128)S(1)}, u32[]{:S(2)}, u32[]{:S(2)}) async-start(f32[128,1,384]{2,1,0:T(1,128)} %bitcast), calls=%async_computation | async-start | bytes 393216 | tf_op jit(solution)/shard_map/all_to_all | solution.py:479
  22.3 9.3 %collective-permute-start = (f32[88,128]{1,0:T(8,128)S(1)}, f32[88,128]{1,0:T(8,128)S(1)}, u32[]{:S(2)}, u32[]{:S(2)}) collective-permute-start(f32[88,128]{1,0:T(8,128)S(1)} %get-tuple-element.24), channel_id=1, source_target_pairs={{64,128},{192,256},{320,384},{448,512},{576,640},{704,768},{832,89... | collective-permute-start | bytes 135176 | tf_op jit(solution)/shard_map/ppermute | solution.py:489
  23.0 15.1 %collective-permute-start.4 = (f32[40,256]{1,0:T(8,128)S(1)}, f32[40,256]{1,0:T(8,128)S(1)}, u32[]{:S(2)}, u32[]{:S(2)}) collective-permute-start(f32[40,256]{1,0:T(8,128)S(1)} %get-tuple-element.32), channel_id=1, source_target_pairs={{0,64},{64,0},{1,65},{65,1},{2,66},{66,2},{3,67},{67,3},{4,68},{68... | collective-permute-start | bytes 122888 | tf_op jit(solution)/shard_map/ppermute | solution.py:483
  27.9 10.1 %collective-permute-start.3 = (f32[32,128]{1,0:T(8,128)S(1)}, f32[32,128]{1,0:T(8,128)S(1)}, u32[]{:S(2)}, u32[]{:S(2)}) collective-permute-start(f32[32,128]{1,0:T(8,128)S(1)} %get-tuple-element.31), channel_id=1, source_target_pairs={{1,2},{3,4},{5,6},{7,8},{9,10},{11,12},{13,14},{15,16},{17,18},{19... | collective-permute-start | bytes 49160 | tf_op jit(solution)/shard_map/ppermute | solution.py:489
  35.0 3.8 %collective-permute-start.1 = (f32[1,256]{1,0:T(1,128)S(1)}, f32[1,256]{1,0:T(1,128)S(1)}, u32[]{:S(2)}, u32[]{:S(2)}) collective-permute-start(f32[1,256]{1,0:T(1,128)S(1)} %get-tuple-element.29), channel_id=1, source_target_pairs={{64,128},{192,256},{320,384},{448,512},{576,640},{704,768},{832,89... | collective-permute-start | bytes 3080 | tf_op jit(solution)/shard_map/ppermute | solution.py:489
  35.7 3.1 %collective-permute-start.2 = (f32[1,128]{1,0:T(1,128)S(1)}, f32[1,128]{1,0:T(1,128)S(1)}, u32[]{:S(2)}, u32[]{:S(2)}) collective-permute-start(f32[1,128]{1,0:T(1,128)S(1)} %get-tuple-element.30), channel_id=1, source_target_pairs={{0,1},{1,0},{2,3},{3,2},{4,5},{5,4},{6,7},{7,6},{8,9},{9,8},{10,11... | collective-permute-start | bytes 1544 | tf_op jit(solution)/shard_map/ppermute | solution.py:483
  39.8 22.0 %all-to-all-start.1 = ((f32[128,1,256]{2,1,0:T(1,128)}), f32[128,1,256]{2,1,0:T(1,128)S(1)}, u32[]{:S(2)}, u32[]{:S(2)}) async-start(f32[128,1,256]{2,1,0:T(1,128)} %bitcast.2), calls=%async_computation.1 | async-start | bytes 262144 | tf_op jit(solution)/shard_map/all_to_all | solution.py:479
  50.8 4.9 %collective-permute-start.5 = (f32[1,256]{1,0:T(1,128)S(1)}, f32[1,256]{1,0:T(1,128)S(1)}, u32[]{:S(2)}, u32[]{:S(2)}) collective-permute-start(f32[1,256]{1,0:T(1,128)S(1)} %get-tuple-element.36), channel_id=1, source_target_pairs={{0,64},{64,0},{1,65},{65,1},{2,66},{66,2},{3,67},{67,3},{4,68},{68... | collective-permute-start | bytes 3080 | tf_op jit(solution)/shard_map/ppermute | solution.py:483

commit v11 on v9

--- a/solution.py
+++ b/solution.py
@@ -278,7 +278,7 @@
 
 
 def second_kernel(
-    z_over_ref, z_in_ref, facing_ref, inside_ref, z_ref, coef_ref, e_ref, q_ref, out_ref, rows_ref
+    z_in_ref, z_over_ref, facing_ref, inside_ref, z_ref, coef_ref, e_ref, q_ref, out_ref, rows_ref
 ):
     nev, rows, _ = e_ref.shape
     upper = lax.axis_index("zl") == 0
@@ -499,7 +499,7 @@
     )
     z_over, z_in = swap_over(z_over, ROWS), swap_in(z_in, "zl")
     q0, message = call(
-        second_kernel, "second", (z_over, z_in, facing, inside, z0, coef, vectors),
+        second_kernel, "second", (z_in, z_over, facing, inside, z0, coef, vectors),
         [field, (2 * group, LANES)], [per_vector],
     )
     got = exchanged(message, GROUP, 2)

time: 106 us -> 105 us (level)
  starting transfers between devices: 30 us -> 28.7 us
    ppermute x2, starting transfers between devices: 5.78 us -> 4.52 us  [swap_in(): return lax.ppermute(x, axis, [(0, 1), (1, 0)])]
where the time goes in v11:
time: 105 us; the launch traced here: 104 us
  blocking collectives  62.4 us (59%)
  starting transfers between devices  28.7 us (27%)
  waiting for transfers between devices  7.06 us (7%)
  Pallas kernels  4.78 us (5%)
    all_to_all x3, blocking collectives, exchanged(): return lax.all_to_all(flat, axes, 0, 0, tiled=True).reshape(x.shape)  62.4 us
    all_to_all x1, starting transfers between devices, exchanged(): return lax.all_to_all(flat, axes, 0, 0, tiled=True).reshape(x.shape)  19.3 us
    all_to_all x1, waiting for transfers between devices, exchanged(): return lax.all_to_all(flat, axes, 0, 0, tiled=True).reshape(x.shape)  6.04 us
    ppermute x3, starting transfers between devices, swap_over(): return lax.ppermute(x, axes, pairs + [(j, i) for i, j in pairs])  4.87 us
    pallas_call x6, Pallas kernels, call(): pl.pallas_call(kernel, out_shape=[jax.ShapeDtypeStruct(shape, jnp.float32...  4.78 us
    ppermute x2, starting transfers between devices, swap_in(): return lax.ppermute(x, axis, [(0, 1), (1, 0)])  4.52 us
  transfers between devices with their start and end apart: 6, of which 2 were waited for; matrix products, arithmetic and copies ran while one was open for 0% of the time, Pallas kernels for 0%

profile of v11, /device:TPU:1, one launch (start us, length us, event | category | flops | bytes accessed | tf_op | source)
XLA Modules:
  0.0 103.7 jit_solution(15648081386939550726)
XLA Ops:
  0.6 2.5 %opening.1 = (f32[32,256]{1,0:T(8,128)S(1)}, f32[40,128]{1,0:T(8,128)S(1)}, f32[32,128]{1,0:T(8,128)S(1)}, f32[32,128]{1,0:T(8,128)S(1)}, f32[384,128]{1,0:T(8,1...) custom-call(f32[4]{0:T(128)} %kinds_hbm.1, f32[32,256]{1,0:T(8,128)} %r_hbm.1, ...), custom_call_target="tpu_custom_call" | custom-call | tf_op jit(solution)/shard_map/opening/pallas_call | solution.py:446
  3.1 19.3 %all-to-all-start = ((f32[128,1,384]{2,1,0:T(1,128)}), f32[128,1,384]{2,1,0:T(1,128)S(1)}, u32[]{:S(2)}, u32[]{:S(2)}) async-start(f32[128,1,384]{2,1,0:T(1,128)} %bitcast), calls=%async_computation | async-start | bytes 393216 | tf_op jit(solution)/shard_map/all_to_all | solution.py:459
  22.5 0.7 collective-permute-start
  23.1 3.5 %collective-permute-start.3 = (f32[32,128]{1,0:T(8,128)S(1)}, f32[32,128]{1,0:T(8,128)S(1)}, u32[]{:S(2)}, u32[]{:S(2)}) collective-permute-start(f32[32,128]{1,0:T(8,128)S(1)} %get-tuple-element.30), channel_id=1, source_target_pairs={{1,2},{3,4},{5,6},{7,8},{9,10},{11,12},{13,14},{15,16},{17,18},{19... | collective-permute-start | bytes 49160 | tf_op jit(solution)/shard_map/ppermute | solution.py:469
  26.7 1.9 %collective-permute-start.4 = (f32[32,128]{1,0:T(8,128)S(1)}, f32[32,128]{1,0:T(8,128)S(1)}, u32[]{:S(2)}, u32[]{:S(2)}) collective-permute-start(f32[32,128]{1,0:T(8,128)S(1)} %get-tuple-element.31), channel_id=1, source_target_pairs={{0,1},{1,0},{2,3},{3,2},{4,5},{5,4},{6,7},{7,6},{8,9},{9,8},{10,11... | collective-permute-start | bytes 49160 | tf_op jit(solution)/shard_map/ppermute | solution.py:463
  28.6 0.0 collective-permute-done.over_ref
  28.6 6.0 %all-to-all-done = f32[128,1,384]{2,1,0:T(1,128)S(1)} async-done(((f32[128,1,384]{2,1,0:T(1,128)}), f32[128,1,384]{2,1,0:T(1,128)S(1)}, u32[]{:S(2)}, u32[]{:S(2)}) %all-to-all-start) | async-done | bytes 196640 | tf_op jit(solution)/shard_map/all_to_all | solution.py:459
  34.7 0.4 first.1
  35.1 2.6 %collective-permute-start.1 = (f32[1,256]{1,0:T(1,128)S(1)}, f32[1,256]{1,0:T(1,128)S(1)}, u32[]{:S(2)}, u32[]{:S(2)}) collective-permute-start(f32[1,256]{1,0:T(1,128)S(1)} %get-tuple-element.28), channel_id=1, source_target_pairs={{0,64},{64,0},{1,65},{65,1},{2,66},{66,2},{3,67},{67,3},{4,68},{68... | collective-permute-start | bytes 3080 | tf_op jit(solution)/shard_map/ppermute | solution.py:463
  37.7 0.7 collective-permute-start.2
  38.4 0.0 collective-permute-done.3.facing_ref
  38.4 0.0 collective-permute-done.4.inside_ref
  38.4 1.0 collective-permute-done.1.z_in_ref
  39.4 0.0 collective-permute-done.2.z_over_ref
  39.4 0.3 second.1
  39.7 22.3 %all_to_all.36 = f32[128,1,256]{2,1,0:T(1,128)S(1)} all-to-all(f32[128,1,256]{2,1,0:T(1,128)S(1)} %bitcast.13), channel_id=1, replica_groups=mesh['zh'=8,'zl'=2,'xy'=32,'core'=2] {'zl','xy','core'}, dimensions={0} | all-to-all | bytes 262144 | tf_op jit(solution)/shard_map/all_to_all | solution.py:459
  62.0 0.6 third.1
  62.6 27.9 %all_to_all.37 = f32[32,1,640]{2,1,0:T(1,128)S(1)} all-to-all(f32[32,1,640]{2,1,0:T(1,128)S(1)} %bitcast.14), channel_id=1, replica_groups=mesh['zh'=8,'zl'=2,'xy'=32,'core'=2] {'zh','zl','core'}, dimensions={0} | all-to-all | bytes 163840 | tf_op jit(solution)/shard_map/all_to_all | solution.py:459
  90.5 0.2 fourth.1
  90.7 12.2 %all_to_all.38 = f32[32,1,1152]{2,1,0:T(1,128)S(1)} all-to-all(f32[32,1,1152]{2,1,0:T(1,128)S(1)} %bitcast.12), channel_id=1, replica_groups=mesh['zh'=8,'zl'=2,'xy'=32,'core'=2] {'xy'}, dimensions={0} | all-to-all | bytes 294912 | tf_op jit(solution)/shard_map/all_to_all | solution.py:459
  102.9 0.8 closing.1
Async XLA Ops:
  3.1 31.5 %all-to-all-start = ((f32[128,1,384]{2,1,0:T(1,128)}), f32[128,1,384]{2,1,0:T(1,128)S(1)}, u32[]{:S(2)}, u32[]{:S(2)}) async-start(f32[128,1,384]{2,1,0:T(1,128)} %bitcast), calls=%async_computation | async-start | bytes 393216 | tf_op jit(solution)/shard_map/all_to_all | solution.py:459
  22.5 6.2 %collective-permute-start = (f32[40,128]{1,0:T(8,128)S(1)}, f32[40,128]{1,0:T(8,128)S(1)}, u32[]{:S(2)}, u32[]{:S(2)}) collective-permute-start(f32[40,128]{1,0:T(8,128)S(1)} %get-tuple-element.23), channel_id=1, source_target_pairs={{64,128},{192,256},{320,384},{448,512},{576,640},{704,768},{832,89... | collective-permute-start | bytes 61448 | tf_op jit(solution)/shard_map/ppermute | solution.py:469
  23.1 15.2 %collective-permute-start.3 = (f32[32,128]{1,0:T(8,128)S(1)}, f32[32,128]{1,0:T(8,128)S(1)}, u32[]{:S(2)}, u32[]{:S(2)}) collective-permute-start(f32[32,128]{1,0:T(8,128)S(1)} %get-tuple-element.30), channel_id=1, source_target_pairs={{1,2},{3,4},{5,6},{7,8},{9,10},{11,12},{13,14},{15,16},{17,18},{19... | collective-permute-start | bytes 49160 | tf_op jit(solution)/shard_map/ppermute | solution.py:469
  26.7 11.7 %collective-permute-start.4 = (f32[32,128]{1,0:T(8,128)S(1)}, f32[32,128]{1,0:T(8,128)S(1)}, u32[]{:S(2)}, u32[]{:S(2)}) collective-permute-start(f32[32,128]{1,0:T(8,128)S(1)} %get-tuple-element.31), channel_id=1, source_target_pairs={{0,1},{1,0},{2,3},{3,2},{4,5},{5,4},{6,7},{7,6},{8,9},{9,8},{10,11... | collective-permute-start | bytes 49160 | tf_op jit(solution)/shard_map/ppermute | solution.py:463
  35.1 4.3 %collective-permute-start.1 = (f32[1,256]{1,0:T(1,128)S(1)}, f32[1,256]{1,0:T(1,128)S(1)}, u32[]{:S(2)}, u32[]{:S(2)}) collective-permute-start(f32[1,256]{1,0:T(1,128)S(1)} %get-tuple-element.28), channel_id=1, source_target_pairs={{0,64},{64,0},{1,65},{65,1},{2,66},{66,2},{3,67},{67,3},{4,68},{68... | collective-permute-start | bytes 3080 | tf_op jit(solution)/shard_map/ppermute | solution.py:463
  37.7 1.7 %collective-permute-start.2 = (f32[1,256]{1,0:T(1,128)S(1)}, f32[1,256]{1,0:T(1,128)S(1)}, u32[]{:S(2)}, u32[]{:S(2)}) collective-permute-start(f32[1,256]{1,0:T(1,128)S(1)} %get-tuple-element.29), channel_id=1, source_target_pairs={{64,128},{192,256},{320,384},{448,512},{576,640},{704,768},{832,89... | collective-permute-start | bytes 3080 | tf_op jit(solution)/shard_map/ppermute | solution.py:469

commit v12 on v11

--- a/solution.py
+++ b/solution.py
@@ -203,22 +203,21 @@
         over_ref[k : k + 1, :] = over[:, k * LANES : (k + 1) * LANES]
     r = r_ref[...]
     first = lax.axis_index("core") == 0
-    block = pl.multiple_of(jnp.where(first, 0, columns - LANES), LANES)
-    other = pl.multiple_of(jnp.where(first, columns - LANES, 0), LANES)
-    turn = jnp.where(first, 0, 1)
     lane = iota((rows, LANES), 1)
-    facing = jnp.zeros((rows, LANES), jnp.float32)
-    inside = facing
+    lefts = jnp.zeros((rows, LANES), jnp.float32)
+    rights = lefts
     for k in range(steps):
         parts[k].wait()
         for e in range(k * chunk, (k + 1) * chunk):
-            project_one(e_ref[e], r, rows_ref, e)
-            edge = pltpu.roll(e_ref[e, :, pl.ds(block, LANES)], e + turn, 1)
-            facing = jnp.where(lane == e, edge, facing)
-            edge = pltpu.roll(e_ref[e, :, pl.ds(other, LANES)], e + 1 - turn, 1)
-            inside = jnp.where(lane == e, edge, inside)
-    facing_ref[...] = facing
-    inside_ref[...] = inside
+            own = e_ref[e]
+            project_one(own, r, rows_ref, e)
+            both = jnp.where(lane < LANES // 2, own[:, :LANES], own[:, columns - LANES :])
+            both = pltpu.roll(both, e, 1) if e > 0 else both
+            lefts = jnp.where(lane == e, both, lefts)
+            rights = jnp.where(lane == (e - 1) % LANES, both, rights)
+    rights = pltpu.roll(rights, 1, 1)
+    facing_ref[...] = jnp.where(first, lefts, rights)
+    inside_ref[...] = jnp.where(first, rights, lefts)
     c = jnp.sum(rows_ref[...], axis=1, keepdims=True)
     start = lane_start(group_place(), nev)
     size = block_ref.shape[0]

time: 105 us -> 105 us (level)
  no operation moved by 1% of the time
where the time goes in v12:
time: 105 us; the launch traced here: 104 us
  blocking collectives  62.4 us (59%)
  starting transfers between devices  28.7 us (27%)
  waiting for transfers between devices  7.06 us (7%)
  Pallas kernels  4.62 us (4%)
    all_to_all x3, blocking collectives, exchanged(): return lax.all_to_all(flat, axes, 0, 0, tiled=True).reshape(x.shape)  62.4 us
    all_to_all x1, starting transfers between devices, exchanged(): return lax.all_to_all(flat, axes, 0, 0, tiled=True).reshape(x.shape)  19.3 us
    all_to_all x1, waiting for transfers between devices, exchanged(): return lax.all_to_all(flat, axes, 0, 0, tiled=True).reshape(x.shape)  6.04 us
    ppermute x3, starting transfers between devices, swap_over(): return lax.ppermute(x, axes, pairs + [(j, i) for i, j in pairs])  4.87 us
    pallas_call x6, Pallas kernels, call(): pl.pallas_call(kernel, out_shape=[jax.ShapeDtypeStruct(shape, jnp.float32...  4.62 us
    ppermute x2, starting transfers between devices, swap_in(): return lax.ppermute(x, axis, [(0, 1), (1, 0)])  4.52 us
  transfers between devices with their start and end apart: 6, of which 2 were waited for; matrix products, arithmetic and copies ran while one was open for 0% of the time, Pallas kernels for 0%

profile of v12, /device:TPU:1, one launch (start us, length us, event | category | flops | bytes accessed | tf_op | source)
XLA Modules:
  0.0 103.5 jit_solution(9145850014897171102)
XLA Ops:
  0.6 2.3 %opening.1 = (f32[32,256]{1,0:T(8,128)S(1)}, f32[40,128]{1,0:T(8,128)S(1)}, f32[32,128]{1,0:T(8,128)S(1)}, f32[32,128]{1,0:T(8,128)S(1)}, f32[384,128]{1,0:T(8,1...) custom-call(f32[4]{0:T(128)} %kinds_hbm.1, f32[32,256]{1,0:T(8,128)} %r_hbm.1, ...), custom_call_target="tpu_custom_call" | custom-call | tf_op jit(solution)/shard_map/opening/pallas_call | solution.py:445
  3.0 19.3 %all-to-all-start = ((f32[128,1,384]{2,1,0:T(1,128)}), f32[128,1,384]{2,1,0:T(1,128)S(1)}, u32[]{:S(2)}, u32[]{:S(2)}) async-start(f32[128,1,384]{2,1,0:T(1,128)} %bitcast), calls=%async_computation | async-start | bytes 393216 | tf_op jit(solution)/shard_map/all_to_all | solution.py:458
  22.3 0.7 collective-permute-start
  23.0 3.5 %collective-permute-start.3 = (f32[32,128]{1,0:T(8,128)S(1)}, f32[32,128]{1,0:T(8,128)S(1)}, u32[]{:S(2)}, u32[]{:S(2)}) collective-permute-start(f32[32,128]{1,0:T(8,128)S(1)} %get-tuple-element.30), channel_id=1, source_target_pairs={{1,2},{3,4},{5,6},{7,8},{9,10},{11,12},{13,14},{15,16},{17,18},{19... | collective-permute-start | bytes 49160 | tf_op jit(solution)/shard_map/ppermute | solution.py:468
  26.5 1.9 %collective-permute-start.4 = (f32[32,128]{1,0:T(8,128)S(1)}, f32[32,128]{1,0:T(8,128)S(1)}, u32[]{:S(2)}, u32[]{:S(2)}) collective-permute-start(f32[32,128]{1,0:T(8,128)S(1)} %get-tuple-element.31), channel_id=1, source_target_pairs={{0,1},{1,0},{2,3},{3,2},{4,5},{5,4},{6,7},{7,6},{8,9},{9,8},{10,11... | collective-permute-start | bytes 49160 | tf_op jit(solution)/shard_map/ppermute | solution.py:462
  28.5 0.0 collective-permute-done.over_ref
  28.5 6.0 %all-to-all-done = f32[128,1,384]{2,1,0:T(1,128)S(1)} async-done(((f32[128,1,384]{2,1,0:T(1,128)}), f32[128,1,384]{2,1,0:T(1,128)S(1)}, u32[]{:S(2)}, u32[]{:S(2)}) %all-to-all-start) | async-done | bytes 196640 | tf_op jit(solution)/shard_map/all_to_all | solution.py:458
  34.5 0.4 first.1
  34.9 2.6 %collective-permute-start.1 = (f32[1,256]{1,0:T(1,128)S(1)}, f32[1,256]{1,0:T(1,128)S(1)}, u32[]{:S(2)}, u32[]{:S(2)}) collective-permute-start(f32[1,256]{1,0:T(1,128)S(1)} %get-tuple-element.28), channel_id=1, source_target_pairs={{0,64},{64,0},{1,65},{65,1},{2,66},{66,2},{3,67},{67,3},{4,68},{68... | collective-permute-start | bytes 3080 | tf_op jit(solution)/shard_map/ppermute | solution.py:462
  37.5 0.7 collective-permute-start.2
  38.2 0.0 collective-permute-done.3.facing_ref
  38.2 0.0 collective-permute-done.4.inside_ref
  38.2 1.0 collective-permute-done.1.z_in_ref
  39.2 0.0 collective-permute-done.2.z_over_ref
  39.2 0.3 second.1
  39.6 22.3 %all_to_all.36 = f32[128,1,256]{2,1,0:T(1,128)S(1)} all-to-all(f32[128,1,256]{2,1,0:T(1,128)S(1)} %bitcast.13), channel_id=1, replica_groups=mesh['zh'=8,'zl'=2,'xy'=32,'core'=2] {'zl','xy','core'}, dimensions={0} | all-to-all | bytes 262144 | tf_op jit(solution)/shard_map/all_to_all | solution.py:458
  61.9 0.6 third.1
  62.5 27.9 %all_to_all.37 = f32[32,1,640]{2,1,0:T(1,128)S(1)} all-to-all(f32[32,1,640]{2,1,0:T(1,128)S(1)} %bitcast.14), channel_id=1, replica_groups=mesh['zh'=8,'zl'=2,'xy'=32,'core'=2] {'zh','zl','core'}, dimensions={0} | all-to-all | bytes 163840 | tf_op jit(solution)/shard_map/all_to_all | solution.py:458
  90.4 0.2 fourth.1
  90.6 12.2 %all_to_all.38 = f32[32,1,1152]{2,1,0:T(1,128)S(1)} all-to-all(f32[32,1,1152]{2,1,0:T(1,128)S(1)} %bitcast.12), channel_id=1, replica_groups=mesh['zh'=8,'zl'=2,'xy'=32,'core'=2] {'xy'}, dimensions={0} | all-to-all | bytes 294912 | tf_op jit(solution)/shard_map/all_to_all | solution.py:458
  102.7 0.8 closing.1
Async XLA Ops:
  3.0 31.5 %all-to-all-start = ((f32[128,1,384]{2,1,0:T(1,128)}), f32[128,1,384]{2,1,0:T(1,128)S(1)}, u32[]{:S(2)}, u32[]{:S(2)}) async-start(f32[128,1,384]{2,1,0:T(1,128)} %bitcast), calls=%async_computation | async-start | bytes 393216 | tf_op jit(solution)/shard_map/all_to_all | solution.py:458
  22.3 6.2 %collective-permute-start = (f32[40,128]{1,0:T(8,128)S(1)}, f32[40,128]{1,0:T(8,128)S(1)}, u32[]{:S(2)}, u32[]{:S(2)}) collective-permute-start(f32[40,128]{1,0:T(8,128)S(1)} %get-tuple-element.23), channel_id=1, source_target_pairs={{64,128},{192,256},{320,384},{448,512},{576,640},{704,768},{832,89... | collective-permute-start | bytes 61448 | tf_op jit(solution)/shard_map/ppermute | solution.py:468
  23.0 15.2 %collective-permute-start.3 = (f32[32,128]{1,0:T(8,128)S(1)}, f32[32,128]{1,0:T(8,128)S(1)}, u32[]{:S(2)}, u32[]{:S(2)}) collective-permute-start(f32[32,128]{1,0:T(8,128)S(1)} %get-tuple-element.30), channel_id=1, source_target_pairs={{1,2},{3,4},{5,6},{7,8},{9,10},{11,12},{13,14},{15,16},{17,18},{19... | collective-permute-start | bytes 49160 | tf_op jit(solution)/shard_map/ppermute | solution.py:468
  26.5 11.7 %collective-permute-start.4 = (f32[32,128]{1,0:T(8,128)S(1)}, f32[32,128]{1,0:T(8,128)S(1)}, u32[]{:S(2)}, u32[]{:S(2)}) collective-permute-start(f32[32,128]{1,0:T(8,128)S(1)} %get-tuple-element.31), channel_id=1, source_target_pairs={{0,1},{1,0},{2,3},{3,2},{4,5},{5,4},{6,7},{7,6},{8,9},{9,8},{10,11... | collective-permute-start | bytes 49160 | tf_op jit(solution)/shard_map/ppermute | solution.py:462
  34.9 4.3 %collective-permute-start.1 = (f32[1,256]{1,0:T(1,128)S(1)}, f32[1,256]{1,0:T(1,128)S(1)}, u32[]{:S(2)}, u32[]{:S(2)}) collective-permute-start(f32[1,256]{1,0:T(1,128)S(1)} %get-tuple-element.28), channel_id=1, source_target_pairs={{0,64},{64,0},{1,65},{65,1},{2,66},{66,2},{3,67},{67,3},{4,68},{68... | collective-permute-start | bytes 3080 | tf_op jit(solution)/shard_map/ppermute | solution.py:462
  37.5 1.7 %collective-permute-start.2 = (f32[1,256]{1,0:T(1,128)S(1)}, f32[1,256]{1,0:T(1,128)S(1)}, u32[]{:S(2)}, u32[]{:S(2)}) collective-permute-start(f32[1,256]{1,0:T(1,128)S(1)} %get-tuple-element.29), channel_id=1, source_target_pairs={{64,128},{192,256},{320,384},{448,512},{576,640},{704,768},{832,89... | collective-permute-start | bytes 3080 | tf_op jit(solution)/shard_map/ppermute | solution.py:468
